TPU v7x, 256 devices: a whole 4x4x8 slice. The times are simulated.
256 devices in a mesh: rep: 8 (over z_lo, core), fsdp: 32 (over z_hi, x, y).
Axes of the slice: x: 4, y: 4, z: 8 (z_hi: 2, z_lo: 4; z = z_hi * 4 + z_lo), core: 2. Of those that a mesh axis runs over, the one named last changes fastest.
Arguments:
- inputs: bfloat16 [32768, 8192], P(('rep', 'fsdp')), may hold values from -6 to 6
- value_weight: bfloat16 [8192, 512], P('fsdp'), may hold values from -0.0625 to 0.0625
- send_slot: int32 [32768], P(('rep', 'fsdp')), may hold values from 0 to 255, as said below
- response_id: int32 [32768], P(('rep', 'fsdp')), may hold values from 0 to 127, as said below
- queries: bfloat16 [65536, 4096], P(('rep', 'fsdp')), may hold values from -6 to 6
- keys: bfloat16 [65536, 512], P(('rep', 'fsdp')), may hold values from -6 to 6
- upstream: bfloat16 [65536, 4096], P(('rep', 'fsdp')), may hold values from -6 to 6
Outputs:
- grad_inputs: bfloat16 [32768, 8192], P(('rep', 'fsdp'))
- grad_queries: bfloat16 [65536, 4096], P(('rep', 'fsdp'))
- grad_keys: bfloat16 [65536, 512], P(('rep', 'fsdp'))
- grad_weight: bfloat16 [8192, 512], P('fsdp')
Inputs may be any that keep to these rules, and one draw needn't show every extreme that they name: `send_slot`: on each device the rows form aligned runs of 8; a run goes whole to one peer, to slots peer * 8 + 0 .. 7 in row order; no two runs of a device share a peer; the first run of every device stays on the device itself. `response_id`: rows of one response are consecutive, lie within one run, and number at most 8; the first run of every device is one response of 8 rows; the last row of every device is a response of its own.
All inputs are finite; a program needn't handle non-finite values.
Results may differ from a plain program's by a relative error of at most 0.012.
Values may be sent and summed in bfloat16 or wider, within the bound.
No kernel may reach another device: no remote copies, remote signals or barrier semaphores. Data moves between devices by JAX's collectives and lax.ppermute only.
A program may use at most 128 MiB of HBM per device.

v0:
```python
import jax
import jax.numpy as jnp
from jax import lax
from jax.experimental import pallas as pl
from jax.experimental.pallas import tpu as pltpu
from jax.sharding import PartitionSpec as P

KVH = 4
GROUP = 8
HD = 128
CAP = 8
TILE = 128
BLOCKS = TILE // CAP
AXES = ("rep", "fsdp")
F32 = jnp.float32
BF16 = jnp.bfloat16
NZL, NCO, NZH, NX, NY = 4, 2, 2, 4, 4
SLICES = NZH * NX
TOKEN = jax.ShapeDtypeStruct((8, 128), jnp.float32)
VMEM = pl.BlockSpec(memory_space=pltpu.VMEM)
ANY = pl.BlockSpec(memory_space=pl.ANY)


def permute(array, move):
    pairs = []
    for e in range(NZL * NCO * NZH * NX * NY):
        place = (e // 64, e // 32 % 2, e // 16 % 2, e // 4 % 4, e % 4)
        zl, co, zh, x, y = move(*place)
        pairs.append((e, (((zl * NCO + co) * NZH + zh) * NX + x % NX) * NY + y % NY))
    return lax.ppermute(array, AXES, pairs)


def along_y(k):
    return lambda zl, co, zh, x, y: (zl, co, zh, x, y + k)


def along_x(k):
    return lambda zl, co, zh, x, y: (zl, co, zh, x + k, y)


def other_core(zl, co, zh, x, y):
    return zl, 1 - co, zh, x, y


def mirror(zl, co, zh, x, y):
    return NZL - 1 - zl, co, 1 - zh, x, y


def flip_zl(bit):
    return lambda zl, co, zh, x, y: (zl ^ bit, co, zh, x, y)


def call(kernel, name, out, *args, ins=None, outs=None, scratch=(), mib=4, flops=0):
    size = sum(a.size * a.dtype.itemsize for a in args) + sum(o.size * o.dtype.itemsize for o in out)
    return pl.pallas_call(
        kernel,
        out_shape=out,
        in_specs=[VMEM] * len(args) if ins is None else ins,
        out_specs=[VMEM] * len(out) if outs is None else outs,
        scratch_shapes=scratch,
        compiler_params=pltpu.CompilerParams(vmem_limit_bytes=mib * 1024 * 1024),
        cost_estimate=pl.CostEstimate(flops=flops, bytes_accessed=size, transcendentals=0),
        name=name,
    )(*args)


def fetch(sources, targets, sems):
    copies = [pltpu.make_async_copy(s, t, sems.at[i]) for i, (s, t) in enumerate(zip(sources, targets, strict=True))]
    for copy in copies:
        copy.start()
    return copies


def at_place():
    rep, fsdp = lax.axis_index("rep"), lax.axis_index("fsdp")
    return lax.rem(rep, NCO), lax.div(fsdp, NX * NY), lax.rem(lax.div(fsdp, NY), NX), lax.rem(fsdp, NY)


def like(shape, dtype):
    return jax.ShapeDtypeStruct(shape, dtype)


def dot(a, b, over):
    return lax.dot_general(a, b, (((over[0],), (over[1],)), ((), ())), preferred_element_type=F32)


def feature_blocks(k):
    core, zh, x, y = at_place()
    for zr in range(NZH):
        for xr in range(NX):
            z = zh + zr - 2 * zh * zr
            slice_at = (z * NX + lax.rem(x - xr + NX, NX)) * NY + lax.rem(y + k, NY)
            for cr in range(NCO):
                yield (zr * NX + xr) * NCO + cr, slice_at * NCO + core + cr - 2 * core * cr


def finish(token):
    token[...] = jnp.zeros(token.shape, token.dtype)


def masks_kernel(slots_in, ids_in, after, masks, slots, ids, sems):
    copies = fetch((slots_in, ids_in), (slots, ids), sems)
    lane = lax.broadcasted_iota(jnp.int32, (CAP, TILE), 1) & (CAP - 1)
    sub = lax.broadcasted_iota(jnp.int32, (CAP, TILE), 0)
    causal = sub <= lane
    plain = causal.astype(jnp.int32)
    for p in range(masks.shape[0]):
        masks[p] = plain
    for copy in copies:
        copy.wait()
    for r in range(slots.shape[0] // CAP):
        keys = jnp.zeros((CAP, TILE), jnp.int32)
        rows = jnp.zeros((CAP, TILE), jnp.int32)
        for j in range(CAP):
            value = ids[r * CAP + j]
            keys = jnp.where(sub == j, value, keys)
            rows = jnp.where(lane == j, value, rows)
        masks[lax.div(slots[r * CAP], CAP)] = jnp.where((keys == rows) & causal, 1, 0)


def run_masks(slots, ids, peers, after):
    index = pltpu.SMEM(slots.shape, jnp.int32)
    scratch = (index, index, pltpu.SemaphoreType.DMA((2,)))
    out = [like((peers, CAP, TILE), jnp.int32)]
    return call(masks_kernel, "masks", out, slots, ids, after, ins=[ANY] * 3, scratch=scratch, mib=56)[0]


def split_kernel(full_in, weight_in, p0, p1, p2, p3, weight, full, sems):
    rows = weight.shape[0]
    here = weight_in.at[pl.ds(pl.multiple_of(at_place()[0] * rows, rows), rows)]
    copies = fetch((full_in, here), (full, weight), sems)
    copies[0].wait()
    width = full.shape[1] // (NY * SLICES * NCO)
    for k, part in enumerate((p0, p1, p2, p3)):
        for at, block in feature_blocks(k):
            part[:, at * width : (at + 1) * width] = full[:, pl.ds(pl.multiple_of(block * width, width), width)]
    copies[1].wait()


def split(full, weight):
    rows, columns = full.shape
    out = [like((rows, columns // NY), full.dtype)] * NY + [like((weight.shape[0] // NCO, weight.shape[1]), weight.dtype)]
    scratch = (pltpu.VMEM(full.shape, full.dtype), pltpu.SemaphoreType.DMA((2,)))
    return call(split_kernel, "split", out, full, weight, ins=[ANY] * 2, scratch=scratch, mib=56)


def join_kernel(p0, p1, p2, p3, full, token):
    finish(token)
    width = p0.shape[1] // (SLICES * NCO)
    for k, part in enumerate((p0, p1, p2, p3)):
        for at, block in feature_blocks(k):
            full[:, pl.ds(pl.multiple_of(block * width, width), width)] = part[:, at * width : (at + 1) * width]


def join(parts):
    rows, columns = parts[0].shape
    return call(join_kernel, "join", [like((rows, columns * NY), parts[0].dtype), TOKEN], *parts, mib=56)


def heads(block, t):
    rows = block[t * TILE : (t + 1) * TILE, :]
    return jnp.concatenate([rows[:, h * HD : (h + 1) * HD] for h in range(GROUP)], axis=0)


def own_block(lanes):
    return lax.broadcasted_iota(jnp.int32, (CAP, lanes), 1) % TILE // CAP


def fold(pairs, block):
    out = pairs[0:CAP]
    for b in range(1, BLOCKS):
        out = jnp.where(block == b, pairs[b * CAP : (b + 1) * CAP], out)
    return out


def unfold(folded, block):
    return jnp.concatenate([jnp.where(block == b, folded, 0.0) for b in range(BLOCKS)], axis=0).astype(BF16)


def scores_kernel(queries, keys, scores):
    block = own_block(GROUP * TILE)
    for t in range(scores.shape[1]):
        pairs = dot(keys[t * TILE : (t + 1) * TILE, :], heads(queries, t), (1, 1))
        scores[0, t] = fold(pairs, block)


def probs_kernel(scores, masks, upstream, *rest):
    grad_v, probs = rest[-2:]
    small, block = own_block(TILE), own_block(GROUP * TILE)
    for t in range(scores.shape[1]):
        mask = masks[t * BLOCKS]
        for b in range(1, BLOCKS):
            mask = jnp.where(small == b, masks[t * BLOCKS + b], mask)
        visible = jnp.concatenate([mask] * GROUP, axis=1) != 0
        masked = jnp.where(visible, scores[0, t] * (1.0 / HD**0.5), -1e30)
        top = jnp.max(masked, axis=0, keepdims=True)
        expo = jnp.where(visible, jnp.exp(masked - top), 0.0)
        prob = expo / jnp.sum(expo, axis=0, keepdims=True)
        probs[0, t] = prob
        grad = dot(unfold(prob, block), heads(upstream, t), (1, 0))
        grad_v[t * TILE : (t + 1) * TILE, :] = grad.astype(BF16)


def dscore_kernel(probs, values, upstream, queries, keys, grad_q, grad_k, token):
    finish(token)
    scale = 1.0 / HD**0.5
    block = own_block(GROUP * TILE)
    for t in range(probs.shape[1]):
        rows = slice(t * TILE, (t + 1) * TILE)
        prob = probs[0, t]
        dprob = fold(dot(values[rows, :], heads(upstream, t), (1, 1)), block)
        delta = jnp.sum(prob * dprob, axis=0, keepdims=True)
        dscore = unfold(prob * (dprob - delta), block)
        grad_k[rows, :] = (dot(dscore, heads(queries, t), (1, 0)) * scale).astype(BF16)
        grad = (dot(dscore, keys[rows, :], (0, 0)) * scale).astype(BF16)
        for h in range(GROUP):
            grad_q[rows, h * HD : (h + 1) * HD] = grad[h * TILE : (h + 1) * TILE]


def per_head(kernel, name, ins, outs, args, flops):
    size = sum(a.size * a.dtype.itemsize for a in args) + sum(o.size * o.dtype.itemsize for o, _ in outs)
    return pl.pallas_call(
        kernel,
        grid=(KVH,),
        out_shape=[o for o, _ in outs],
        in_specs=ins,
        out_specs=[s for _, s in outs],
        compiler_params=pltpu.CompilerParams(vmem_limit_bytes=56 * 1024 * 1024),
        cost_estimate=pl.CostEstimate(flops=flops, bytes_accessed=size, transcendentals=0),
        name=name,
    )(*args)


def attention_specs(slots):
    wide = pl.BlockSpec((slots, GROUP * HD), lambda k: (0, k))
    narrow = pl.BlockSpec((slots, HD), lambda k: (0, k))
    tiles = slots // TILE
    folded = pl.BlockSpec((1, tiles, CAP, GROUP * TILE), lambda k: (k, 0, 0, 0))
    return wide, narrow, folded, like((KVH, tiles, CAP, GROUP * TILE), F32)


def attention_scores(queries, keys):
    wide, narrow, folded, shape = attention_specs(queries.shape[0])
    flops = 2 * queries.size * TILE
    return per_head(scores_kernel, "scores", [wide, narrow], [(shape, folded)], (queries, keys), flops)[0]


def attention_probs(scores, masks, upstream, after):
    slots = upstream.shape[0]
    wide, narrow, folded, shape = attention_specs(slots)
    masks_spec = pl.BlockSpec(masks.shape, lambda k: (0, 0, 0))
    outs = [(like((slots, KVH * HD), BF16), narrow), (shape, folded)]
    flops = 2 * upstream.size * TILE
    return per_head(probs_kernel, "probs", [folded, masks_spec, wide] + [ANY] * len(after), outs, (scores, masks, upstream, *after), flops)


def attention_dscore(probs, values, upstream, queries, keys):
    wide, narrow, folded, _ = attention_specs(queries.shape[0])
    token = (TOKEN, pl.BlockSpec(TOKEN.shape, lambda k: (0, 0)))
    outs = [(like(queries.shape, BF16), wide), (like(keys.shape, BF16), narrow), token]
    args = (probs, values, upstream, queries, keys)
    flops = 6 * upstream.size * TILE
    return per_head(dscore_kernel, "dscore", [folded, narrow, wide, wide, narrow], outs, args, flops)


def slice_of(weights, s):
    half = weights.shape[1] // NZH
    rows = slice(s // NX * half, (s // NX + 1) * half)
    return jnp.concatenate([weights[cr * NX + s % NX, rows] for cr in range(NCO)], axis=0)


def partial_kernel(*refs):
    ins, (v0, v1, v2, v3, x, w, sems) = refs[: NY + SLICES], refs[NY + SLICES :]
    rows, width = x.shape[1], w.shape[1]
    copies = fetch(ins, [x.at[k] for k in range(NY)] + [w.at[i] for i in range(SLICES)], sems)
    for copy in copies:
        copy.wait()
    total = None
    for s in range(SLICES):
        stack = jnp.concatenate([x[k, :, s * width : (s + 1) * width] for k in range(NY)], axis=0)
        term = dot(stack, slice_of(w, s), (1, 0))
        total = term if total is None else total + term
    for k, out in enumerate((v0, v1, v2, v3)):
        out[...] = total[k * rows : (k + 1) * rows].astype(out.dtype)


def staged(*groups):
    stacks = [pltpu.VMEM((len(g), *g[0].shape), g[0].dtype) for g in groups]
    return (*stacks, pltpu.SemaphoreType.DMA((sum(map(len, groups)),)))


def partial_values(pieces, weights):
    rows, width = pieces[0].shape[0], weights[0].shape[1]
    out = [like((rows, width), F32)] + [like((rows, width), BF16)] * (NY - 1)
    flops = 2 * NY * pieces[0].size * width
    ins, scratch = [ANY] * (NY + SLICES), staged(pieces, weights)
    return call(partial_kernel, "partial_values", out, *pieces, *weights, ins=ins, scratch=scratch, mib=56, flops=flops)


def place_kernel(slot, own, a, b, c, after, out):
    rows = own[...] + a[...].astype(F32) + b[...].astype(F32) + c[...].astype(F32)
    at = lax.broadcasted_iota(jnp.int32, (out.shape[0], own.shape[0]), 0)
    chosen = jnp.where(at == slot[...], 1.0, 0.0).astype(BF16)
    out[...] = dot(chosen, rows.astype(BF16), (1, 0)).astype(BF16)


def pick_kernel(*refs):
    slot, buffer, out = refs[0], refs[1], refs[-1]
    at = lax.broadcasted_iota(jnp.int32, (buffer.shape[0], out.shape[0]), 0)
    chosen = jnp.where(at == slot[...], 1.0, 0.0).astype(BF16)
    out[...] = dot(chosen, buffer[...], (0, 0)).astype(BF16)


def back_kernel(*refs):
    ins, (_, g0, g1, g2, g3, r, w, sems) = refs[: NY + SLICES], refs[NY + SLICES :]
    rows, width = r.shape[1], w.shape[1]
    copies = fetch(ins, [r.at[k] for k in range(NY)] + [w.at[i] for i in range(SLICES)], sems)
    for copy in copies:
        copy.wait()
    stack = r[...].reshape(NY * rows, r.shape[2])
    for s in range(SLICES):
        grad = dot(stack, slice_of(w, s), (1, 1)).astype(BF16)
        for k, out in enumerate((g0, g1, g2, g3)):
            out[:, s * width : (s + 1) * width] = grad[k * rows : (k + 1) * rows]


def back(grads, weights, after):
    rows, width = grads[0].shape
    columns = SLICES * weights[0].shape[0]
    flops = 2 * NY * rows * width * columns
    ins, scratch = [ANY] * (NY + SLICES + 1), staged(grads, weights)
    out = [like((rows, columns), BF16)] * NY
    return call(back_kernel, "back", out, *grads, *weights, after, ins=ins, scratch=scratch, mib=56, flops=flops)


def share_kernel(*refs):
    ins, (_, own, other, x, r, sems) = refs[: 2 * NY], refs[2 * NY :]
    half = own.shape[1]
    copies = fetch(ins, [x.at[k] for k in range(NY)] + [r.at[k] for k in range(NY)], sems)
    for copy in copies:
        copy.wait()
    grads = r[...].reshape(NY * r.shape[1], r.shape[2])
    for s in range(SLICES):
        stack = jnp.concatenate([x[k, :, s * NCO * half : (s + 1) * NCO * half] for k in range(NY)], axis=0)
        share = dot(stack, grads, (0, 0))
        own[s] = share[:half]
        other[s] = share[half:].astype(other.dtype)


def shares(pieces, grads, after):
    half, width = pieces[0].shape[1] // SLICES // NCO, grads[0].shape[1]
    shape = (SLICES, half, width)
    flops = 2 * NY * pieces[0].size * width
    out = [like(shape, F32), like(shape, BF16)]
    ins, scratch = [ANY] * (2 * NY + 1), staged(pieces, grads)
    return call(share_kernel, "shares", out, *pieces, *grads, after, ins=ins, scratch=scratch, mib=20, flops=flops)


def core_sum_kernel(own, got, keep, s1, s2, s3):
    for zr in range(NZH):
        for xr, out in enumerate((keep, s1, s2, s3)):
            out[zr] = (own[zr * NX + xr] + got[zr * NX + xr].astype(F32)).astype(out.dtype)


def x_sum_kernel(keep, a, b, c, p1, p2, p3, near, far):
    for zr, out in enumerate((near, far)):
        total = keep[zr] + a[zr].astype(F32) + b[zr].astype(F32) + c[zr].astype(F32)
        out[...] = total.astype(out.dtype)


def stack_kernel(a, b, out):
    rows = a.shape[0]
    out[:rows] = a[...]
    out[rows:] = b[...]


def pair_sum_kernel(*refs):
    a, b, out = refs[0], refs[1], refs[-1]
    out[...] = (a[...].astype(F32) + b[...].astype(F32)).astype(out.dtype)


def halves_kernel(mine, other, out):
    core, rows = at_place()[0], mine.shape[0]
    out[pl.ds(pl.multiple_of(core * rows, rows), rows), :] = mine[...]
    out[pl.ds(pl.multiple_of((1 - core) * rows, rows), rows), :] = other[...]


def body(inputs, value_weight, send_slot, response_id, queries, keys, upstream):
    peers = lax.axis_size("fsdp")
    slots, rows = queries.shape[0], inputs.shape[0]
    half, width = value_weight.shape[0] // NCO, value_weight.shape[1]
    slot = send_slot.reshape(1, rows)

    def exchange(buffer):
        return lax.all_to_all(buffer, "fsdp", split_axis=0, concat_axis=0, tiled=True)

    *pieces, near = split(inputs, value_weight)
    masks = exchange(run_masks(send_slot, response_id, peers, near))
    pieces = [pieces[0]] + [permute(pieces[k], along_y(k)) for k in range(1, NY)]
    pair = call(stack_kernel, "pair", [like((NZH * half, width), BF16)], near, permute(near, mirror))[0]
    weights = [pair] + [permute(pair, along_x(k)) for k in range(1, NX)]
    weights += [permute(weight, other_core) for weight in weights]

    scores = attention_scores(queries, keys)
    grad_v, probs = attention_probs(scores, masks, upstream, (pair, pieces[1], pieces[3]))
    returned = exchange(grad_v)
    after = (pieces[2], *weights[1:NX])
    order, out = [VMEM] * 2 + [ANY] * NX, [like((rows, width), BF16)]
    row_grad = call(pick_kernel, "pick", out, slot, returned, *after, ins=order)[0]
    grads = [row_grad] + [permute(row_grad, along_y(k)) for k in range(1, NY)]

    partial, *parts = partial_values(pieces, weights)
    own, other = shares(pieces, grads, parts[0])
    got = permute(other, other_core)
    out = [like((NZH, half, width), F32)] + [like((NZH, half, width), BF16)] * (NX - 1)
    keep, *sends = call(core_sum_kernel, "core_sum", out, own, got, mib=8)
    arrived = [permute(send, along_x(-k)) for k, send in enumerate(sends, 1)]

    mine, *sends = back(grads, weights, keep)
    parts = [permute(part, along_y(-k)) for k, part in enumerate(parts, 1)]
    columns = [mine] + [permute(send, along_y(-k)) for k, send in enumerate(sends, 1)]

    order, out = [VMEM] * NX + [ANY] * (NY - 1), [like((half, width), F32), like((half, width), BF16)]
    near, far = call(x_sum_kernel, "x_sum", out, keep, *arrived, *parts, ins=order)
    order, out = [VMEM] * 5 + [ANY], [like((slots, width), BF16)]
    value_buffer = call(place_kernel, "place", out, slot, partial, *parts, near, ins=order)[0]
    values = exchange(value_buffer)
    grad_q, grad_k, scored = attention_dscore(probs, values, upstream, queries, keys)
    grad_inputs, joined = join(columns)

    small, order = [like((half, width), BF16)], [VMEM, VMEM, ANY]
    total = call(pair_sum_kernel, "mirror_sum", small, near, permute(far, mirror), scored, ins=order)[0]
    total = call(pair_sum_kernel, "z_sum", small, total, permute(total, flip_zl(1)), joined, ins=order)[0]
    total = call(pair_sum_kernel, "z_sum", small, total, permute(total, flip_zl(2)))[0]
    out = [like((NCO * half, width), BF16)]
    grad_weight = call(halves_kernel, "halves", out, total, permute(total, other_core))[0]
    return grad_inputs, grad_q, grad_k, grad_weight


def solution(mesh):
    spread, sharded = P(("rep", "fsdp"), None), P("fsdp", None)
    line = P(("rep", "fsdp"))
    return jax.shard_map(
        body,
        mesh=mesh,
        in_specs=(spread, sharded, line, line, spread, spread, spread),
        out_specs=(spread, spread, spread, sharded),
        check_vma=False,
    )
```

profile of v0, /device:TPU:1, one launch (start us, length us, event | category | flops | bytes accessed | tf_op | source)
XLA Modules:
  0.0 163.0 jit_solution(9325548478937007163)
XLA Ops:
  0.6 3.5 %split.1 = (bf16[128,2048]{1,0:T(8,128)(2,1)}, bf16[128,2048]{1,0:T(8,128)(2,1)}, bf16[128,2048]{1,0:T(8,128)(2,1)}, bf16[128,2048]{1,0:T(8,128)(2,1)}, bf16[128,512]{1,0:T(8,128)(2,1)}) custom-call(bf16[128,8192]{1,0:T(8,128)(2,1)} %full_in.1, bf16[256,512]{1,0:T(8,128)(2,1)} %weight_in.1), custom_call_target="tpu_custom_call" | custom-call | bytes 4587520 | tf_op jit(solution)/shard_map/split/pallas_call | solution.py:55
  4.2 2.2 %collective-permute-start.1 = (bf16[128,2048]{1,0:T(8,128)(2,1)}, bf16[128,2048]{1,0:T(8,128)(2,1)S(1)}, u32[]{:S(2)}, u32[]{:S(2)}) collective-permute-start(bf16[128,2048]{1,0:T(8,128)(2,1)} %get-tuple-element.33), channel_id=1, source_target_pairs={{0,1},{1,2},{2,3},{3,0},{4,5},{5,6},{6,7},{7,4},{8,9},{9,10},{10,1... | collective-permute-start | bytes 1572872 | tf_op jit(solution)/shard_map/ppermute | solution.py:30
  9.3 12.3 %all-to-all-start = ((s32[32,8,128]{2,1,0:T(8,128)}), s32[32,8,128]{2,1,0:T(8,128)S(1)}, u32[]{:S(2)}, u32[]{:S(2)}) async-start(s32[32,8,128]{2,1,0:T(8,128)} %masks.1), calls=%async_computation | async-start | bytes 262144 | tf_op jit(solution)/shard_map/all_to_all | solution.py:395
  21.6 3.9 %collective-permute-start = (bf16[128,512]{1,0:T(8,128)(2,1)}, bf16[128,512]{1,0:T(8,128)(2,1)S(1)}, u32[]{:S(2)}, u32[]{:S(2)}) collective-permute-start(bf16[128,512]{1,0:T(8,128)(2,1)} %get-tuple-element.32.after.a), channel_id=1, source_target_pairs={{0,208},{1,209},{2,210},{3,211},{4,212},{5,213},{6,214},{7,215},{8... | collective-permute-start | bytes 393224 | tf_op jit(solution)/shard_map/ppermute | solution.py:30
  25.5 2.7 %collective-permute-start.3 = (bf16[128,2048]{1,0:T(8,128)(2,1)}, bf16[128,2048]{1,0:T(8,128)(2,1)S(1)}, u32[]{:S(2)}, u32[]{:S(2)}) collective-permute-start(bf16[128,2048]{1,0:T(8,128)(2,1)} %get-tuple-element.36), channel_id=1, source_target_pairs={{0,2},{1,3},{2,0},{3,1},{4,6},{5,7},{6,4},{7,5},{8,10},{9,11},{10,... | collective-permute-start | bytes 1572872 | tf_op jit(solution)/shard_map/ppermute | solution.py:30
  28.2 4.0 %scores.1 = f32[4,2,8,1024]{3,2,1,0:T(8,128)} custom-call(bf16[256,4096]{1,0:T(8,128)(2,1)} %queries.3, bf16[256,512]{1,0:T(8,128)(2,1)} %keys.3), custom_call_target="tpu_custom_call" | custom-call | flops 268435456 | bytes 2621440 | tf_op jit(solution)/shard_map/scores/pallas_call | solution.py:222
  32.2 2.9 %collective-permute-done.b = bf16[128,512]{1,0:T(8,128)(2,1)S(1)} collective-permute-done((bf16[128,512]{1,0:T(8,128)(2,1)}, bf16[128,512]{1,0:T(8,128)(2,1)S(1)}, u32[]{:S(2)}, u32[]{:S(2)}) %collective-permute-start) | collective-permute-done | bytes 131104 | tf_op jit(solution)/shard_map/ppermute | solution.py:30
  38.0 4.2 %probs.1 = (bf16[256,512]{1,0:T(8,128)(2,1)}, f32[4,2,8,1024]{3,2,1,0:T(8,128)}) custom-call(f32[4,2,8,1024]{3,2,1,0:T(8,128)} %scores.1, s32[32,8,128]{2,1,0:T(8,128)} %copy-done.26, bf16[256,4096]{1,0:T(8,128)(2,1)} %upstream.3, bf16[256,512]{1,0:T(8,128)(2,1)} %copy-done, bf16[128,2048]{1,0:T(8,128)(2,1)} %copy-done.3, bf16[128,2048]{1,0:T(8,128)(2,1)} %copy-done.5), custom_call_target="tpu_custom_call" | custom-call | flops 268435456 | bytes 4325376 | tf_op jit(solution)/shard_map/probs/pallas_call | solution.py:222
  42.2 6.9 %all-to-all-start.1 = ((bf16[32,8,512]{2,1,0:T(8,128)(2,1)}), bf16[32,8,512]{2,1,0:T(8,128)(2,1)S(1)}, u32[]{:S(2)}, u32[]{:S(2)}) async-start(bf16[32,8,512]{2,1,0:T(8,128)(2,1)} %bitcast.9), calls=%async_computation.1 | async-start | bytes 524288 | tf_op jit(solution)/shard_map/all_to_all | solution.py:395
  49.1 2.8 %collective-permute-start.5 = (bf16[256,512]{1,0:T(8,128)(2,1)}, bf16[256,512]{1,0:T(8,128)(2,1)S(1)}, u32[]{:S(2)}, u32[]{:S(2)}) collective-permute-start(bf16[256,512]{1,0:T(8,128)(2,1)} %copy-done), channel_id=1, source_target_pairs={{0,8},{1,9},{2,10},{3,11},{4,12},{5,13},{6,14},{7,15},{8,0},{9,1},... | collective-permute-start | bytes 786440 | tf_op jit(solution)/shard_map/ppermute | solution.py:30
  52.8 2.7 %collective-permute-start.10 = (bf16[256,512]{1,0:T(8,128)(2,1)}, bf16[256,512]{1,0:T(8,128)(2,1)S(1)}, u32[]{:S(2)}, u32[]{:S(2)}) collective-permute-start(bf16[256,512]{1,0:T(8,128)(2,1)} %copy-done), channel_id=1, source_target_pairs={{0,32},{1,33},{2,34},{3,35},{4,36},{5,37},{6,38},{7,39},{8,40},{9,... | collective-permute-start | bytes 786440 | tf_op jit(solution)/shard_map/ppermute | solution.py:30
  55.6 2.2 %collective-permute-done.5.refs_4_.refs_6_ = bf16[256,512]{1,0:T(8,128)(2,1)S(1)} collective-permute-done((bf16[256,512]{1,0:T(8,128)(2,1)}, bf16[256,512]{1,0:T(8,128)(2,1)S(1)}, u32[]{:S(2)}, u32[]{:S(2)}) %collective-permute-start.5) | collective-permute-done | bytes 262176 | tf_op jit(solution)/shard_map/ppermute | solution.py:30
  57.8 3.7 %collective-permute-start.12 = (bf16[256,512]{1,0:T(8,128)(2,1)S(1)}, bf16[256,512]{1,0:T(8,128)(2,1)S(1)}, u32[]{:S(2)}, u32[]{:S(2)}) collective-permute-start(bf16[256,512]{1,0:T(8,128)(2,1)S(1)} %collective-permute-done.5.refs_4_.refs_6_), channel_id=1, source_target_pairs={{0,32},{1,33},{2,34},{3,35},{4,36},{5,37},{6,38},{7,39},{8,40},{9,... | collective-permute-start | bytes 786440 | tf_op jit(solution)/shard_map/ppermute | solution.py:30
  61.4 4.2 %collective-permute-done.6.refs_5_.refs_7_ = bf16[256,512]{1,0:T(8,128)(2,1)S(1)} collective-permute-done((bf16[256,512]{1,0:T(8,128)(2,1)}, bf16[256,512]{1,0:T(8,128)(2,1)S(1)}, u32[]{:S(2)}, u32[]{:S(2)}) %collective-permute-start.6) | collective-permute-done | bytes 262176 | tf_op jit(solution)/shard_map/ppermute | solution.py:30
  68.9 2.4 %collective-permute-start.8 = (bf16[128,512]{1,0:T(8,128)(2,1)S(1)}, bf16[128,512]{1,0:T(8,128)(2,1)S(1)}, u32[]{:S(2)}, u32[]{:S(2)}) collective-permute-start(bf16[128,512]{1,0:T(8,128)(2,1)S(1)} %pick.1.refs_4_.refs_0_), channel_id=1, source_target_pairs={{0,2},{1,3},{2,0},{3,1},{4,6},{5,7},{6,4},{7,5},{8,10},{9,11},{10,... | collective-permute-start | bytes 393224 | tf_op jit(solution)/shard_map/ppermute | solution.py:30
  73.3 4.4 %partial_values.1 = (f32[128,512]{1,0:T(8,128)}, bf16[128,512]{1,0:T(8,128)(2,1)}, bf16[128,512]{1,0:T(8,128)(2,1)}, bf16[128,512]{1,0:T(8,128)(2,1)}) custom-call(bf16[128,2048]{1,0:T(8,128)(2,1)} %get-tuple-element.37.refs_0_, bf16[128,2048]{1,0:T(8,128)(2,1)} %copy-done.3, bf16[128,2048]{1,0:T(8,128)(2,1)} %copy-done.1, bf16[128,2048]{1,0:T(8,128)(2,1)} %copy-done.5, ...), custom_call_target="tpu_custom_call" | custom-call | flops 1073741824 | bytes 4849664 | tf_op jit(solution)/shard_map/partial_values/pallas_call | solution.py:55
  79.8 2.2 %shares.1 = (f32[8,128,512]{2,1,0:T(8,128)S(1)}, bf16[8,128,512]{2,1,0:T(8,128)(2,1)S(1)}) custom-call(bf16[128,2048]{1,0:T(8,128)(2,1)S(1)} %copy-done.12, bf16[128,2048]{1,0:T(8,128)(2,1)S(1)} %copy-done.4, bf16[128,2048]{1,0:T(8,128)(2,1)S(1)} %copy-done.2, bf16[128,2048]{1,0:T(8,128)(2,1)S(1)} %copy-done.6, bf16[128,512]{1,0:T(8,128)(2,1)S(1)} %pick.1.refs_4_.refs_0_, ...), custom_call_target="tpu_custom_call" | custom-call | flops 1073741824 | bytes 5898240 | tf_op jit(solution)/shard_map/shares/pallas_call | solution.py:55
  83.0 2.1 %collective-permute-start.18 = (bf16[128,512]{1,0:T(8,128)(2,1)S(1)}, bf16[128,512]{1,0:T(8,128)(2,1)S(1)}, u32[]{:S(2)}, u32[]{:S(2)}) collective-permute-start(bf16[128,512]{1,0:T(8,128)(2,1)S(1)} %copy-done.21), channel_id=1, source_target_pairs={{0,3},{1,0},{2,1},{3,2},{4,7},{5,4},{6,5},{7,6},{8,11},{9,8},{10,9... | collective-permute-start | bytes 393224 | tf_op jit(solution)/shard_map/ppermute | solution.py:30
  85.5 2.3 %collective-permute-start.21 = (bf16[2,128,512]{2,1,0:T(8,128)(2,1)S(1)}, bf16[2,128,512]{2,1,0:T(8,128)(2,1)S(1)}, u32[]{:S(2)}, u32[]{:S(2)}) collective-permute-start(bf16[2,128,512]{2,1,0:T(8,128)(2,1)S(1)} %get-tuple-element.51), channel_id=1, source_target_pairs={{0,12},{1,13},{2,14},{3,15},{4,0},{5,1},{6,2},{7,3},{8,4},{9,5},{1... | collective-permute-start | bytes 786440 | tf_op jit(solution)/shard_map/ppermute | solution.py:30
  88.5 2.4 %collective-permute-start.19 = (bf16[128,512]{1,0:T(8,128)(2,1)S(1)}, bf16[128,512]{1,0:T(8,128)(2,1)S(1)}, u32[]{:S(2)}, u32[]{:S(2)}) collective-permute-start(bf16[128,512]{1,0:T(8,128)(2,1)S(1)} %copy-done.32), channel_id=1, source_target_pairs={{0,2},{1,3},{2,0},{3,1},{4,6},{5,7},{6,4},{7,5},{8,10},{9,11},{10,... | collective-permute-start | bytes 393224 | tf_op jit(solution)/shard_map/ppermute | solution.py:30
  91.1 3.0 %collective-permute-done.19.p2.b = bf16[128,512]{1,0:T(8,128)(2,1)S(1)} collective-permute-done((bf16[128,512]{1,0:T(8,128)(2,1)S(1)}, bf16[128,512]{1,0:T(8,128)(2,1)S(1)}, u32[]{:S(2)}, u32[]{:S(2)}) %collective-permute-start.19) | collective-permute-done | bytes 131104 | tf_op jit(solution)/shard_map/ppermute | solution.py:30
  94.1 3.5 %collective-permute-done.20.p3.c = bf16[128,512]{1,0:T(8,128)(2,1)S(1)} collective-permute-done((bf16[128,512]{1,0:T(8,128)(2,1)S(1)}, bf16[128,512]{1,0:T(8,128)(2,1)S(1)}, u32[]{:S(2)}, u32[]{:S(2)}) %collective-permute-start.20) | collective-permute-done | bytes 131104 | tf_op jit(solution)/shard_map/ppermute | solution.py:30
  97.6 5.5 %collective-permute-done.23.c = bf16[2,128,512]{2,1,0:T(8,128)(2,1)S(1)} collective-permute-done((bf16[2,128,512]{2,1,0:T(8,128)(2,1)S(1)}, bf16[2,128,512]{2,1,0:T(8,128)(2,1)S(1)}, u32[]{:S(2)}, u32[]{:S(2)}) %collective-permute-start.23) | collective-permute-done | bytes 262176 | tf_op jit(solution)/shard_map/ppermute | solution.py:30
  104.2 8.6 %all-to-all-start.2 = ((bf16[32,8,512]{2,1,0:T(8,128)(2,1)}), bf16[32,8,512]{2,1,0:T(8,128)(2,1)S(1)}, u32[]{:S(2)}, u32[]{:S(2)}) async-start(bf16[32,8,512]{2,1,0:T(8,128)(2,1)} %bitcast.3), calls=%async_computation.2 | async-start | bytes 524288 | tf_op jit(solution)/shard_map/all_to_all | solution.py:395
  112.8 4.4 %back.1 = (bf16[128,2048]{1,0:T(8,128)(2,1)}, bf16[128,2048]{1,0:T(8,128)(2,1)}, bf16[128,2048]{1,0:T(8,128)(2,1)}, bf16[128,2048]{1,0:T(8,128)(2,1)}) custom-call(bf16[128,512]{1,0:T(8,128)(2,1)} %copy-done.14, bf16[128,512]{1,0:T(8,128)(2,1)} %copy-done.18, bf16[128,512]{1,0:T(8,128)(2,1)} %copy-done.19, bf16[128,512]{1,0:T(8,128)(2,1)} %copy-done.20, ...), custom_call_target="tpu_custom_call" | custom-call | flops 1073741824 | bytes 5242880 | tf_op jit(solution)/shard_map/back/pallas_call | solution.py:55
  117.2 2.5 %collective-permute-start.15 = (bf16[128,2048]{1,0:T(8,128)(2,1)}, bf16[128,2048]{1,0:T(8,128)(2,1)S(1)}, u32[]{:S(2)}, u32[]{:S(2)}) collective-permute-start(bf16[128,2048]{1,0:T(8,128)(2,1)} %get-tuple-element.43), channel_id=1, source_target_pairs={{0,3},{1,0},{2,1},{3,2},{4,7},{5,4},{6,5},{7,6},{8,11},{9,8},{10,9... | collective-permute-start | bytes 1572872 | tf_op jit(solution)/shard_map/ppermute | solution.py:30
  120.9 3.8 %collective-permute-start.24 = (bf16[128,512]{1,0:T(8,128)(2,1)S(1)}, bf16[128,512]{1,0:T(8,128)(2,1)S(1)}, u32[]{:S(2)}, u32[]{:S(2)}) collective-permute-start(bf16[128,512]{1,0:T(8,128)(2,1)S(1)} %get-tuple-element.57), channel_id=1, source_target_pairs={{0,208},{1,209},{2,210},{3,211},{4,212},{5,213},{6,214},{7,215},{8... | collective-permute-start | bytes 393224 | tf_op jit(solution)/shard_map/ppermute | solution.py:30
  125.7 6.4 %dscore.1 = (bf16[256,4096]{1,0:T(8,128)(2,1)}, bf16[256,512]{1,0:T(8,128)(2,1)}, f32[8,128]{1,0:T(8,128)}) custom-call(f32[4,2,8,1024]{3,2,1,0:T(8,128)} %get-tuple-element.47.probs, bf16[256,512]{1,0:T(8,128)(2,1)} %bitcast.8, bf16[256,4096]{1,0:T(8,128)(2,1)} %upstream.3, bf16[256,4096]{1,0:T(8,128)(2,1)} %queries.3, bf16[256,512]{1,0:T(8,128)(2,1)} %keys.3), custom_call_target="tpu_custom_call" | custom-call | flops 805306368 | bytes 7344128 | tf_op jit(solution)/shard_map/dscore/pallas_call | solution.py:222
  132.9 2.1 %collective-permute-done.16.p2 = bf16[128,2048]{1,0:T(8,128)(2,1)S(1)} collective-permute-done((bf16[128,2048]{1,0:T(8,128)(2,1)}, bf16[128,2048]{1,0:T(8,128)(2,1)S(1)}, u32[]{:S(2)}, u32[]{:S(2)}) %collective-permute-start.16) | collective-permute-done | bytes 524320 | tf_op jit(solution)/shard_map/ppermute | solution.py:30
  135.0 12.4 %collective-permute-done.17.p3 = bf16[128,2048]{1,0:T(8,128)(2,1)S(1)} collective-permute-done((bf16[128,2048]{1,0:T(8,128)(2,1)}, bf16[128,2048]{1,0:T(8,128)(2,1)S(1)}, u32[]{:S(2)}, u32[]{:S(2)}) %collective-permute-start.17) | collective-permute-done | bytes 524320 | tf_op jit(solution)/shard_map/ppermute | solution.py:30
  148.2 3.3 %join.1 = (bf16[128,8192]{1,0:T(8,128)(2,1)}, f32[8,128]{1,0:T(8,128)}) custom-call(bf16[128,2048]{1,0:T(8,128)(2,1)} %get-tuple-element.42.p0, bf16[128,2048]{1,0:T(8,128)(2,1)} %copy-done.23, bf16[128,2048]{1,0:T(8,128)(2,1)} %copy-done.24, bf16[128,2048]{1,0:T(8,128)(2,1)} %copy-done.25), custom_call_target="tpu_custom_call" | custom-call | bytes 4198400 | tf_op jit(solution)/shard_map/join/pallas_call | solution.py:55
  152.3 8.4 %collective-permute-done.26.refs_1_ = bf16[128,512]{1,0:T(8,128)(2,1)S(1)} collective-permute-done((bf16[128,512]{1,0:T(8,128)(2,1)S(1)}, bf16[128,512]{1,0:T(8,128)(2,1)S(1)}, u32[]{:S(2)}, u32[]{:S(2)}) %collective-permute-start.26) | collective-permute-done | bytes 131104 | tf_op jit(solution)/shard_map/ppermute | solution.py:30
  (114 shorter events, 24.4 us)
Async XLA Ops:
  4.2 32.2 %collective-permute-start.1 = (bf16[128,2048]{1,0:T(8,128)(2,1)}, bf16[128,2048]{1,0:T(8,128)(2,1)S(1)}, u32[]{:S(2)}, u32[]{:S(2)}) collective-permute-start(bf16[128,2048]{1,0:T(8,128)(2,1)} %get-tuple-element.33), channel_id=1, source_target_pairs={{0,1},{1,2},{2,3},{3,0},{4,5},{5,6},{6,7},{7,4},{8,9},{9,10},{10,1... | collective-permute-start | bytes 1572872 | tf_op jit(solution)/shard_map/ppermute | solution.py:30
  6.4 30.1 %collective-permute-start.2 = (bf16[128,2048]{1,0:T(8,128)(2,1)}, bf16[128,2048]{1,0:T(8,128)(2,1)S(1)}, u32[]{:S(2)}, u32[]{:S(2)}) collective-permute-start(bf16[128,2048]{1,0:T(8,128)(2,1)} %get-tuple-element.34), channel_id=1, source_target_pairs={{0,3},{1,0},{2,1},{3,2},{4,7},{5,4},{6,5},{7,6},{8,11},{9,8},{10,9... | collective-permute-start | bytes 1572872 | tf_op jit(solution)/shard_map/ppermute | solution.py:30
  9.3 27.1 %all-to-all-start = ((s32[32,8,128]{2,1,0:T(8,128)}), s32[32,8,128]{2,1,0:T(8,128)S(1)}, u32[]{:S(2)}, u32[]{:S(2)}) async-start(s32[32,8,128]{2,1,0:T(8,128)} %masks.1), calls=%async_computation | async-start | bytes 262144 | tf_op jit(solution)/shard_map/all_to_all | solution.py:395
  21.6 13.4 %collective-permute-start = (bf16[128,512]{1,0:T(8,128)(2,1)}, bf16[128,512]{1,0:T(8,128)(2,1)S(1)}, u32[]{:S(2)}, u32[]{:S(2)}) collective-permute-start(bf16[128,512]{1,0:T(8,128)(2,1)} %get-tuple-element.32.after.a), channel_id=1, source_target_pairs={{0,208},{1,209},{2,210},{3,211},{4,212},{5,213},{6,214},{7,215},{8... | collective-permute-start | bytes 393224 | tf_op jit(solution)/shard_map/ppermute | solution.py:30
  25.5 42.0 %collective-permute-start.3 = (bf16[128,2048]{1,0:T(8,128)(2,1)}, bf16[128,2048]{1,0:T(8,128)(2,1)S(1)}, u32[]{:S(2)}, u32[]{:S(2)}) collective-permute-start(bf16[128,2048]{1,0:T(8,128)(2,1)} %get-tuple-element.36), channel_id=1, source_target_pairs={{0,2},{1,3},{2,0},{3,1},{4,6},{5,7},{6,4},{7,5},{8,10},{9,11},{10,... | collective-permute-start | bytes 1572872 | tf_op jit(solution)/shard_map/ppermute | solution.py:30
  35.1 32.4 %copy-start.15 = (s32[128]{0:T(128)S(1)}, s32[128]{0:T(128)}, u32[]{:S(2)}) copy-start(s32[128]{0:T(128)} %slots_in.1) | copy-start | bytes 1540
  35.1 20.4 %collective-permute-start.4 = (bf16[256,512]{1,0:T(8,128)(2,1)S(1)}, bf16[256,512]{1,0:T(8,128)(2,1)S(1)}, u32[]{:S(2)}, u32[]{:S(2)}) collective-permute-start(bf16[256,512]{1,0:T(8,128)(2,1)S(1)} %pair.1.rest_0_.refs_4_), channel_id=1, source_target_pairs={{0,4},{1,5},{2,6},{3,7},{4,8},{5,9},{6,10},{7,11},{8,12},{9,13},{1... | collective-permute-start | bytes 786440 | tf_op jit(solution)/shard_map/ppermute | solution.py:30
  42.2 25.3 %all-to-all-start.1 = ((bf16[32,8,512]{2,1,0:T(8,128)(2,1)}), bf16[32,8,512]{2,1,0:T(8,128)(2,1)S(1)}, u32[]{:S(2)}, u32[]{:S(2)}) async-start(bf16[32,8,512]{2,1,0:T(8,128)(2,1)} %bitcast.9), calls=%async_computation.1 | async-start | bytes 524288 | tf_op jit(solution)/shard_map/all_to_all | solution.py:395
  49.1 8.7 %collective-permute-start.5 = (bf16[256,512]{1,0:T(8,128)(2,1)}, bf16[256,512]{1,0:T(8,128)(2,1)S(1)}, u32[]{:S(2)}, u32[]{:S(2)}) collective-permute-start(bf16[256,512]{1,0:T(8,128)(2,1)} %copy-done), channel_id=1, source_target_pairs={{0,8},{1,9},{2,10},{3,11},{4,12},{5,13},{6,14},{7,15},{8,0},{9,1},... | collective-permute-start | bytes 786440 | tf_op jit(solution)/shard_map/ppermute | solution.py:30
  51.9 13.7 %collective-permute-start.6 = (bf16[256,512]{1,0:T(8,128)(2,1)}, bf16[256,512]{1,0:T(8,128)(2,1)S(1)}, u32[]{:S(2)}, u32[]{:S(2)}) collective-permute-start(bf16[256,512]{1,0:T(8,128)(2,1)} %copy-done), channel_id=1, source_target_pairs={{0,12},{1,13},{2,14},{3,15},{4,0},{5,1},{6,2},{7,3},{8,4},{9,5},{1... | collective-permute-start | bytes 786440 | tf_op jit(solution)/shard_map/ppermute | solution.py:30
  52.8 16.1 %collective-permute-start.10 = (bf16[256,512]{1,0:T(8,128)(2,1)}, bf16[256,512]{1,0:T(8,128)(2,1)S(1)}, u32[]{:S(2)}, u32[]{:S(2)}) collective-permute-start(bf16[256,512]{1,0:T(8,128)(2,1)} %copy-done), channel_id=1, source_target_pairs={{0,32},{1,33},{2,34},{3,35},{4,36},{5,37},{6,38},{7,39},{8,40},{9,... | collective-permute-start | bytes 786440 | tf_op jit(solution)/shard_map/ppermute | solution.py:30
  55.5 15.8 %collective-permute-start.11 = (bf16[256,512]{1,0:T(8,128)(2,1)S(1)}, bf16[256,512]{1,0:T(8,128)(2,1)S(1)}, u32[]{:S(2)}, u32[]{:S(2)}) collective-permute-start(bf16[256,512]{1,0:T(8,128)(2,1)S(1)} %collective-permute-done.4.refs_3_.refs_5_), channel_id=1, source_target_pairs={{0,32},{1,33},{2,34},{3,35},{4,36},{5,37},{6,38},{7,39},{8,40},{9,... | collective-permute-start | bytes 786440 | tf_op jit(solution)/shard_map/ppermute | solution.py:30
  57.8 14.7 %collective-permute-start.12 = (bf16[256,512]{1,0:T(8,128)(2,1)S(1)}, bf16[256,512]{1,0:T(8,128)(2,1)S(1)}, u32[]{:S(2)}, u32[]{:S(2)}) collective-permute-start(bf16[256,512]{1,0:T(8,128)(2,1)S(1)} %collective-permute-done.5.refs_4_.refs_6_), channel_id=1, source_target_pairs={{0,32},{1,33},{2,34},{3,35},{4,36},{5,37},{6,38},{7,39},{8,40},{9,... | collective-permute-start | bytes 786440 | tf_op jit(solution)/shard_map/ppermute | solution.py:30
  65.6 6.9 %collective-permute-start.13 = (bf16[256,512]{1,0:T(8,128)(2,1)S(1)}, bf16[256,512]{1,0:T(8,128)(2,1)S(1)}, u32[]{:S(2)}, u32[]{:S(2)}) collective-permute-start(bf16[256,512]{1,0:T(8,128)(2,1)S(1)} %collective-permute-done.6.refs_5_.refs_7_), channel_id=1, source_target_pairs={{0,32},{1,33},{2,34},{3,35},{4,36},{5,37},{6,38},{7,39},{8,40},{9,... | collective-permute-start | bytes 786440 | tf_op jit(solution)/shard_map/ppermute | solution.py:30
  67.7 10.0 %collective-permute-start.7 = (bf16[128,512]{1,0:T(8,128)(2,1)S(1)}, bf16[128,512]{1,0:T(8,128)(2,1)S(1)}, u32[]{:S(2)}, u32[]{:S(2)}) collective-permute-start(bf16[128,512]{1,0:T(8,128)(2,1)S(1)} %pick.1.refs_4_.refs_0_), channel_id=1, source_target_pairs={{0,1},{1,2},{2,3},{3,0},{4,5},{5,6},{6,7},{7,4},{8,9},{9,10},{10,1... | collective-permute-start | bytes 393224 | tf_op jit(solution)/shard_map/ppermute | solution.py:30
  68.9 8.8 %collective-permute-start.8 = (bf16[128,512]{1,0:T(8,128)(2,1)S(1)}, bf16[128,512]{1,0:T(8,128)(2,1)S(1)}, u32[]{:S(2)}, u32[]{:S(2)}) collective-permute-start(bf16[128,512]{1,0:T(8,128)(2,1)S(1)} %pick.1.refs_4_.refs_0_), channel_id=1, source_target_pairs={{0,2},{1,3},{2,0},{3,1},{4,6},{5,7},{6,4},{7,5},{8,10},{9,11},{10,... | collective-permute-start | bytes 393224 | tf_op jit(solution)/shard_map/ppermute | solution.py:30
  71.3 6.4 %collective-permute-start.9 = (bf16[128,512]{1,0:T(8,128)(2,1)S(1)}, bf16[128,512]{1,0:T(8,128)(2,1)S(1)}, u32[]{:S(2)}, u32[]{:S(2)}) collective-permute-start(bf16[128,512]{1,0:T(8,128)(2,1)S(1)} %pick.1.refs_4_.refs_0_), channel_id=1, source_target_pairs={{0,3},{1,0},{2,1},{3,2},{4,7},{5,4},{6,5},{7,6},{8,11},{9,8},{10,9... | collective-permute-start | bytes 393224 | tf_op jit(solution)/shard_map/ppermute | solution.py:30
  82.0 3.2 %collective-permute-start.14 = (bf16[8,128,512]{2,1,0:T(8,128)(2,1)S(1)}, bf16[8,128,512]{2,1,0:T(8,128)(2,1)S(1)}, u32[]{:S(2)}, u32[]{:S(2)}) collective-permute-start(bf16[8,128,512]{2,1,0:T(8,128)(2,1)S(1)} %get-tuple-element.40), channel_id=1, source_target_pairs={{0,32},{1,33},{2,34},{3,35},{4,36},{5,37},{6,38},{7,39},{8,40},{9,... | collective-permute-start | bytes 3145736 | tf_op jit(solution)/shard_map/ppermute | solution.py:30
  83.0 7.9 %collective-permute-start.18 = (bf16[128,512]{1,0:T(8,128)(2,1)S(1)}, bf16[128,512]{1,0:T(8,128)(2,1)S(1)}, u32[]{:S(2)}, u32[]{:S(2)}) collective-permute-start(bf16[128,512]{1,0:T(8,128)(2,1)S(1)} %copy-done.21), channel_id=1, source_target_pairs={{0,3},{1,0},{2,1},{3,2},{4,7},{5,4},{6,5},{7,6},{8,11},{9,8},{10,9... | collective-permute-start | bytes 393224 | tf_op jit(solution)/shard_map/ppermute | solution.py:30
  85.5 12.1 %collective-permute-start.21 = (bf16[2,128,512]{2,1,0:T(8,128)(2,1)S(1)}, bf16[2,128,512]{2,1,0:T(8,128)(2,1)S(1)}, u32[]{:S(2)}, u32[]{:S(2)}) collective-permute-start(bf16[2,128,512]{2,1,0:T(8,128)(2,1)S(1)} %get-tuple-element.51), channel_id=1, source_target_pairs={{0,12},{1,13},{2,14},{3,15},{4,0},{5,1},{6,2},{7,3},{8,4},{9,5},{1... | collective-permute-start | bytes 786440 | tf_op jit(solution)/shard_map/ppermute | solution.py:30
  87.7 9.9 %collective-permute-start.22 = (bf16[2,128,512]{2,1,0:T(8,128)(2,1)S(1)}, bf16[2,128,512]{2,1,0:T(8,128)(2,1)S(1)}, u32[]{:S(2)}, u32[]{:S(2)}) collective-permute-start(bf16[2,128,512]{2,1,0:T(8,128)(2,1)S(1)} %get-tuple-element.52), channel_id=1, source_target_pairs={{0,8},{1,9},{2,10},{3,11},{4,12},{5,13},{6,14},{7,15},{8,0},{9,1},... | collective-permute-start | bytes 786440 | tf_op jit(solution)/shard_map/ppermute | solution.py:30
  88.5 14.6 %collective-permute-start.23 = (bf16[2,128,512]{2,1,0:T(8,128)(2,1)S(1)}, bf16[2,128,512]{2,1,0:T(8,128)(2,1)S(1)}, u32[]{:S(2)}, u32[]{:S(2)}) collective-permute-start(bf16[2,128,512]{2,1,0:T(8,128)(2,1)S(1)} %get-tuple-element.53), channel_id=1, source_target_pairs={{0,4},{1,5},{2,6},{3,7},{4,8},{5,9},{6,10},{7,11},{8,12},{9,13},{1... | collective-permute-start | bytes 786440 | tf_op jit(solution)/shard_map/ppermute | solution.py:30
  88.5 5.6 %collective-permute-start.19 = (bf16[128,512]{1,0:T(8,128)(2,1)S(1)}, bf16[128,512]{1,0:T(8,128)(2,1)S(1)}, u32[]{:S(2)}, u32[]{:S(2)}) collective-permute-start(bf16[128,512]{1,0:T(8,128)(2,1)S(1)} %copy-done.32), channel_id=1, source_target_pairs={{0,2},{1,3},{2,0},{3,1},{4,6},{5,7},{6,4},{7,5},{8,10},{9,11},{10,... | collective-permute-start | bytes 393224 | tf_op jit(solution)/shard_map/ppermute | solution.py:30
  90.9 6.7 %collective-permute-start.20 = (bf16[128,512]{1,0:T(8,128)(2,1)S(1)}, bf16[128,512]{1,0:T(8,128)(2,1)S(1)}, u32[]{:S(2)}, u32[]{:S(2)}) collective-permute-start(bf16[128,512]{1,0:T(8,128)(2,1)S(1)} %copy-done.31), channel_id=1, source_target_pairs={{0,1},{1,2},{2,3},{3,0},{4,5},{5,6},{6,7},{7,4},{8,9},{9,10},{10,1... | collective-permute-start | bytes 393224 | tf_op jit(solution)/shard_map/ppermute | solution.py:30
  104.2 20.8 %all-to-all-start.2 = ((bf16[32,8,512]{2,1,0:T(8,128)(2,1)}), bf16[32,8,512]{2,1,0:T(8,128)(2,1)S(1)}, u32[]{:S(2)}, u32[]{:S(2)}) async-start(bf16[32,8,512]{2,1,0:T(8,128)(2,1)} %bitcast.3), calls=%async_computation.2 | async-start | bytes 524288 | tf_op jit(solution)/shard_map/all_to_all | solution.py:395
  117.2 15.7 %collective-permute-start.15 = (bf16[128,2048]{1,0:T(8,128)(2,1)}, bf16[128,2048]{1,0:T(8,128)(2,1)S(1)}, u32[]{:S(2)}, u32[]{:S(2)}) collective-permute-start(bf16[128,2048]{1,0:T(8,128)(2,1)} %get-tuple-element.43), channel_id=1, source_target_pairs={{0,3},{1,0},{2,1},{3,2},{4,7},{5,4},{6,5},{7,6},{8,11},{9,8},{10,9... | collective-permute-start | bytes 1572872 | tf_op jit(solution)/shard_map/ppermute | solution.py:30
  119.7 15.3 %collective-permute-start.16 = (bf16[128,2048]{1,0:T(8,128)(2,1)}, bf16[128,2048]{1,0:T(8,128)(2,1)S(1)}, u32[]{:S(2)}, u32[]{:S(2)}) collective-permute-start(bf16[128,2048]{1,0:T(8,128)(2,1)} %get-tuple-element.44), channel_id=1, source_target_pairs={{0,2},{1,3},{2,0},{3,1},{4,6},{5,7},{6,4},{7,5},{8,10},{9,11},{10,... | collective-permute-start | bytes 1572872 | tf_op jit(solution)/shard_map/ppermute | solution.py:30
  120.3 27.1 %collective-permute-start.17 = (bf16[128,2048]{1,0:T(8,128)(2,1)}, bf16[128,2048]{1,0:T(8,128)(2,1)S(1)}, u32[]{:S(2)}, u32[]{:S(2)}) collective-permute-start(bf16[128,2048]{1,0:T(8,128)(2,1)} %get-tuple-element.45), channel_id=1, source_target_pairs={{0,1},{1,2},{2,3},{3,0},{4,5},{5,6},{6,7},{7,4},{8,9},{9,10},{10,1... | collective-permute-start | bytes 1572872 | tf_op jit(solution)/shard_map/ppermute | solution.py:30
  120.9 11.2 %collective-permute-start.24 = (bf16[128,512]{1,0:T(8,128)(2,1)S(1)}, bf16[128,512]{1,0:T(8,128)(2,1)S(1)}, u32[]{:S(2)}, u32[]{:S(2)}) collective-permute-start(bf16[128,512]{1,0:T(8,128)(2,1)S(1)} %get-tuple-element.57), channel_id=1, source_target_pairs={{0,208},{1,209},{2,210},{3,211},{4,212},{5,213},{6,214},{7,215},{8... | collective-permute-start | bytes 393224 | tf_op jit(solution)/shard_map/ppermute | solution.py:30
  132.8 18.7 %collective-permute-start.25 = (bf16[128,512]{1,0:T(8,128)(2,1)S(1)}, bf16[128,512]{1,0:T(8,128)(2,1)S(1)}, u32[]{:S(2)}, u32[]{:S(2)}) collective-permute-start(bf16[128,512]{1,0:T(8,128)(2,1)S(1)} %mirror_sum.1.refs_0_), channel_id=1, source_target_pairs={{0,64},{1,65},{2,66},{3,67},{4,68},{5,69},{6,70},{7,71},{8,72},{9,... | collective-permute-start | bytes 393224 | tf_op jit(solution)/shard_map/ppermute | solution.py:30
  152.2 8.5 %collective-permute-start.26 = (bf16[128,512]{1,0:T(8,128)(2,1)S(1)}, bf16[128,512]{1,0:T(8,128)(2,1)S(1)}, u32[]{:S(2)}, u32[]{:S(2)}) collective-permute-start(bf16[128,512]{1,0:T(8,128)(2,1)S(1)} %z_sum.2.refs_0_), channel_id=1, source_target_pairs={{0,128},{1,129},{2,130},{3,131},{4,132},{5,133},{6,134},{7,135},{8... | collective-permute-start | bytes 393224 | tf_op jit(solution)/shard_map/ppermute | solution.py:30
  160.7 1.6 collective-permute-start.27
  (32 other events, 223.6 us)
where the time goes:
time: 164 us; the launch traced here: 163 us
  starting transfers between devices  73.1 us (45%)
  waiting for transfers between devices  45.5 us (28%)
  Pallas kernels  36 us (22%)
  local copies, waits for them, and re-layouts  7.29 us (4%)
    ppermute x28, starting transfers between devices, permute(): return lax.ppermute(array, AXES, pairs)  45.3 us
    ppermute x28, waiting for transfers between devices, permute(): return lax.ppermute(array, AXES, pairs)  45.2 us
    all_to_all x3, starting transfers between devices, exchange(): lax.all_to_all(buffer, 'fsdp', split_axis=0, concat_axis=0, tiled=True)  27.8 us
    pallas_call x15, Pallas kernels, call(): pl.pallas_call(kernel, out_shape=out, in_specs=[VMEM] * len(args) if ins...  21.5 us
    pallas_call x3, Pallas kernels, per_head(): pl.pallas_call(kernel, grid=(KVH,), out_shape=[o for o, _ in outs], in_sp...  14.6 us
    unnamed x66, local copies, waits for them, and re-layouts  7.29 us
  transfers between devices with their start and end apart: 31, of which 13 were waited for; matrix products, arithmetic and copies ran while one was open for 0% of the time, Pallas kernels for 17%

commit v1 on v0

--- a/solution.py
+++ b/solution.py
@@ -98,7 +98,7 @@
     token[...] = jnp.zeros(token.shape, token.dtype)
 
 
-def masks_kernel(slots_in, ids_in, after, masks, slots, ids, sems):
+def masks_kernel(slots_in, ids_in, masks, slots, ids, sems):
     copies = fetch((slots_in, ids_in), (slots, ids), sems)
     lane = lax.broadcasted_iota(jnp.int32, (CAP, TILE), 1) & (CAP - 1)
     sub = lax.broadcasted_iota(jnp.int32, (CAP, TILE), 0)
@@ -118,30 +118,27 @@
         masks[lax.div(slots[r * CAP], CAP)] = jnp.where((keys == rows) & causal, 1, 0)
 
 
-def run_masks(slots, ids, peers, after):
+def run_masks(slots, ids, peers):
     index = pltpu.SMEM(slots.shape, jnp.int32)
     scratch = (index, index, pltpu.SemaphoreType.DMA((2,)))
     out = [like((peers, CAP, TILE), jnp.int32)]
-    return call(masks_kernel, "masks", out, slots, ids, after, ins=[ANY] * 3, scratch=scratch, mib=56)[0]
-
-
-def split_kernel(full_in, weight_in, p0, p1, p2, p3, weight, full, sems):
-    rows = weight.shape[0]
-    here = weight_in.at[pl.ds(pl.multiple_of(at_place()[0] * rows, rows), rows)]
-    copies = fetch((full_in, here), (full, weight), sems)
-    copies[0].wait()
+    return call(masks_kernel, "masks", out, slots, ids, ins=[ANY] * 2, scratch=scratch, mib=56)[0]
+
+
+def split_kernel(full_in, after, p0, p1, p2, p3, full, sems):
+    for copy in fetch((full_in,), (full,), sems):
+        copy.wait()
     width = full.shape[1] // (NY * SLICES * NCO)
     for k, part in enumerate((p0, p1, p2, p3)):
         for at, block in feature_blocks(k):
             part[:, at * width : (at + 1) * width] = full[:, pl.ds(pl.multiple_of(block * width, width), width)]
-    copies[1].wait()
-
-
-def split(full, weight):
+
+
+def split(full, after):
     rows, columns = full.shape
-    out = [like((rows, columns // NY), full.dtype)] * NY + [like((weight.shape[0] // NCO, weight.shape[1]), weight.dtype)]
-    scratch = (pltpu.VMEM(full.shape, full.dtype), pltpu.SemaphoreType.DMA((2,)))
-    return call(split_kernel, "split", out, full, weight, ins=[ANY] * 2, scratch=scratch, mib=56)
+    out = [like((rows, columns // NY), full.dtype)] * NY
+    scratch = (pltpu.VMEM(full.shape, full.dtype), pltpu.SemaphoreType.DMA((1,)))
+    return call(split_kernel, "split", out, full, after, ins=[ANY] * 2, scratch=scratch, mib=56)
 
 
 def join_kernel(p0, p1, p2, p3, full, token):
@@ -177,28 +174,45 @@
     return jnp.concatenate([jnp.where(block == b, folded, 0.0) for b in range(BLOCKS)], axis=0).astype(BF16)
 
 
-def scores_kernel(queries, keys, scores):
+def head_blocks(array):
+    width = GROUP * HD
+    return [array.at[:, pl.ds(k * width, width)] for k in range(KVH)]
+
+
+def scores_kernel(queries, keys_in, scores, q, keys, sems):
+    copies = fetch([keys_in] + head_blocks(queries), [keys] + [q.at[k] for k in range(KVH)], sems)
     block = own_block(GROUP * TILE)
-    for t in range(scores.shape[1]):
-        pairs = dot(keys[t * TILE : (t + 1) * TILE, :], heads(queries, t), (1, 1))
-        scores[0, t] = fold(pairs, block)
-
-
-def probs_kernel(scores, masks, upstream, *rest):
-    grad_v, probs = rest[-2:]
+    copies[0].wait()
+    for k in range(KVH):
+        copies[1 + k].wait()
+        for t in range(scores.shape[1]):
+            pairs = dot(keys[t * TILE : (t + 1) * TILE, k * HD : (k + 1) * HD], heads(q[k], t), (1, 1))
+            scores[k, t] = fold(pairs, block)
+
+
+def probs_kernel(scores_in, masks_in, upstream, *rest):
+    grad_v, probs, u, scores, masks, sems = rest[-6:]
+    sources = [scores_in, masks_in] + head_blocks(upstream)
+    copies = fetch(sources, [scores, masks] + [u.at[k] for k in range(KVH)], sems)
     small, block = own_block(TILE), own_block(GROUP * TILE)
+    copies[0].wait()
+    copies[1].wait()
+    seen = []
     for t in range(scores.shape[1]):
         mask = masks[t * BLOCKS]
         for b in range(1, BLOCKS):
             mask = jnp.where(small == b, masks[t * BLOCKS + b], mask)
-        visible = jnp.concatenate([mask] * GROUP, axis=1) != 0
-        masked = jnp.where(visible, scores[0, t] * (1.0 / HD**0.5), -1e30)
-        top = jnp.max(masked, axis=0, keepdims=True)
-        expo = jnp.where(visible, jnp.exp(masked - top), 0.0)
-        prob = expo / jnp.sum(expo, axis=0, keepdims=True)
-        probs[0, t] = prob
-        grad = dot(unfold(prob, block), heads(upstream, t), (1, 0))
-        grad_v[t * TILE : (t + 1) * TILE, :] = grad.astype(BF16)
+        seen.append(jnp.concatenate([mask] * GROUP, axis=1) != 0)
+    for k in range(KVH):
+        copies[2 + k].wait()
+        for t, visible in enumerate(seen):
+            masked = jnp.where(visible, scores[k, t] * (1.0 / HD**0.5), -1e30)
+            top = jnp.max(masked, axis=0, keepdims=True)
+            expo = jnp.where(visible, jnp.exp(masked - top), 0.0)
+            prob = expo / jnp.sum(expo, axis=0, keepdims=True)
+            probs[k, t] = prob
+            grad = dot(unfold(prob, block), heads(u[k], t), (1, 0))
+            grad_v[t * TILE : (t + 1) * TILE, k * HD : (k + 1) * HD] = grad.astype(BF16)
 
 
 def dscore_kernel(probs, values, upstream, queries, keys, grad_q, grad_k, token):
@@ -239,19 +253,28 @@
     return wide, narrow, folded, like((KVH, tiles, CAP, GROUP * TILE), F32)
 
 
+def folded_shape(slots):
+    return (KVH, slots // TILE, CAP, GROUP * TILE)
+
+
 def attention_scores(queries, keys):
-    wide, narrow, folded, shape = attention_specs(queries.shape[0])
+    slots = queries.shape[0]
+    sems = pltpu.SemaphoreType.DMA((1 + KVH,))
+    scratch = (pltpu.VMEM((KVH, slots, GROUP * HD), BF16), pltpu.VMEM(keys.shape, BF16), sems)
+    out = [like(folded_shape(slots), F32)]
     flops = 2 * queries.size * TILE
-    return per_head(scores_kernel, "scores", [wide, narrow], [(shape, folded)], (queries, keys), flops)[0]
+    return call(scores_kernel, "scores", out, queries, keys, ins=[ANY] * 2, scratch=scratch, mib=56, flops=flops)[0]
 
 
 def attention_probs(scores, masks, upstream, after):
     slots = upstream.shape[0]
-    wide, narrow, folded, shape = attention_specs(slots)
-    masks_spec = pl.BlockSpec(masks.shape, lambda k: (0, 0, 0))
-    outs = [(like((slots, KVH * HD), BF16), narrow), (shape, folded)]
+    u = pltpu.VMEM((KVH, slots, GROUP * HD), BF16)
+    sems = pltpu.SemaphoreType.DMA((2 + KVH,))
+    scratch = (u, pltpu.VMEM(scores.shape, F32), pltpu.VMEM(masks.shape, jnp.int32), sems)
+    out = [like((slots, KVH * HD), BF16), like(scores.shape, F32)]
     flops = 2 * upstream.size * TILE
-    return per_head(probs_kernel, "probs", [folded, masks_spec, wide] + [ANY] * len(after), outs, (scores, masks, upstream, *after), flops)
+    ins = [ANY] * (3 + len(after))
+    return call(probs_kernel, "probs", out, scores, masks, upstream, *after, ins=ins, scratch=scratch, mib=56, flops=flops)
 
 
 def attention_dscore(probs, values, upstream, queries, keys):
@@ -270,7 +293,7 @@
 
 
 def partial_kernel(*refs):
-    ins, (v0, v1, v2, v3, x, w, sems) = refs[: NY + SLICES], refs[NY + SLICES :]
+    ins, (_, v0, v1, v2, v3, x, w, sems) = refs[: NY + SLICES], refs[NY + SLICES :]
     rows, width = x.shape[1], w.shape[1]
     copies = fetch(ins, [x.at[k] for k in range(NY)] + [w.at[i] for i in range(SLICES)], sems)
     for copy in copies:
@@ -289,12 +312,12 @@
     return (*stacks, pltpu.SemaphoreType.DMA((sum(map(len, groups)),)))
 
 
-def partial_values(pieces, weights):
+def partial_values(pieces, weights, after):
     rows, width = pieces[0].shape[0], weights[0].shape[1]
     out = [like((rows, width), F32)] + [like((rows, width), BF16)] * (NY - 1)
     flops = 2 * NY * pieces[0].size * width
-    ins, scratch = [ANY] * (NY + SLICES), staged(pieces, weights)
-    return call(partial_kernel, "partial_values", out, *pieces, *weights, ins=ins, scratch=scratch, mib=56, flops=flops)
+    ins, scratch = [ANY] * (NY + SLICES + 1), staged(pieces, weights)
+    return call(partial_kernel, "partial_values", out, *pieces, *weights, after, ins=ins, scratch=scratch, mib=56, flops=flops)
 
 
 def place_kernel(slot, own, a, b, c, after, out):
@@ -312,7 +335,8 @@
 
 
 def back_kernel(*refs):
-    ins, (_, g0, g1, g2, g3, r, w, sems) = refs[: NY + SLICES], refs[NY + SLICES :]
+    ins, (_, g0, g1, g2, g3, token, r, w, sems) = refs[: NY + SLICES], refs[NY + SLICES :]
+    finish(token)
     rows, width = r.shape[1], w.shape[1]
     copies = fetch(ins, [r.at[k] for k in range(NY)] + [w.at[i] for i in range(SLICES)], sems)
     for copy in copies:
@@ -329,12 +353,13 @@
     columns = SLICES * weights[0].shape[0]
     flops = 2 * NY * rows * width * columns
     ins, scratch = [ANY] * (NY + SLICES + 1), staged(grads, weights)
-    out = [like((rows, columns), BF16)] * NY
+    out = [like((rows, columns), BF16)] * NY + [TOKEN]
     return call(back_kernel, "back", out, *grads, *weights, after, ins=ins, scratch=scratch, mib=56, flops=flops)
 
 
 def share_kernel(*refs):
-    ins, (_, own, other, x, r, sems) = refs[: 2 * NY], refs[2 * NY :]
+    ins, (own, other, token, x, r, sems) = refs[: 2 * NY], refs[-6:]
+    finish(token)
     half = own.shape[1]
     copies = fetch(ins, [x.at[k] for k in range(NY)] + [r.at[k] for k in range(NY)], sems)
     for copy in copies:
@@ -351,9 +376,9 @@
     half, width = pieces[0].shape[1] // SLICES // NCO, grads[0].shape[1]
     shape = (SLICES, half, width)
     flops = 2 * NY * pieces[0].size * width
-    out = [like(shape, F32), like(shape, BF16)]
-    ins, scratch = [ANY] * (2 * NY + 1), staged(pieces, grads)
-    return call(share_kernel, "shares", out, *pieces, *grads, after, ins=ins, scratch=scratch, mib=20, flops=flops)
+    out = [like(shape, F32), like(shape, BF16), TOKEN]
+    ins, scratch = [ANY] * (2 * NY + len(after)), staged(pieces, grads)
+    return call(share_kernel, "shares", out, *pieces, *grads, *after, ins=ins, scratch=scratch, mib=20, flops=flops)
 
 
 def core_sum_kernel(own, got, keep, s1, s2, s3):
@@ -362,16 +387,17 @@
             out[zr] = (own[zr * NX + xr] + got[zr * NX + xr].astype(F32)).astype(out.dtype)
 
 
-def x_sum_kernel(keep, a, b, c, p1, p2, p3, near, far):
+def x_sum_kernel(keep, a, b, c, after, near, far):
     for zr, out in enumerate((near, far)):
         total = keep[zr] + a[zr].astype(F32) + b[zr].astype(F32) + c[zr].astype(F32)
         out[...] = total.astype(out.dtype)
 
 
 def stack_kernel(a, b, out):
-    rows = a.shape[0]
-    out[:rows] = a[...]
-    out[rows:] = b[...]
+    rows = a.shape[0] // NCO
+    here = pl.ds(pl.multiple_of(at_place()[0] * rows, rows), rows)
+    out[:rows] = a[here, :]
+    out[rows:] = b[here, :]
 
 
 def pair_sum_kernel(*refs):
@@ -379,7 +405,7 @@
     out[...] = (a[...].astype(F32) + b[...].astype(F32)).astype(out.dtype)
 
 
-def halves_kernel(mine, other, out):
+def halves_kernel(mine, other, after, out):
     core, rows = at_place()[0], mine.shape[0]
     out[pl.ds(pl.multiple_of(core * rows, rows), rows), :] = mine[...]
     out[pl.ds(pl.multiple_of((1 - core) * rows, rows), rows), :] = other[...]
@@ -394,46 +420,49 @@
     def exchange(buffer):
         return lax.all_to_all(buffer, "fsdp", split_axis=0, concat_axis=0, tiled=True)
 
-    *pieces, near = split(inputs, value_weight)
-    masks = exchange(run_masks(send_slot, response_id, peers, near))
+    mask = run_masks(send_slot, response_id, peers)
+    masks = exchange(mask)
+    mirrored = permute(value_weight, mirror)
+    pieces = split(inputs, mask)
     pieces = [pieces[0]] + [permute(pieces[k], along_y(k)) for k in range(1, NY)]
-    pair = call(stack_kernel, "pair", [like((NZH * half, width), BF16)], near, permute(near, mirror))[0]
+    pair = call(stack_kernel, "pair", [like((NZH * half, width), BF16)], value_weight, mirrored)[0]
     weights = [pair] + [permute(pair, along_x(k)) for k in range(1, NX)]
     weights += [permute(weight, other_core) for weight in weights]
 
     scores = attention_scores(queries, keys)
-    grad_v, probs = attention_probs(scores, masks, upstream, (pair, pieces[1], pieces[3]))
+    grad_v, probs = attention_probs(scores, masks, upstream, (pair,))
     returned = exchange(grad_v)
-    after = (pieces[2], *weights[1:NX])
-    order, out = [VMEM] * 2 + [ANY] * NX, [like((rows, width), BF16)]
-    row_grad = call(pick_kernel, "pick", out, slot, returned, *after, ins=order)[0]
+    order, out = [VMEM] * 2 + [ANY] * (NY - 1), [like((rows, width), BF16)]
+    row_grad = call(pick_kernel, "pick", out, slot, returned, *pieces[1:], ins=order)[0]
     grads = [row_grad] + [permute(row_grad, along_y(k)) for k in range(1, NY)]
 
-    partial, *parts = partial_values(pieces, weights)
-    own, other = shares(pieces, grads, parts[0])
+    own, other, shared = shares(pieces, grads, weights[1:NX])
+    partial, *parts = partial_values(pieces, weights, shared)
+    parts = [permute(part, along_y(-k)) for k, part in enumerate(parts, 1)]
     got = permute(other, other_core)
     out = [like((NZH, half, width), F32)] + [like((NZH, half, width), BF16)] * (NX - 1)
     keep, *sends = call(core_sum_kernel, "core_sum", out, own, got, mib=8)
     arrived = [permute(send, along_x(-k)) for k, send in enumerate(sends, 1)]
 
-    mine, *sends = back(grads, weights, keep)
-    parts = [permute(part, along_y(-k)) for k, part in enumerate(parts, 1)]
+    mine, *sends, backed = back(grads, weights, keep)
     columns = [mine] + [permute(send, along_y(-k)) for k, send in enumerate(sends, 1)]
 
-    order, out = [VMEM] * NX + [ANY] * (NY - 1), [like((half, width), F32), like((half, width), BF16)]
-    near, far = call(x_sum_kernel, "x_sum", out, keep, *arrived, *parts, ins=order)
-    order, out = [VMEM] * 5 + [ANY], [like((slots, width), BF16)]
-    value_buffer = call(place_kernel, "place", out, slot, partial, *parts, near, ins=order)[0]
+    out = [like((half, width), F32), like((half, width), BF16)]
+    near, far = call(x_sum_kernel, "x_sum", out, keep, *arrived, backed, ins=[VMEM] * NX + [ANY])
+    small, order = [like((half, width), BF16)], [VMEM, VMEM, ANY]
+    total = call(pair_sum_kernel, "mirror_sum", small, near, permute(far, mirror), *parts, ins=[VMEM] * 2 + [ANY] * (NY - 1))[0]
+
+    after, out = [VMEM] * 5 + [ANY], [like((slots, width), BF16)]
+    value_buffer = call(place_kernel, "place", out, slot, partial, *parts, total, ins=after)[0]
     values = exchange(value_buffer)
     grad_q, grad_k, scored = attention_dscore(probs, values, upstream, queries, keys)
     grad_inputs, joined = join(columns)
 
-    small, order = [like((half, width), BF16)], [VMEM, VMEM, ANY]
-    total = call(pair_sum_kernel, "mirror_sum", small, near, permute(far, mirror), scored, ins=order)[0]
-    total = call(pair_sum_kernel, "z_sum", small, total, permute(total, flip_zl(1)), joined, ins=order)[0]
+    after = [VMEM] * 2 + [ANY] * NY
+    total = call(pair_sum_kernel, "z_sum", small, total, permute(total, flip_zl(1)), scored, *columns[1:], ins=after)[0]
     total = call(pair_sum_kernel, "z_sum", small, total, permute(total, flip_zl(2)))[0]
     out = [like((NCO * half, width), BF16)]
-    grad_weight = call(halves_kernel, "halves", out, total, permute(total, other_core))[0]
+    grad_weight = call(halves_kernel, "halves", out, total, permute(total, other_core), joined, ins=order)[0]
     return grad_inputs, grad_q, grad_k, grad_weight
 
 

time: 164 us -> 152 us (0.927)
  starting transfers between devices: 73.1 us -> 67.4 us
  waiting for transfers between devices: 45.5 us -> 43.4 us
  Pallas kernels: 36 us -> 34.2 us
    ppermute x28, waiting for transfers between devices: 45.2 us -> 31.1 us  [permute(): return lax.ppermute(array, AXES, pairs)]
    all_to_all x3, waiting for transfers between devices: 0.29 us -> 12.2 us  [exchange(): lax.all_to_all(buffer, 'fsdp', split_axis=0, concat_axis=0, tiled=True)]
    pallas_call x3 -> x1, Pallas kernels: 14.6 us -> 6.41 us  [per_head(): pl.pallas_call(kernel, grid=(KVH,), out_shape=[o for o, _ in outs], in_sp...]
    pallas_call x15 -> x17, Pallas kernels: 21.5 us -> 27.8 us  [call(): pl.pallas_call(kernel, out_shape=out, in_specs=[VMEM] * len(args) if ins...]
    all_to_all x3, starting transfers between devices: 27.8 us -> 24.5 us  [exchange(): lax.all_to_all(buffer, 'fsdp', split_axis=0, concat_axis=0, tiled=True)]
    ppermute x28, starting transfers between devices: 45.3 us -> 42.9 us  [permute(): return lax.ppermute(array, AXES, pairs)]
    unnamed x66 -> x68, local copies, waits for them, and re-layouts: 7.29 us -> 5.75 us
  transfers between devices with their start and end apart: 31 -> 31, of which waited for: 13 -> 12; matrix products, arithmetic and copies ran while one was open for 0% -> 0% of each run, Pallas kernels for 17% -> 20%
where the time goes in v1:
time: 152 us
  starting transfers between devices  67.4 us (44%)
  waiting for transfers between devices  43.4 us (29%)
  Pallas kernels  34.2 us (23%)
  local copies, waits for them, and re-layouts  5.75 us (4%)
    ppermute x28, starting transfers between devices, permute(): return lax.ppermute(array, AXES, pairs)  42.9 us
    ppermute x28, waiting for transfers between devices, permute(): return lax.ppermute(array, AXES, pairs)  31.1 us
    pallas_call x17, Pallas kernels, call(): pl.pallas_call(kernel, out_shape=out, in_specs=[VMEM] * len(args) if ins...  27.8 us
    all_to_all x3, starting transfers between devices, exchange(): lax.all_to_all(buffer, 'fsdp', split_axis=0, concat_axis=0, tiled=True)  24.5 us
    all_to_all x3, waiting for transfers between devices, exchange(): lax.all_to_all(buffer, 'fsdp', split_axis=0, concat_axis=0, tiled=True)  12.2 us
    pallas_call x1, Pallas kernels, per_head(): pl.pallas_call(kernel, grid=(KVH,), out_shape=[o for o, _ in outs], in_sp...  6.41 us
    unnamed x68, local copies, waits for them, and re-layouts  5.75 us
  transfers between devices with their start and end apart: 31, of which 12 were waited for; matrix products, arithmetic and copies ran while one was open for 0% of the time, Pallas kernels for 20%

profile of v1, /device:TPU:1, one launch (start us, length us, event | category | flops | bytes accessed | tf_op | source)
XLA Modules:
  0.0 151.8 jit_solution(9044114007103108904)
XLA Ops:
  0.6 6.5 %collective-permute-start = (bf16[256,512]{1,0:T(8,128)(2,1)}, bf16[256,512]{1,0:T(8,128)(2,1)S(1)}, u32[]{:S(2)}, u32[]{:S(2)}) collective-permute-start(bf16[256,512]{1,0:T(8,128)(2,1)} %a.1), channel_id=1, source_target_pairs={{0,208},{1,209},{2,210},{3,211},{4,212},{5,213},{6,214},{7,215},{8... | collective-permute-start | bytes 786440 | tf_op jit(solution)/shard_map/ppermute | solution.py:30
  7.1 1.4 masks.1.after
  8.5 8.1 %all-to-all-start = ((s32[32,8,128]{2,1,0:T(8,128)}), s32[32,8,128]{2,1,0:T(8,128)S(1)}, u32[]{:S(2)}, u32[]{:S(2)}) async-start(s32[32,8,128]{2,1,0:T(8,128)} %masks.1.after), calls=%async_computation | async-start | bytes 262144 | tf_op jit(solution)/shard_map/all_to_all | solution.py:421
  16.7 3.5 %split.1 = (bf16[128,2048]{1,0:T(8,128)(2,1)}, bf16[128,2048]{1,0:T(8,128)(2,1)}, bf16[128,2048]{1,0:T(8,128)(2,1)}, bf16[128,2048]{1,0:T(8,128)(2,1)}) custom-call(bf16[128,8192]{1,0:T(8,128)(2,1)} %full_in.1, s32[32,8,128]{2,1,0:T(8,128)} %masks.1.after), custom_call_target="tpu_custom_call" | custom-call | bytes 4325376 | tf_op jit(solution)/shard_map/split/pallas_call | solution.py:55
  20.2 1.3 collective-permute-start.1
  21.5 2.4 %collective-permute-start.2 = (bf16[128,2048]{1,0:T(8,128)(2,1)}, bf16[128,2048]{1,0:T(8,128)(2,1)S(1)}, u32[]{:S(2)}, u32[]{:S(2)}) collective-permute-start(bf16[128,2048]{1,0:T(8,128)(2,1)} %get-tuple-element.35), channel_id=1, source_target_pairs={{0,2},{1,3},{2,0},{3,1},{4,6},{5,7},{6,4},{7,5},{8,10},{9,11},{10,... | collective-permute-start | bytes 1572872 | tf_op jit(solution)/shard_map/ppermute | solution.py:30
  25.1 3.1 %scores.1.scores_in = f32[4,2,8,1024]{3,2,1,0:T(8,128)} custom-call(bf16[256,4096]{1,0:T(8,128)(2,1)} %queries.3, bf16[256,512]{1,0:T(8,128)(2,1)} %keys.1), custom_call_target="tpu_custom_call" | custom-call | flops 268435456 | bytes 2621440 | tf_op jit(solution)/shard_map/scores/pallas_call | solution.py:55
  29.6 3.3 %probs.1 = (bf16[256,512]{1,0:T(8,128)(2,1)}, f32[4,2,8,1024]{3,2,1,0:T(8,128)}) custom-call(f32[4,2,8,1024]{3,2,1,0:T(8,128)} %scores.1.scores_in, s32[32,8,128]{2,1,0:T(8,128)} %copy-done.26, bf16[256,4096]{1,0:T(8,128)(2,1)} %upstream.3, bf16[256,512]{1,0:T(8,128)(2,1)} %copy-done), custom_call_target="tpu_custom_call" | custom-call | flops 268435456 | bytes 3276800 | tf_op jit(solution)/shard_map/probs/pallas_call | solution.py:55
  32.9 9.2 %all-to-all-start.1 = ((bf16[32,8,512]{2,1,0:T(8,128)(2,1)}), bf16[32,8,512]{2,1,0:T(8,128)(2,1)S(1)}, u32[]{:S(2)}, u32[]{:S(2)}) async-start(bf16[32,8,512]{2,1,0:T(8,128)(2,1)} %bitcast.9), calls=%async_computation.1 | async-start | bytes 524288 | tf_op jit(solution)/shard_map/all_to_all | solution.py:421
  42.1 1.3 collective-permute-start.7
  43.5 2.4 %collective-permute-start.8 = (bf16[256,512]{1,0:T(8,128)(2,1)S(1)}, bf16[256,512]{1,0:T(8,128)(2,1)S(1)}, u32[]{:S(2)}, u32[]{:S(2)}) collective-permute-start(bf16[256,512]{1,0:T(8,128)(2,1)S(1)} %copy-done.1), channel_id=1, source_target_pairs={{0,8},{1,9},{2,10},{3,11},{4,12},{5,13},{6,14},{7,15},{8,0},{9,1},... | collective-permute-start | bytes 786440 | tf_op jit(solution)/shard_map/ppermute | solution.py:30
  47.4 6.8 %all-to-all-done.1 = bf16[32,8,512]{2,1,0:T(8,128)(2,1)S(1)} async-done(((bf16[32,8,512]{2,1,0:T(8,128)(2,1)}), bf16[32,8,512]{2,1,0:T(8,128)(2,1)S(1)}, u32[]{:S(2)}, u32[]{:S(2)}) %all-to-all-start.1) | async-done | bytes 262176 | tf_op jit(solution)/shard_map/all_to_all | solution.py:421
  54.5 2.2 %collective-permute-start.5 = (bf16[128,512]{1,0:T(8,128)(2,1)S(1)}, bf16[128,512]{1,0:T(8,128)(2,1)S(1)}, u32[]{:S(2)}, u32[]{:S(2)}) collective-permute-start(bf16[128,512]{1,0:T(8,128)(2,1)S(1)} %pick.1.refs_4_.refs_0_), channel_id=1, source_target_pairs={{0,2},{1,3},{2,0},{3,1},{4,6},{5,7},{6,4},{7,5},{8,10},{9,11},{10,... | collective-permute-start | bytes 393224 | tf_op jit(solution)/shard_map/ppermute | solution.py:30
  58.4 2.5 %collective-permute-done.4.refs_5_.refs_1_ = bf16[128,512]{1,0:T(8,128)(2,1)S(1)} collective-permute-done((bf16[128,512]{1,0:T(8,128)(2,1)S(1)}, bf16[128,512]{1,0:T(8,128)(2,1)S(1)}, u32[]{:S(2)}, u32[]{:S(2)}) %collective-permute-start.4) | collective-permute-done | bytes 131104 | tf_op jit(solution)/shard_map/ppermute | solution.py:30
  61.5 2.2 %shares.1 = (f32[8,128,512]{2,1,0:T(8,128)S(1)}, bf16[8,128,512]{2,1,0:T(8,128)(2,1)S(1)}, f32[8,128]{1,0:T(8,128)S(1)}) custom-call(bf16[128,2048]{1,0:T(8,128)(2,1)S(1)} %copy-done.8, bf16[128,2048]{1,0:T(8,128)(2,1)S(1)} %collective-permute-done.1.refs_2_.refs_1_, bf16[128,2048]{1,0:T(8,128)(2,1)S(1)} %collective-permute-done.2.refs_3_.refs_2_, ...), custom_call_target="tpu_custom_call" | custom-call | flops 1073741824 | bytes 6557696 | tf_op jit(solution)/shard_map/shares/pallas_call | solution.py:55
  63.7 5.3 %collective-permute-start.14 = (bf16[8,128,512]{2,1,0:T(8,128)(2,1)S(1)}, bf16[8,128,512]{2,1,0:T(8,128)(2,1)S(1)}, u32[]{:S(2)}, u32[]{:S(2)}) collective-permute-start(bf16[8,128,512]{2,1,0:T(8,128)(2,1)S(1)} %get-tuple-element.39), channel_id=1, source_target_pairs={{0,32},{1,33},{2,34},{3,35},{4,36},{5,37},{6,38},{7,39},{8,40},{9,... | collective-permute-start | bytes 3145736 | tf_op jit(solution)/shard_map/ppermute | solution.py:30
  70.0 1.3 collective-permute-done.14.got
  72.4 1.6 %collective-permute-start.21 = (bf16[2,128,512]{2,1,0:T(8,128)(2,1)S(1)}, bf16[2,128,512]{2,1,0:T(8,128)(2,1)S(1)}, u32[]{:S(2)}, u32[]{:S(2)}) collective-permute-start(bf16[2,128,512]{2,1,0:T(8,128)(2,1)S(1)} %get-tuple-element.52), channel_id=1, source_target_pairs={{0,12},{1,13},{2,14},{3,15},{4,0},{5,1},{6,2},{7,3},{8,4},{9,5},{1... | collective-permute-start | bytes 786440 | tf_op jit(solution)/shard_map/ppermute | solution.py:30
  75.5 4.2 %partial_values.1 = (f32[128,512]{1,0:T(8,128)}, bf16[128,512]{1,0:T(8,128)(2,1)}, bf16[128,512]{1,0:T(8,128)(2,1)}, bf16[128,512]{1,0:T(8,128)(2,1)}) custom-call(bf16[128,2048]{1,0:T(8,128)(2,1)} %get-tuple-element.37.refs_0_, bf16[128,2048]{1,0:T(8,128)(2,1)} %copy-done.2, bf16[128,2048]{1,0:T(8,128)(2,1)} %copy-done.3, bf16[128,2048]{1,0:T(8,128)(2,1)} %copy-done.4, ...), custom_call_target="tpu_custom_call" | custom-call | flops 1073741824 | bytes 4853760 | tf_op jit(solution)/shard_map/partial_values/pallas_call | solution.py:55
  79.8 2.3 %collective-permute-start.18 = (bf16[128,512]{1,0:T(8,128)(2,1)}, bf16[128,512]{1,0:T(8,128)(2,1)S(1)}, u32[]{:S(2)}, u32[]{:S(2)}) collective-permute-start(bf16[128,512]{1,0:T(8,128)(2,1)} %get-tuple-element.49), channel_id=1, source_target_pairs={{0,3},{1,0},{2,1},{3,2},{4,7},{5,4},{6,5},{7,6},{8,11},{9,8},{10,9... | collective-permute-start | bytes 393224 | tf_op jit(solution)/shard_map/ppermute | solution.py:30
  82.1 4.4 %back.1 = (bf16[128,2048]{1,0:T(8,128)(2,1)}, bf16[128,2048]{1,0:T(8,128)(2,1)}, bf16[128,2048]{1,0:T(8,128)(2,1)}, bf16[128,2048]{1,0:T(8,128)(2,1)}, f32[8,128]{1,0:T(8,128)}) custom-call(bf16[128,512]{1,0:T(8,128)(2,1)} %copy-done.16, bf16[128,512]{1,0:T(8,128)(2,1)} %copy-done.22, bf16[128,512]{1,0:T(8,128)(2,1)} %copy-done.23, ...), custom_call_target="tpu_custom_call" | custom-call | flops 1073741824 | bytes 5246976 | tf_op jit(solution)/shard_map/back/pallas_call | solution.py:55
  87.3 2.1 %collective-permute-done.23.c = bf16[2,128,512]{2,1,0:T(8,128)(2,1)S(1)} collective-permute-done((bf16[2,128,512]{2,1,0:T(8,128)(2,1)S(1)}, bf16[2,128,512]{2,1,0:T(8,128)(2,1)S(1)}, u32[]{:S(2)}, u32[]{:S(2)}) %collective-permute-start.23) | collective-permute-done | bytes 262176 | tf_op jit(solution)/shard_map/ppermute | solution.py:30
  91.6 4.4 %collective-permute-done.24.refs_1_ = bf16[128,512]{1,0:T(8,128)(2,1)S(1)} collective-permute-done((bf16[128,512]{1,0:T(8,128)(2,1)S(1)}, bf16[128,512]{1,0:T(8,128)(2,1)S(1)}, u32[]{:S(2)}, u32[]{:S(2)}) %collective-permute-start.24) | collective-permute-done | bytes 131104 | tf_op jit(solution)/shard_map/ppermute | solution.py:30
  97.1 7.1 %all-to-all-start.2 = ((bf16[32,8,512]{2,1,0:T(8,128)(2,1)}), bf16[32,8,512]{2,1,0:T(8,128)(2,1)S(1)}, u32[]{:S(2)}, u32[]{:S(2)}) async-start(bf16[32,8,512]{2,1,0:T(8,128)(2,1)} %bitcast.3), calls=%async_computation.2 | async-start | bytes 524288 | tf_op jit(solution)/shard_map/all_to_all | solution.py:421
  104.2 2.5 %collective-permute-start.15 = (bf16[128,2048]{1,0:T(8,128)(2,1)}, bf16[128,2048]{1,0:T(8,128)(2,1)S(1)}, u32[]{:S(2)}, u32[]{:S(2)}) collective-permute-start(bf16[128,2048]{1,0:T(8,128)(2,1)} %get-tuple-element.42), channel_id=1, source_target_pairs={{0,3},{1,0},{2,1},{3,2},{4,7},{5,4},{6,5},{7,6},{8,11},{9,8},{10,9... | collective-permute-start | bytes 1572872 | tf_op jit(solution)/shard_map/ppermute | solution.py:30
  107.9 2.9 %collective-permute-start.25 = (bf16[128,512]{1,0:T(8,128)(2,1)S(1)}, bf16[128,512]{1,0:T(8,128)(2,1)S(1)}, u32[]{:S(2)}, u32[]{:S(2)}) collective-permute-start(bf16[128,512]{1,0:T(8,128)(2,1)S(1)} %mirror_sum.1.after.refs_0_), channel_id=1, source_target_pairs={{0,64},{1,65},{2,66},{3,67},{4,68},{5,69},{6,70},{7,71},{8,72},{9,... | collective-permute-start | bytes 393224 | tf_op jit(solution)/shard_map/ppermute | solution.py:30
  110.8 5.4 %all-to-all-done.2 = bf16[32,8,512]{2,1,0:T(8,128)(2,1)S(1)} async-done(((bf16[32,8,512]{2,1,0:T(8,128)(2,1)}), bf16[32,8,512]{2,1,0:T(8,128)(2,1)S(1)}, u32[]{:S(2)}, u32[]{:S(2)}) %all-to-all-start.2) | async-done | bytes 262176 | tf_op jit(solution)/shard_map/all_to_all | solution.py:421
  116.9 6.4 %dscore.1 = (bf16[256,4096]{1,0:T(8,128)(2,1)}, bf16[256,512]{1,0:T(8,128)(2,1)}, f32[8,128]{1,0:T(8,128)}) custom-call(f32[4,2,8,1024]{3,2,1,0:T(8,128)} %get-tuple-element.46.probs, bf16[256,512]{1,0:T(8,128)(2,1)} %bitcast.8, bf16[256,4096]{1,0:T(8,128)(2,1)} %upstream.3, bf16[256,4096]{1,0:T(8,128)(2,1)} %queries.3, bf16[256,512]{1,0:T(8,128)(2,1)} %keys.1), custom_call_target="tpu_custom_call" | custom-call | flops 805306368 | bytes 7344128 | tf_op jit(solution)/shard_map/dscore/pallas_call | solution.py:236
  123.4 12.0 %collective-permute-done.17.p3.refs_5_ = bf16[128,2048]{1,0:T(8,128)(2,1)S(1)} collective-permute-done((bf16[128,2048]{1,0:T(8,128)(2,1)S(1)}, bf16[128,2048]{1,0:T(8,128)(2,1)S(1)}, u32[]{:S(2)}, u32[]{:S(2)}) %collective-permute-start.17) | collective-permute-done | bytes 524320 | tf_op jit(solution)/shard_map/ppermute | solution.py:30
  136.1 3.5 %collective-permute-start.26 = (bf16[128,512]{1,0:T(8,128)(2,1)S(1)}, bf16[128,512]{1,0:T(8,128)(2,1)S(1)}, u32[]{:S(2)}, u32[]{:S(2)}) collective-permute-start(bf16[128,512]{1,0:T(8,128)(2,1)S(1)} %z_sum.2.refs_0_), channel_id=1, source_target_pairs={{0,128},{1,129},{2,130},{3,131},{4,132},{5,133},{6,134},{7,135},{8... | collective-permute-start | bytes 393224 | tf_op jit(solution)/shard_map/ppermute | solution.py:30
  139.6 6.2 %collective-permute-done.26.refs_1_ = bf16[128,512]{1,0:T(8,128)(2,1)S(1)} collective-permute-done((bf16[128,512]{1,0:T(8,128)(2,1)S(1)}, bf16[128,512]{1,0:T(8,128)(2,1)S(1)}, u32[]{:S(2)}, u32[]{:S(2)}) %collective-permute-start.26) | collective-permute-done | bytes 131104 | tf_op jit(solution)/shard_map/ppermute | solution.py:30
  147.0 3.3 %join.1 = (bf16[128,8192]{1,0:T(8,128)(2,1)}, f32[8,128]{1,0:T(8,128)}) custom-call(bf16[128,2048]{1,0:T(8,128)(2,1)} %get-tuple-element.41.p0, bf16[128,2048]{1,0:T(8,128)(2,1)} %copy-done.5, bf16[128,2048]{1,0:T(8,128)(2,1)} %copy-done.6, bf16[128,2048]{1,0:T(8,128)(2,1)} %copy-done.7), custom_call_target="tpu_custom_call" | custom-call | bytes 4198400 | tf_op jit(solution)/shard_map/join/pallas_call | solution.py:55
  (116 shorter events, 19.4 us)
Async XLA Ops:
  0.6 27.6 %collective-permute-start = (bf16[256,512]{1,0:T(8,128)(2,1)}, bf16[256,512]{1,0:T(8,128)(2,1)S(1)}, u32[]{:S(2)}, u32[]{:S(2)}) collective-permute-start(bf16[256,512]{1,0:T(8,128)(2,1)} %a.1), channel_id=1, source_target_pairs={{0,208},{1,209},{2,210},{3,211},{4,212},{5,213},{6,214},{7,215},{8... | collective-permute-start | bytes 786440 | tf_op jit(solution)/shard_map/ppermute | solution.py:30
  8.5 20.4 %all-to-all-start = ((s32[32,8,128]{2,1,0:T(8,128)}), s32[32,8,128]{2,1,0:T(8,128)S(1)}, u32[]{:S(2)}, u32[]{:S(2)}) async-start(s32[32,8,128]{2,1,0:T(8,128)} %masks.1.after), calls=%async_computation | async-start | bytes 262144 | tf_op jit(solution)/shard_map/all_to_all | solution.py:421
  20.2 25.6 %collective-permute-start.1 = (bf16[128,2048]{1,0:T(8,128)(2,1)}, bf16[128,2048]{1,0:T(8,128)(2,1)S(1)}, u32[]{:S(2)}, u32[]{:S(2)}) collective-permute-start(bf16[128,2048]{1,0:T(8,128)(2,1)} %get-tuple-element.34), channel_id=1, source_target_pairs={{0,1},{1,2},{2,3},{3,0},{4,5},{5,6},{6,7},{7,4},{8,9},{9,10},{10,1... | collective-permute-start | bytes 1572872 | tf_op jit(solution)/shard_map/ppermute | solution.py:30
  21.5 25.5 %collective-permute-start.2 = (bf16[128,2048]{1,0:T(8,128)(2,1)}, bf16[128,2048]{1,0:T(8,128)(2,1)S(1)}, u32[]{:S(2)}, u32[]{:S(2)}) collective-permute-start(bf16[128,2048]{1,0:T(8,128)(2,1)} %get-tuple-element.35), channel_id=1, source_target_pairs={{0,2},{1,3},{2,0},{3,1},{4,6},{5,7},{6,4},{7,5},{8,10},{9,11},{10,... | collective-permute-start | bytes 1572872 | tf_op jit(solution)/shard_map/ppermute | solution.py:30
  23.9 23.5 %collective-permute-start.3 = (bf16[128,2048]{1,0:T(8,128)(2,1)}, bf16[128,2048]{1,0:T(8,128)(2,1)S(1)}, u32[]{:S(2)}, u32[]{:S(2)}) collective-permute-start(bf16[128,2048]{1,0:T(8,128)(2,1)} %get-tuple-element.36), channel_id=1, source_target_pairs={{0,3},{1,0},{2,1},{3,2},{4,7},{5,4},{6,5},{7,6},{8,11},{9,8},{10,9... | collective-permute-start | bytes 1572872 | tf_op jit(solution)/shard_map/ppermute | solution.py:30
  29.0 32.5 %copy-start.8 = (bf16[128,2048]{1,0:T(8,128)(2,1)S(1)}, bf16[128,2048]{1,0:T(8,128)(2,1)}, u32[]{:S(2)}) copy-start(bf16[128,2048]{1,0:T(8,128)(2,1)} %get-tuple-element.37.refs_0_) | copy-start | bytes 1572868
  32.9 21.3 %all-to-all-start.1 = ((bf16[32,8,512]{2,1,0:T(8,128)(2,1)}), bf16[32,8,512]{2,1,0:T(8,128)(2,1)S(1)}, u32[]{:S(2)}, u32[]{:S(2)}) async-start(bf16[32,8,512]{2,1,0:T(8,128)(2,1)} %bitcast.9), calls=%async_computation.1 | async-start | bytes 524288 | tf_op jit(solution)/shard_map/all_to_all | solution.py:421
  42.1 14.6 %collective-permute-start.7 = (bf16[256,512]{1,0:T(8,128)(2,1)S(1)}, bf16[256,512]{1,0:T(8,128)(2,1)S(1)}, u32[]{:S(2)}, u32[]{:S(2)}) collective-permute-start(bf16[256,512]{1,0:T(8,128)(2,1)S(1)} %copy-done.1), channel_id=1, source_target_pairs={{0,4},{1,5},{2,6},{3,7},{4,8},{5,9},{6,10},{7,11},{8,12},{9,13},{1... | collective-permute-start | bytes 786440 | tf_op jit(solution)/shard_map/ppermute | solution.py:30
  43.5 14.3 %collective-permute-start.8 = (bf16[256,512]{1,0:T(8,128)(2,1)S(1)}, bf16[256,512]{1,0:T(8,128)(2,1)S(1)}, u32[]{:S(2)}, u32[]{:S(2)}) collective-permute-start(bf16[256,512]{1,0:T(8,128)(2,1)S(1)} %copy-done.1), channel_id=1, source_target_pairs={{0,8},{1,9},{2,10},{3,11},{4,12},{5,13},{6,14},{7,15},{8,0},{9,1},... | collective-permute-start | bytes 786440 | tf_op jit(solution)/shard_map/ppermute | solution.py:30
  45.9 12.6 %collective-permute-start.9 = (bf16[256,512]{1,0:T(8,128)(2,1)S(1)}, bf16[256,512]{1,0:T(8,128)(2,1)S(1)}, u32[]{:S(2)}, u32[]{:S(2)}) collective-permute-start(bf16[256,512]{1,0:T(8,128)(2,1)S(1)} %copy-done.1), channel_id=1, source_target_pairs={{0,12},{1,13},{2,14},{3,15},{4,0},{5,1},{6,2},{7,3},{8,4},{9,5},{1... | collective-permute-start | bytes 786440 | tf_op jit(solution)/shard_map/ppermute | solution.py:30
  54.4 6.5 %collective-permute-start.4 = (bf16[128,512]{1,0:T(8,128)(2,1)S(1)}, bf16[128,512]{1,0:T(8,128)(2,1)S(1)}, u32[]{:S(2)}, u32[]{:S(2)}) collective-permute-start(bf16[128,512]{1,0:T(8,128)(2,1)S(1)} %pick.1.refs_4_.refs_0_), channel_id=1, source_target_pairs={{0,1},{1,2},{2,3},{3,0},{4,5},{5,6},{6,7},{7,4},{8,9},{9,10},{10,1... | collective-permute-start | bytes 393224 | tf_op jit(solution)/shard_map/ppermute | solution.py:30
  54.5 6.4 %collective-permute-start.5 = (bf16[128,512]{1,0:T(8,128)(2,1)S(1)}, bf16[128,512]{1,0:T(8,128)(2,1)S(1)}, u32[]{:S(2)}, u32[]{:S(2)}) collective-permute-start(bf16[128,512]{1,0:T(8,128)(2,1)S(1)} %pick.1.refs_4_.refs_0_), channel_id=1, source_target_pairs={{0,2},{1,3},{2,0},{3,1},{4,6},{5,7},{6,4},{7,5},{8,10},{9,11},{10,... | collective-permute-start | bytes 393224 | tf_op jit(solution)/shard_map/ppermute | solution.py:30
  56.7 4.8 %collective-permute-start.6 = (bf16[128,512]{1,0:T(8,128)(2,1)S(1)}, bf16[128,512]{1,0:T(8,128)(2,1)S(1)}, u32[]{:S(2)}, u32[]{:S(2)}) collective-permute-start(bf16[128,512]{1,0:T(8,128)(2,1)S(1)} %pick.1.refs_4_.refs_0_), channel_id=1, source_target_pairs={{0,3},{1,0},{2,1},{3,2},{4,7},{5,4},{6,5},{7,6},{8,11},{9,8},{10,9... | collective-permute-start | bytes 393224 | tf_op jit(solution)/shard_map/ppermute | solution.py:30
  63.7 7.5 %collective-permute-start.14 = (bf16[8,128,512]{2,1,0:T(8,128)(2,1)S(1)}, bf16[8,128,512]{2,1,0:T(8,128)(2,1)S(1)}, u32[]{:S(2)}, u32[]{:S(2)}) collective-permute-start(bf16[8,128,512]{2,1,0:T(8,128)(2,1)S(1)} %get-tuple-element.39), channel_id=1, source_target_pairs={{0,32},{1,33},{2,34},{3,35},{4,36},{5,37},{6,38},{7,39},{8,40},{9,... | collective-permute-start | bytes 3145736 | tf_op jit(solution)/shard_map/ppermute | solution.py:30
  69.0 5.0 %collective-permute-start.10 = (bf16[256,512]{1,0:T(8,128)(2,1)S(1)}, bf16[256,512]{1,0:T(8,128)(2,1)S(1)}, u32[]{:S(2)}, u32[]{:S(2)}) collective-permute-start(bf16[256,512]{1,0:T(8,128)(2,1)S(1)} %copy-done.1), channel_id=1, source_target_pairs={{0,32},{1,33},{2,34},{3,35},{4,36},{5,37},{6,38},{7,39},{8,40},{9,... | collective-permute-start | bytes 786440 | tf_op jit(solution)/shard_map/ppermute | solution.py:30
  69.1 5.4 %collective-permute-start.11 = (bf16[256,512]{1,0:T(8,128)(2,1)S(1)}, bf16[256,512]{1,0:T(8,128)(2,1)S(1)}, u32[]{:S(2)}, u32[]{:S(2)}) collective-permute-start(bf16[256,512]{1,0:T(8,128)(2,1)S(1)} %collective-permute-done.7.refs_8_.refs_5_), channel_id=1, source_target_pairs={{0,32},{1,33},{2,34},{3,35},{4,36},{5,37},{6,38},{7,39},{8,40},{9,... | collective-permute-start | bytes 786440 | tf_op jit(solution)/shard_map/ppermute | solution.py:30
  69.5 5.2 %collective-permute-start.12 = (bf16[256,512]{1,0:T(8,128)(2,1)S(1)}, bf16[256,512]{1,0:T(8,128)(2,1)S(1)}, u32[]{:S(2)}, u32[]{:S(2)}) collective-permute-start(bf16[256,512]{1,0:T(8,128)(2,1)S(1)} %collective-permute-done.8.refs_9_.refs_6_), channel_id=1, source_target_pairs={{0,32},{1,33},{2,34},{3,35},{4,36},{5,37},{6,38},{7,39},{8,40},{9,... | collective-permute-start | bytes 786440 | tf_op jit(solution)/shard_map/ppermute | solution.py:30
  69.6 5.1 %collective-permute-start.13 = (bf16[256,512]{1,0:T(8,128)(2,1)S(1)}, bf16[256,512]{1,0:T(8,128)(2,1)S(1)}, u32[]{:S(2)}, u32[]{:S(2)}) collective-permute-start(bf16[256,512]{1,0:T(8,128)(2,1)S(1)} %collective-permute-done.9.refs_10_.refs_7_), channel_id=1, source_target_pairs={{0,32},{1,33},{2,34},{3,35},{4,36},{5,37},{6,38},{7,39},{8,40},{9,... | collective-permute-start | bytes 786440 | tf_op jit(solution)/shard_map/ppermute | solution.py:30
  72.4 14.1 %collective-permute-start.21 = (bf16[2,128,512]{2,1,0:T(8,128)(2,1)S(1)}, bf16[2,128,512]{2,1,0:T(8,128)(2,1)S(1)}, u32[]{:S(2)}, u32[]{:S(2)}) collective-permute-start(bf16[2,128,512]{2,1,0:T(8,128)(2,1)S(1)} %get-tuple-element.52), channel_id=1, source_target_pairs={{0,12},{1,13},{2,14},{3,15},{4,0},{5,1},{6,2},{7,3},{8,4},{9,5},{1... | collective-permute-start | bytes 786440 | tf_op jit(solution)/shard_map/ppermute | solution.py:30
  74.0 13.2 %collective-permute-start.22 = (bf16[2,128,512]{2,1,0:T(8,128)(2,1)S(1)}, bf16[2,128,512]{2,1,0:T(8,128)(2,1)S(1)}, u32[]{:S(2)}, u32[]{:S(2)}) collective-permute-start(bf16[2,128,512]{2,1,0:T(8,128)(2,1)S(1)} %get-tuple-element.53), channel_id=1, source_target_pairs={{0,8},{1,9},{2,10},{3,11},{4,12},{5,13},{6,14},{7,15},{8,0},{9,1},... | collective-permute-start | bytes 786440 | tf_op jit(solution)/shard_map/ppermute | solution.py:30
  74.5 14.9 %collective-permute-start.23 = (bf16[2,128,512]{2,1,0:T(8,128)(2,1)S(1)}, bf16[2,128,512]{2,1,0:T(8,128)(2,1)S(1)}, u32[]{:S(2)}, u32[]{:S(2)}) collective-permute-start(bf16[2,128,512]{2,1,0:T(8,128)(2,1)S(1)} %get-tuple-element.54), channel_id=1, source_target_pairs={{0,4},{1,5},{2,6},{3,7},{4,8},{5,9},{6,10},{7,11},{8,12},{9,13},{1... | collective-permute-start | bytes 786440 | tf_op jit(solution)/shard_map/ppermute | solution.py:30
  79.8 10.9 %collective-permute-start.18 = (bf16[128,512]{1,0:T(8,128)(2,1)}, bf16[128,512]{1,0:T(8,128)(2,1)S(1)}, u32[]{:S(2)}, u32[]{:S(2)}) collective-permute-start(bf16[128,512]{1,0:T(8,128)(2,1)} %get-tuple-element.49), channel_id=1, source_target_pairs={{0,3},{1,0},{2,1},{3,2},{4,7},{5,4},{6,5},{7,6},{8,11},{9,8},{10,9... | collective-permute-start | bytes 393224 | tf_op jit(solution)/shard_map/ppermute | solution.py:30
  82.1 8.6 %collective-permute-start.19 = (bf16[128,512]{1,0:T(8,128)(2,1)}, bf16[128,512]{1,0:T(8,128)(2,1)S(1)}, u32[]{:S(2)}, u32[]{:S(2)}) collective-permute-start(bf16[128,512]{1,0:T(8,128)(2,1)} %get-tuple-element.50), channel_id=1, source_target_pairs={{0,2},{1,3},{2,0},{3,1},{4,6},{5,7},{6,4},{7,5},{8,10},{9,11},{10,... | collective-permute-start | bytes 393224 | tf_op jit(solution)/shard_map/ppermute | solution.py:30
  86.5 5.1 %collective-permute-start.20 = (bf16[128,512]{1,0:T(8,128)(2,1)S(1)}, bf16[128,512]{1,0:T(8,128)(2,1)S(1)}, u32[]{:S(2)}, u32[]{:S(2)}) collective-permute-start(bf16[128,512]{1,0:T(8,128)(2,1)S(1)} %copy-done.33), channel_id=1, source_target_pairs={{0,1},{1,2},{2,3},{3,0},{4,5},{5,6},{6,7},{7,4},{8,9},{9,10},{10,1... | collective-permute-start | bytes 393224 | tf_op jit(solution)/shard_map/ppermute | solution.py:30
  90.2 5.9 %collective-permute-start.24 = (bf16[128,512]{1,0:T(8,128)(2,1)S(1)}, bf16[128,512]{1,0:T(8,128)(2,1)S(1)}, u32[]{:S(2)}, u32[]{:S(2)}) collective-permute-start(bf16[128,512]{1,0:T(8,128)(2,1)S(1)} %get-tuple-element.57), channel_id=1, source_target_pairs={{0,208},{1,209},{2,210},{3,211},{4,212},{5,213},{6,214},{7,215},{8... | collective-permute-start | bytes 393224 | tf_op jit(solution)/shard_map/ppermute | solution.py:30
  97.1 19.2 %all-to-all-start.2 = ((bf16[32,8,512]{2,1,0:T(8,128)(2,1)}), bf16[32,8,512]{2,1,0:T(8,128)(2,1)S(1)}, u32[]{:S(2)}, u32[]{:S(2)}) async-start(bf16[32,8,512]{2,1,0:T(8,128)(2,1)} %bitcast.3), calls=%async_computation.2 | async-start | bytes 524288 | tf_op jit(solution)/shard_map/all_to_all | solution.py:421
  104.2 19.1 %collective-permute-start.15 = (bf16[128,2048]{1,0:T(8,128)(2,1)}, bf16[128,2048]{1,0:T(8,128)(2,1)S(1)}, u32[]{:S(2)}, u32[]{:S(2)}) collective-permute-start(bf16[128,2048]{1,0:T(8,128)(2,1)} %get-tuple-element.42), channel_id=1, source_target_pairs={{0,3},{1,0},{2,1},{3,2},{4,7},{5,4},{6,5},{7,6},{8,11},{9,8},{10,9... | collective-permute-start | bytes 1572872 | tf_op jit(solution)/shard_map/ppermute | solution.py:30
  106.7 16.6 %collective-permute-start.16 = (bf16[128,2048]{1,0:T(8,128)(2,1)S(1)}, bf16[128,2048]{1,0:T(8,128)(2,1)S(1)}, u32[]{:S(2)}, u32[]{:S(2)}) collective-permute-start(bf16[128,2048]{1,0:T(8,128)(2,1)S(1)} %copy-done.32), channel_id=1, source_target_pairs={{0,2},{1,3},{2,0},{3,1},{4,6},{5,7},{6,4},{7,5},{8,10},{9,11},{10,... | collective-permute-start | bytes 1572872 | tf_op jit(solution)/shard_map/ppermute | solution.py:30
  107.3 28.1 %collective-permute-start.17 = (bf16[128,2048]{1,0:T(8,128)(2,1)S(1)}, bf16[128,2048]{1,0:T(8,128)(2,1)S(1)}, u32[]{:S(2)}, u32[]{:S(2)}) collective-permute-start(bf16[128,2048]{1,0:T(8,128)(2,1)S(1)} %copy-done.31), channel_id=1, source_target_pairs={{0,1},{1,2},{2,3},{3,0},{4,5},{5,6},{6,7},{7,4},{8,9},{9,10},{10,1... | collective-permute-start | bytes 1572872 | tf_op jit(solution)/shard_map/ppermute | solution.py:30
  107.9 15.5 %collective-permute-start.25 = (bf16[128,512]{1,0:T(8,128)(2,1)S(1)}, bf16[128,512]{1,0:T(8,128)(2,1)S(1)}, u32[]{:S(2)}, u32[]{:S(2)}) collective-permute-start(bf16[128,512]{1,0:T(8,128)(2,1)S(1)} %mirror_sum.1.after.refs_0_), channel_id=1, source_target_pairs={{0,64},{1,65},{2,66},{3,67},{4,68},{5,69},{6,70},{7,71},{8,72},{9,... | collective-permute-start | bytes 393224 | tf_op jit(solution)/shard_map/ppermute | solution.py:30
  136.1 9.7 %collective-permute-start.26 = (bf16[128,512]{1,0:T(8,128)(2,1)S(1)}, bf16[128,512]{1,0:T(8,128)(2,1)S(1)}, u32[]{:S(2)}, u32[]{:S(2)}) collective-permute-start(bf16[128,512]{1,0:T(8,128)(2,1)S(1)} %z_sum.2.refs_0_), channel_id=1, source_target_pairs={{0,128},{1,129},{2,130},{3,131},{4,132},{5,133},{6,134},{7,135},{8... | collective-permute-start | bytes 393224 | tf_op jit(solution)/shard_map/ppermute | solution.py:30
  145.9 4.5 %collective-permute-start.27 = (bf16[128,512]{1,0:T(8,128)(2,1)S(1)}, bf16[128,512]{1,0:T(8,128)(2,1)S(1)}, u32[]{:S(2)}, u32[]{:S(2)}) collective-permute-start(bf16[128,512]{1,0:T(8,128)(2,1)S(1)} %z_sum.3.mine), channel_id=1, source_target_pairs={{0,32},{1,33},{2,34},{3,35},{4,36},{5,37},{6,38},{7,39},{8,40},{9,... | collective-permute-start | bytes 393224 | tf_op jit(solution)/shard_map/ppermute | solution.py:30
  (33 other events, 328.9 us)

commit v2 on v1

--- a/solution.py
+++ b/solution.py
@@ -458,9 +458,9 @@
     grad_q, grad_k, scored = attention_dscore(probs, values, upstream, queries, keys)
     grad_inputs, joined = join(columns)
 
-    after = [VMEM] * 2 + [ANY] * NY
-    total = call(pair_sum_kernel, "z_sum", small, total, permute(total, flip_zl(1)), scored, *columns[1:], ins=after)[0]
-    total = call(pair_sum_kernel, "z_sum", small, total, permute(total, flip_zl(2)))[0]
+    after = [VMEM] * 2 + [ANY] * (NY - 1)
+    total = call(pair_sum_kernel, "z_sum", small, total, permute(total, flip_zl(1)), *columns[1:], ins=after)[0]
+    total = call(pair_sum_kernel, "z_sum", small, total, permute(total, flip_zl(2)), scored, ins=order)[0]
     out = [like((NCO * half, width), BF16)]
     grad_weight = call(halves_kernel, "halves", out, total, permute(total, other_core), joined, ins=order)[0]
     return grad_inputs, grad_q, grad_k, grad_weight

time: 152 us -> 139 us (0.914)
  waiting for transfers between devices: 43.4 us -> 30.4 us
    ppermute x28, waiting for transfers between devices: 31.1 us -> 23.6 us  [permute(): return lax.ppermute(array, AXES, pairs)]
    all_to_all x3, waiting for transfers between devices: 12.2 us -> 6.78 us  [exchange(): lax.all_to_all(buffer, 'fsdp', split_axis=0, concat_axis=0, tiled=True)]
    unnamed x68 -> x64, local copies, waits for them, and re-layouts: 5.75 us -> 5.76 us
  transfers between devices with their start and end apart: 31 -> 31, of which waited for: 12 -> 10; matrix products, arithmetic and copies ran while one was open for 0% -> 0% of each run, Pallas kernels for 20% -> 23%
where the time goes in v2:
time: 139 us; the launch traced here: 138 us
  starting transfers between devices  66.8 us (48%)
  Pallas kernels  34.1 us (25%)
  waiting for transfers between devices  30.4 us (22%)
  local copies, waits for them, and re-layouts  5.76 us (4%)
    ppermute x28, starting transfers between devices, permute(): return lax.ppermute(array, AXES, pairs)  42.3 us
    pallas_call x17, Pallas kernels, call(): pl.pallas_call(kernel, out_shape=out, in_specs=[VMEM] * len(args) if ins...  27.7 us
    all_to_all x3, starting transfers between devices, exchange(): lax.all_to_all(buffer, 'fsdp', split_axis=0, concat_axis=0, tiled=True)  24.5 us
    ppermute x28, waiting for transfers between devices, permute(): return lax.ppermute(array, AXES, pairs)  23.6 us
    all_to_all x3, waiting for transfers between devices, exchange(): lax.all_to_all(buffer, 'fsdp', split_axis=0, concat_axis=0, tiled=True)  6.78 us
    pallas_call x1, Pallas kernels, per_head(): pl.pallas_call(kernel, grid=(KVH,), out_shape=[o for o, _ in outs], in_sp...  6.41 us
    unnamed x64, local copies, waits for them, and re-layouts  5.76 us
  transfers between devices with their start and end apart: 31, of which 10 were waited for; matrix products, arithmetic and copies ran while one was open for 0% of the time, Pallas kernels for 23%

profile of v2, /device:TPU:1, one launch (start us, length us, event | category | flops | bytes accessed | tf_op | source)
XLA Modules:
  0.0 138.1 jit_solution(14871110916021502091)
XLA Ops:
  0.6 6.5 %collective-permute-start = (bf16[256,512]{1,0:T(8,128)(2,1)}, bf16[256,512]{1,0:T(8,128)(2,1)S(1)}, u32[]{:S(2)}, u32[]{:S(2)}) collective-permute-start(bf16[256,512]{1,0:T(8,128)(2,1)} %a.1), channel_id=1, source_target_pairs={{0,208},{1,209},{2,210},{3,211},{4,212},{5,213},{6,214},{7,215},{8... | collective-permute-start | bytes 786440 | tf_op jit(solution)/shard_map/ppermute | solution.py:30
  7.1 1.4 %masks.1.after = s32[32,8,128]{2,1,0:T(8,128)} custom-call(s32[128]{0:T(128)} %slots_in.1, s32[128]{0:T(128)} %ids_in.1), custom_call_target="tpu_custom_call" | custom-call | bytes 132096 | tf_op jit(solution)/shard_map/masks/pallas_call | solution.py:55
  8.5 8.1 %all-to-all-start = ((s32[32,8,128]{2,1,0:T(8,128)}), s32[32,8,128]{2,1,0:T(8,128)S(1)}, u32[]{:S(2)}, u32[]{:S(2)}) async-start(s32[32,8,128]{2,1,0:T(8,128)} %masks.1.after), calls=%async_computation | async-start | bytes 262144 | tf_op jit(solution)/shard_map/all_to_all | solution.py:421
  16.7 3.5 %split.1 = (bf16[128,2048]{1,0:T(8,128)(2,1)}, bf16[128,2048]{1,0:T(8,128)(2,1)}, bf16[128,2048]{1,0:T(8,128)(2,1)}, bf16[128,2048]{1,0:T(8,128)(2,1)}) custom-call(bf16[128,8192]{1,0:T(8,128)(2,1)} %full_in.1, s32[32,8,128]{2,1,0:T(8,128)} %masks.1.after), custom_call_target="tpu_custom_call" | custom-call | bytes 4325376 | tf_op jit(solution)/shard_map/split/pallas_call | solution.py:55
  20.2 1.3 collective-permute-start.1
  21.5 2.4 %collective-permute-start.2 = (bf16[128,2048]{1,0:T(8,128)(2,1)}, bf16[128,2048]{1,0:T(8,128)(2,1)S(1)}, u32[]{:S(2)}, u32[]{:S(2)}) collective-permute-start(bf16[128,2048]{1,0:T(8,128)(2,1)} %get-tuple-element.35), channel_id=1, source_target_pairs={{0,2},{1,3},{2,0},{3,1},{4,6},{5,7},{6,4},{7,5},{8,10},{9,11},{10,... | collective-permute-start | bytes 1572872 | tf_op jit(solution)/shard_map/ppermute | solution.py:30
  25.1 3.1 %scores.1.scores_in = f32[4,2,8,1024]{3,2,1,0:T(8,128)} custom-call(bf16[256,4096]{1,0:T(8,128)(2,1)} %queries.3, bf16[256,512]{1,0:T(8,128)(2,1)} %keys.1), custom_call_target="tpu_custom_call" | custom-call | flops 268435456 | bytes 2621440 | tf_op jit(solution)/shard_map/scores/pallas_call | solution.py:55
  29.6 3.2 %probs.1 = (bf16[256,512]{1,0:T(8,128)(2,1)}, f32[4,2,8,1024]{3,2,1,0:T(8,128)}) custom-call(f32[4,2,8,1024]{3,2,1,0:T(8,128)} %scores.1.scores_in, s32[32,8,128]{2,1,0:T(8,128)} %copy-done.26, bf16[256,4096]{1,0:T(8,128)(2,1)} %upstream.3, bf16[256,512]{1,0:T(8,128)(2,1)} %copy-done), custom_call_target="tpu_custom_call" | custom-call | flops 268435456 | bytes 3276800 | tf_op jit(solution)/shard_map/probs/pallas_call | solution.py:55
  32.9 9.2 %all-to-all-start.1 = ((bf16[32,8,512]{2,1,0:T(8,128)(2,1)}), bf16[32,8,512]{2,1,0:T(8,128)(2,1)S(1)}, u32[]{:S(2)}, u32[]{:S(2)}) async-start(bf16[32,8,512]{2,1,0:T(8,128)(2,1)} %bitcast.9), calls=%async_computation.1 | async-start | bytes 524288 | tf_op jit(solution)/shard_map/all_to_all | solution.py:421
  42.1 1.3 collective-permute-start.7
  43.4 2.4 %collective-permute-start.8 = (bf16[256,512]{1,0:T(8,128)(2,1)S(1)}, bf16[256,512]{1,0:T(8,128)(2,1)S(1)}, u32[]{:S(2)}, u32[]{:S(2)}) collective-permute-start(bf16[256,512]{1,0:T(8,128)(2,1)S(1)} %copy-done.1), channel_id=1, source_target_pairs={{0,8},{1,9},{2,10},{3,11},{4,12},{5,13},{6,14},{7,15},{8,0},{9,1},... | collective-permute-start | bytes 786440 | tf_op jit(solution)/shard_map/ppermute | solution.py:30
  47.4 6.8 %all-to-all-done.1 = bf16[32,8,512]{2,1,0:T(8,128)(2,1)S(1)} async-done(((bf16[32,8,512]{2,1,0:T(8,128)(2,1)}), bf16[32,8,512]{2,1,0:T(8,128)(2,1)S(1)}, u32[]{:S(2)}, u32[]{:S(2)}) %all-to-all-start.1) | async-done | bytes 262176 | tf_op jit(solution)/shard_map/all_to_all | solution.py:421
  54.5 2.2 %collective-permute-start.5 = (bf16[128,512]{1,0:T(8,128)(2,1)S(1)}, bf16[128,512]{1,0:T(8,128)(2,1)S(1)}, u32[]{:S(2)}, u32[]{:S(2)}) collective-permute-start(bf16[128,512]{1,0:T(8,128)(2,1)S(1)} %pick.1.refs_4_.refs_0_), channel_id=1, source_target_pairs={{0,2},{1,3},{2,0},{3,1},{4,6},{5,7},{6,4},{7,5},{8,10},{9,11},{10,... | collective-permute-start | bytes 393224 | tf_op jit(solution)/shard_map/ppermute | solution.py:30
  58.4 2.5 %collective-permute-done.4.refs_5_.refs_1_ = bf16[128,512]{1,0:T(8,128)(2,1)S(1)} collective-permute-done((bf16[128,512]{1,0:T(8,128)(2,1)S(1)}, bf16[128,512]{1,0:T(8,128)(2,1)S(1)}, u32[]{:S(2)}, u32[]{:S(2)}) %collective-permute-start.4) | collective-permute-done | bytes 131104 | tf_op jit(solution)/shard_map/ppermute | solution.py:30
  61.5 2.2 %shares.1 = (f32[8,128,512]{2,1,0:T(8,128)S(1)}, bf16[8,128,512]{2,1,0:T(8,128)(2,1)S(1)}, f32[8,128]{1,0:T(8,128)S(1)}) custom-call(bf16[128,2048]{1,0:T(8,128)(2,1)S(1)} %copy-done.8, bf16[128,2048]{1,0:T(8,128)(2,1)S(1)} %collective-permute-done.1.refs_2_.refs_1_, bf16[128,2048]{1,0:T(8,128)(2,1)S(1)} %collective-permute-done.2.refs_3_.refs_2_, ...), custom_call_target="tpu_custom_call" | custom-call | flops 1073741824 | bytes 6557696 | tf_op jit(solution)/shard_map/shares/pallas_call | solution.py:55
  63.7 5.3 %collective-permute-start.14 = (bf16[8,128,512]{2,1,0:T(8,128)(2,1)S(1)}, bf16[8,128,512]{2,1,0:T(8,128)(2,1)S(1)}, u32[]{:S(2)}, u32[]{:S(2)}) collective-permute-start(bf16[8,128,512]{2,1,0:T(8,128)(2,1)S(1)} %get-tuple-element.39), channel_id=1, source_target_pairs={{0,32},{1,33},{2,34},{3,35},{4,36},{5,37},{6,38},{7,39},{8,40},{9,... | collective-permute-start | bytes 3145736 | tf_op jit(solution)/shard_map/ppermute | solution.py:30
  70.0 1.3 collective-permute-done.14.got
  72.3 1.6 %collective-permute-start.21 = (bf16[2,128,512]{2,1,0:T(8,128)(2,1)S(1)}, bf16[2,128,512]{2,1,0:T(8,128)(2,1)S(1)}, u32[]{:S(2)}, u32[]{:S(2)}) collective-permute-start(bf16[2,128,512]{2,1,0:T(8,128)(2,1)S(1)} %get-tuple-element.52), channel_id=1, source_target_pairs={{0,12},{1,13},{2,14},{3,15},{4,0},{5,1},{6,2},{7,3},{8,4},{9,5},{1... | collective-permute-start | bytes 786440 | tf_op jit(solution)/shard_map/ppermute | solution.py:30
  75.4 4.3 %partial_values.1 = (f32[128,512]{1,0:T(8,128)}, bf16[128,512]{1,0:T(8,128)(2,1)}, bf16[128,512]{1,0:T(8,128)(2,1)}, bf16[128,512]{1,0:T(8,128)(2,1)}) custom-call(bf16[128,2048]{1,0:T(8,128)(2,1)} %get-tuple-element.37.refs_0_, bf16[128,2048]{1,0:T(8,128)(2,1)} %copy-done.2, bf16[128,2048]{1,0:T(8,128)(2,1)} %copy-done.3, bf16[128,2048]{1,0:T(8,128)(2,1)} %copy-done.4, ...), custom_call_target="tpu_custom_call" | custom-call | flops 1073741824 | bytes 4853760 | tf_op jit(solution)/shard_map/partial_values/pallas_call | solution.py:55
  79.7 2.3 %collective-permute-start.18 = (bf16[128,512]{1,0:T(8,128)(2,1)}, bf16[128,512]{1,0:T(8,128)(2,1)S(1)}, u32[]{:S(2)}, u32[]{:S(2)}) collective-permute-start(bf16[128,512]{1,0:T(8,128)(2,1)} %get-tuple-element.49), channel_id=1, source_target_pairs={{0,3},{1,0},{2,1},{3,2},{4,7},{5,4},{6,5},{7,6},{8,11},{9,8},{10,9... | collective-permute-start | bytes 393224 | tf_op jit(solution)/shard_map/ppermute | solution.py:30
  82.1 4.4 %back.1 = (bf16[128,2048]{1,0:T(8,128)(2,1)}, bf16[128,2048]{1,0:T(8,128)(2,1)}, bf16[128,2048]{1,0:T(8,128)(2,1)}, bf16[128,2048]{1,0:T(8,128)(2,1)}, f32[8,128]{1,0:T(8,128)}) custom-call(bf16[128,512]{1,0:T(8,128)(2,1)} %copy-done.16, bf16[128,512]{1,0:T(8,128)(2,1)} %copy-done.22, bf16[128,512]{1,0:T(8,128)(2,1)} %copy-done.23, ...), custom_call_target="tpu_custom_call" | custom-call | flops 1073741824 | bytes 5246976 | tf_op jit(solution)/shard_map/back/pallas_call | solution.py:55
  87.2 2.1 %collective-permute-done.23.c = bf16[2,128,512]{2,1,0:T(8,128)(2,1)S(1)} collective-permute-done((bf16[2,128,512]{2,1,0:T(8,128)(2,1)S(1)}, bf16[2,128,512]{2,1,0:T(8,128)(2,1)S(1)}, u32[]{:S(2)}, u32[]{:S(2)}) %collective-permute-start.23) | collective-permute-done | bytes 262176 | tf_op jit(solution)/shard_map/ppermute | solution.py:30
  90.6 2.0 %collective-permute-start.15 = (bf16[128,2048]{1,0:T(8,128)(2,1)}, bf16[128,2048]{1,0:T(8,128)(2,1)S(1)}, u32[]{:S(2)}, u32[]{:S(2)}) collective-permute-start(bf16[128,2048]{1,0:T(8,128)(2,1)} %get-tuple-element.42), channel_id=1, source_target_pairs={{0,3},{1,0},{2,1},{3,2},{4,7},{5,4},{6,5},{7,6},{8,11},{9,8},{10,9... | collective-permute-start | bytes 1572872 | tf_op jit(solution)/shard_map/ppermute | solution.py:30
  92.6 1.8 %collective-permute-start.16 = (bf16[128,2048]{1,0:T(8,128)(2,1)}, bf16[128,2048]{1,0:T(8,128)(2,1)S(1)}, u32[]{:S(2)}, u32[]{:S(2)}) collective-permute-start(bf16[128,2048]{1,0:T(8,128)(2,1)} %get-tuple-element.43), channel_id=1, source_target_pairs={{0,2},{1,3},{2,0},{3,1},{4,6},{5,7},{6,4},{7,5},{8,10},{9,11},{10,... | collective-permute-start | bytes 1572872 | tf_op jit(solution)/shard_map/ppermute | solution.py:30
  94.4 1.6 %collective-permute-done.24.refs_1_ = bf16[128,512]{1,0:T(8,128)(2,1)S(1)} collective-permute-done((bf16[128,512]{1,0:T(8,128)(2,1)S(1)}, bf16[128,512]{1,0:T(8,128)(2,1)S(1)}, u32[]{:S(2)}, u32[]{:S(2)}) %collective-permute-start.24) | collective-permute-done | bytes 131104 | tf_op jit(solution)/shard_map/ppermute | solution.py:30
  97.0 7.1 %all-to-all-start.2 = ((bf16[32,8,512]{2,1,0:T(8,128)(2,1)}), bf16[32,8,512]{2,1,0:T(8,128)(2,1)S(1)}, u32[]{:S(2)}, u32[]{:S(2)}) async-start(bf16[32,8,512]{2,1,0:T(8,128)(2,1)} %bitcast.3), calls=%async_computation.2 | async-start | bytes 524288 | tf_op jit(solution)/shard_map/all_to_all | solution.py:421
  104.1 3.2 %collective-permute-start.25 = (bf16[128,512]{1,0:T(8,128)(2,1)S(1)}, bf16[128,512]{1,0:T(8,128)(2,1)S(1)}, u32[]{:S(2)}, u32[]{:S(2)}) collective-permute-start(bf16[128,512]{1,0:T(8,128)(2,1)S(1)} %mirror_sum.1.after.refs_0_), channel_id=1, source_target_pairs={{0,64},{1,65},{2,66},{3,67},{4,68},{5,69},{6,70},{7,71},{8,72},{9,... | collective-permute-start | bytes 393224 | tf_op jit(solution)/shard_map/ppermute | solution.py:30
  107.3 3.8 %collective-permute-done.25.refs_1_ = bf16[128,512]{1,0:T(8,128)(2,1)S(1)} collective-permute-done((bf16[128,512]{1,0:T(8,128)(2,1)S(1)}, bf16[128,512]{1,0:T(8,128)(2,1)S(1)}, u32[]{:S(2)}, u32[]{:S(2)}) %collective-permute-start.25) | collective-permute-done | bytes 131104 | tf_op jit(solution)/shard_map/ppermute | solution.py:30
  111.1 10.7 %collective-permute-done.17.p3.refs_4_ = bf16[128,2048]{1,0:T(8,128)(2,1)S(1)} collective-permute-done((bf16[128,2048]{1,0:T(8,128)(2,1)}, bf16[128,2048]{1,0:T(8,128)(2,1)S(1)}, u32[]{:S(2)}, u32[]{:S(2)}) %collective-permute-start.17) | collective-permute-done | bytes 524320 | tf_op jit(solution)/shard_map/ppermute | solution.py:30
  121.8 2.7 %collective-permute-start.26 = (bf16[128,512]{1,0:T(8,128)(2,1)S(1)}, bf16[128,512]{1,0:T(8,128)(2,1)S(1)}, u32[]{:S(2)}, u32[]{:S(2)}) collective-permute-start(bf16[128,512]{1,0:T(8,128)(2,1)S(1)} %z_sum.2.refs_0_), channel_id=1, source_target_pairs={{0,128},{1,129},{2,130},{3,131},{4,132},{5,133},{6,134},{7,135},{8... | collective-permute-start | bytes 393224 | tf_op jit(solution)/shard_map/ppermute | solution.py:30
  125.3 6.4 %dscore.1 = (bf16[256,4096]{1,0:T(8,128)(2,1)}, bf16[256,512]{1,0:T(8,128)(2,1)}, f32[8,128]{1,0:T(8,128)}) custom-call(f32[4,2,8,1024]{3,2,1,0:T(8,128)} %get-tuple-element.46.probs, bf16[256,512]{1,0:T(8,128)(2,1)} %bitcast.8, bf16[256,4096]{1,0:T(8,128)(2,1)} %upstream.3, bf16[256,4096]{1,0:T(8,128)(2,1)} %queries.3, bf16[256,512]{1,0:T(8,128)(2,1)} %keys.1), custom_call_target="tpu_custom_call" | custom-call | flops 805306368 | bytes 7344128 | tf_op jit(solution)/shard_map/dscore/pallas_call | solution.py:236
  133.4 3.3 %join.1 = (bf16[128,8192]{1,0:T(8,128)(2,1)}, f32[8,128]{1,0:T(8,128)}) custom-call(bf16[128,2048]{1,0:T(8,128)(2,1)} %get-tuple-element.41.p0, bf16[128,2048]{1,0:T(8,128)(2,1)} %copy-done.5, bf16[128,2048]{1,0:T(8,128)(2,1)} %copy-done.6, bf16[128,2048]{1,0:T(8,128)(2,1)} %copy-done.7), custom_call_target="tpu_custom_call" | custom-call | bytes 4198400 | tf_op jit(solution)/shard_map/join/pallas_call | solution.py:55
  (112 shorter events, 17.1 us)
Async XLA Ops:
  0.6 27.6 %collective-permute-start = (bf16[256,512]{1,0:T(8,128)(2,1)}, bf16[256,512]{1,0:T(8,128)(2,1)S(1)}, u32[]{:S(2)}, u32[]{:S(2)}) collective-permute-start(bf16[256,512]{1,0:T(8,128)(2,1)} %a.1), channel_id=1, source_target_pairs={{0,208},{1,209},{2,210},{3,211},{4,212},{5,213},{6,214},{7,215},{8... | collective-permute-start | bytes 786440 | tf_op jit(solution)/shard_map/ppermute | solution.py:30
  8.5 20.4 %all-to-all-start = ((s32[32,8,128]{2,1,0:T(8,128)}), s32[32,8,128]{2,1,0:T(8,128)S(1)}, u32[]{:S(2)}, u32[]{:S(2)}) async-start(s32[32,8,128]{2,1,0:T(8,128)} %masks.1.after), calls=%async_computation | async-start | bytes 262144 | tf_op jit(solution)/shard_map/all_to_all | solution.py:421
  20.2 25.6 %collective-permute-start.1 = (bf16[128,2048]{1,0:T(8,128)(2,1)}, bf16[128,2048]{1,0:T(8,128)(2,1)S(1)}, u32[]{:S(2)}, u32[]{:S(2)}) collective-permute-start(bf16[128,2048]{1,0:T(8,128)(2,1)} %get-tuple-element.34), channel_id=1, source_target_pairs={{0,1},{1,2},{2,3},{3,0},{4,5},{5,6},{6,7},{7,4},{8,9},{9,10},{10,1... | collective-permute-start | bytes 1572872 | tf_op jit(solution)/shard_map/ppermute | solution.py:30
  21.5 25.5 %collective-permute-start.2 = (bf16[128,2048]{1,0:T(8,128)(2,1)}, bf16[128,2048]{1,0:T(8,128)(2,1)S(1)}, u32[]{:S(2)}, u32[]{:S(2)}) collective-permute-start(bf16[128,2048]{1,0:T(8,128)(2,1)} %get-tuple-element.35), channel_id=1, source_target_pairs={{0,2},{1,3},{2,0},{3,1},{4,6},{5,7},{6,4},{7,5},{8,10},{9,11},{10,... | collective-permute-start | bytes 1572872 | tf_op jit(solution)/shard_map/ppermute | solution.py:30
  23.9 23.5 %collective-permute-start.3 = (bf16[128,2048]{1,0:T(8,128)(2,1)}, bf16[128,2048]{1,0:T(8,128)(2,1)S(1)}, u32[]{:S(2)}, u32[]{:S(2)}) collective-permute-start(bf16[128,2048]{1,0:T(8,128)(2,1)} %get-tuple-element.36), channel_id=1, source_target_pairs={{0,3},{1,0},{2,1},{3,2},{4,7},{5,4},{6,5},{7,6},{8,11},{9,8},{10,9... | collective-permute-start | bytes 1572872 | tf_op jit(solution)/shard_map/ppermute | solution.py:30
  29.0 32.5 %copy-start.8 = (bf16[128,2048]{1,0:T(8,128)(2,1)S(1)}, bf16[128,2048]{1,0:T(8,128)(2,1)}, u32[]{:S(2)}) copy-start(bf16[128,2048]{1,0:T(8,128)(2,1)} %get-tuple-element.37.refs_0_) | copy-start | bytes 1572868
  32.9 21.3 %all-to-all-start.1 = ((bf16[32,8,512]{2,1,0:T(8,128)(2,1)}), bf16[32,8,512]{2,1,0:T(8,128)(2,1)S(1)}, u32[]{:S(2)}, u32[]{:S(2)}) async-start(bf16[32,8,512]{2,1,0:T(8,128)(2,1)} %bitcast.9), calls=%async_computation.1 | async-start | bytes 524288 | tf_op jit(solution)/shard_map/all_to_all | solution.py:421
  42.1 14.6 %collective-permute-start.7 = (bf16[256,512]{1,0:T(8,128)(2,1)S(1)}, bf16[256,512]{1,0:T(8,128)(2,1)S(1)}, u32[]{:S(2)}, u32[]{:S(2)}) collective-permute-start(bf16[256,512]{1,0:T(8,128)(2,1)S(1)} %copy-done.1), channel_id=1, source_target_pairs={{0,4},{1,5},{2,6},{3,7},{4,8},{5,9},{6,10},{7,11},{8,12},{9,13},{1... | collective-permute-start | bytes 786440 | tf_op jit(solution)/shard_map/ppermute | solution.py:30
  43.4 14.3 %collective-permute-start.8 = (bf16[256,512]{1,0:T(8,128)(2,1)S(1)}, bf16[256,512]{1,0:T(8,128)(2,1)S(1)}, u32[]{:S(2)}, u32[]{:S(2)}) collective-permute-start(bf16[256,512]{1,0:T(8,128)(2,1)S(1)} %copy-done.1), channel_id=1, source_target_pairs={{0,8},{1,9},{2,10},{3,11},{4,12},{5,13},{6,14},{7,15},{8,0},{9,1},... | collective-permute-start | bytes 786440 | tf_op jit(solution)/shard_map/ppermute | solution.py:30
  45.8 12.6 %collective-permute-start.9 = (bf16[256,512]{1,0:T(8,128)(2,1)S(1)}, bf16[256,512]{1,0:T(8,128)(2,1)S(1)}, u32[]{:S(2)}, u32[]{:S(2)}) collective-permute-start(bf16[256,512]{1,0:T(8,128)(2,1)S(1)} %copy-done.1), channel_id=1, source_target_pairs={{0,12},{1,13},{2,14},{3,15},{4,0},{5,1},{6,2},{7,3},{8,4},{9,5},{1... | collective-permute-start | bytes 786440 | tf_op jit(solution)/shard_map/ppermute | solution.py:30
  54.4 6.5 %collective-permute-start.4 = (bf16[128,512]{1,0:T(8,128)(2,1)S(1)}, bf16[128,512]{1,0:T(8,128)(2,1)S(1)}, u32[]{:S(2)}, u32[]{:S(2)}) collective-permute-start(bf16[128,512]{1,0:T(8,128)(2,1)S(1)} %pick.1.refs_4_.refs_0_), channel_id=1, source_target_pairs={{0,1},{1,2},{2,3},{3,0},{4,5},{5,6},{6,7},{7,4},{8,9},{9,10},{10,1... | collective-permute-start | bytes 393224 | tf_op jit(solution)/shard_map/ppermute | solution.py:30
  54.5 6.4 %collective-permute-start.5 = (bf16[128,512]{1,0:T(8,128)(2,1)S(1)}, bf16[128,512]{1,0:T(8,128)(2,1)S(1)}, u32[]{:S(2)}, u32[]{:S(2)}) collective-permute-start(bf16[128,512]{1,0:T(8,128)(2,1)S(1)} %pick.1.refs_4_.refs_0_), channel_id=1, source_target_pairs={{0,2},{1,3},{2,0},{3,1},{4,6},{5,7},{6,4},{7,5},{8,10},{9,11},{10,... | collective-permute-start | bytes 393224 | tf_op jit(solution)/shard_map/ppermute | solution.py:30
  56.7 4.8 %collective-permute-start.6 = (bf16[128,512]{1,0:T(8,128)(2,1)S(1)}, bf16[128,512]{1,0:T(8,128)(2,1)S(1)}, u32[]{:S(2)}, u32[]{:S(2)}) collective-permute-start(bf16[128,512]{1,0:T(8,128)(2,1)S(1)} %pick.1.refs_4_.refs_0_), channel_id=1, source_target_pairs={{0,3},{1,0},{2,1},{3,2},{4,7},{5,4},{6,5},{7,6},{8,11},{9,8},{10,9... | collective-permute-start | bytes 393224 | tf_op jit(solution)/shard_map/ppermute | solution.py:30
  63.7 7.5 %collective-permute-start.14 = (bf16[8,128,512]{2,1,0:T(8,128)(2,1)S(1)}, bf16[8,128,512]{2,1,0:T(8,128)(2,1)S(1)}, u32[]{:S(2)}, u32[]{:S(2)}) collective-permute-start(bf16[8,128,512]{2,1,0:T(8,128)(2,1)S(1)} %get-tuple-element.39), channel_id=1, source_target_pairs={{0,32},{1,33},{2,34},{3,35},{4,36},{5,37},{6,38},{7,39},{8,40},{9,... | collective-permute-start | bytes 3145736 | tf_op jit(solution)/shard_map/ppermute | solution.py:30
  69.0 5.0 %collective-permute-start.10 = (bf16[256,512]{1,0:T(8,128)(2,1)S(1)}, bf16[256,512]{1,0:T(8,128)(2,1)S(1)}, u32[]{:S(2)}, u32[]{:S(2)}) collective-permute-start(bf16[256,512]{1,0:T(8,128)(2,1)S(1)} %copy-done.1), channel_id=1, source_target_pairs={{0,32},{1,33},{2,34},{3,35},{4,36},{5,37},{6,38},{7,39},{8,40},{9,... | collective-permute-start | bytes 786440 | tf_op jit(solution)/shard_map/ppermute | solution.py:30
  69.1 5.3 %collective-permute-start.11 = (bf16[256,512]{1,0:T(8,128)(2,1)S(1)}, bf16[256,512]{1,0:T(8,128)(2,1)S(1)}, u32[]{:S(2)}, u32[]{:S(2)}) collective-permute-start(bf16[256,512]{1,0:T(8,128)(2,1)S(1)} %collective-permute-done.7.refs_8_.refs_5_), channel_id=1, source_target_pairs={{0,32},{1,33},{2,34},{3,35},{4,36},{5,37},{6,38},{7,39},{8,40},{9,... | collective-permute-start | bytes 786440 | tf_op jit(solution)/shard_map/ppermute | solution.py:30
  69.5 5.1 %collective-permute-start.12 = (bf16[256,512]{1,0:T(8,128)(2,1)S(1)}, bf16[256,512]{1,0:T(8,128)(2,1)S(1)}, u32[]{:S(2)}, u32[]{:S(2)}) collective-permute-start(bf16[256,512]{1,0:T(8,128)(2,1)S(1)} %collective-permute-done.8.refs_9_.refs_6_), channel_id=1, source_target_pairs={{0,32},{1,33},{2,34},{3,35},{4,36},{5,37},{6,38},{7,39},{8,40},{9,... | collective-permute-start | bytes 786440 | tf_op jit(solution)/shard_map/ppermute | solution.py:30
  69.6 5.0 %collective-permute-start.13 = (bf16[256,512]{1,0:T(8,128)(2,1)S(1)}, bf16[256,512]{1,0:T(8,128)(2,1)S(1)}, u32[]{:S(2)}, u32[]{:S(2)}) collective-permute-start(bf16[256,512]{1,0:T(8,128)(2,1)S(1)} %collective-permute-done.9.refs_10_.refs_7_), channel_id=1, source_target_pairs={{0,32},{1,33},{2,34},{3,35},{4,36},{5,37},{6,38},{7,39},{8,40},{9,... | collective-permute-start | bytes 786440 | tf_op jit(solution)/shard_map/ppermute | solution.py:30
  72.3 14.1 %collective-permute-start.21 = (bf16[2,128,512]{2,1,0:T(8,128)(2,1)S(1)}, bf16[2,128,512]{2,1,0:T(8,128)(2,1)S(1)}, u32[]{:S(2)}, u32[]{:S(2)}) collective-permute-start(bf16[2,128,512]{2,1,0:T(8,128)(2,1)S(1)} %get-tuple-element.52), channel_id=1, source_target_pairs={{0,12},{1,13},{2,14},{3,15},{4,0},{5,1},{6,2},{7,3},{8,4},{9,5},{1... | collective-permute-start | bytes 786440 | tf_op jit(solution)/shard_map/ppermute | solution.py:30
  74.0 13.3 %collective-permute-start.22 = (bf16[2,128,512]{2,1,0:T(8,128)(2,1)S(1)}, bf16[2,128,512]{2,1,0:T(8,128)(2,1)S(1)}, u32[]{:S(2)}, u32[]{:S(2)}) collective-permute-start(bf16[2,128,512]{2,1,0:T(8,128)(2,1)S(1)} %get-tuple-element.53), channel_id=1, source_target_pairs={{0,8},{1,9},{2,10},{3,11},{4,12},{5,13},{6,14},{7,15},{8,0},{9,1},... | collective-permute-start | bytes 786440 | tf_op jit(solution)/shard_map/ppermute | solution.py:30
  74.4 14.9 %collective-permute-start.23 = (bf16[2,128,512]{2,1,0:T(8,128)(2,1)S(1)}, bf16[2,128,512]{2,1,0:T(8,128)(2,1)S(1)}, u32[]{:S(2)}, u32[]{:S(2)}) collective-permute-start(bf16[2,128,512]{2,1,0:T(8,128)(2,1)S(1)} %get-tuple-element.54), channel_id=1, source_target_pairs={{0,4},{1,5},{2,6},{3,7},{4,8},{5,9},{6,10},{7,11},{8,12},{9,13},{1... | collective-permute-start | bytes 786440 | tf_op jit(solution)/shard_map/ppermute | solution.py:30
  79.7 12.9 %collective-permute-start.18 = (bf16[128,512]{1,0:T(8,128)(2,1)}, bf16[128,512]{1,0:T(8,128)(2,1)S(1)}, u32[]{:S(2)}, u32[]{:S(2)}) collective-permute-start(bf16[128,512]{1,0:T(8,128)(2,1)} %get-tuple-element.49), channel_id=1, source_target_pairs={{0,3},{1,0},{2,1},{3,2},{4,7},{5,4},{6,5},{7,6},{8,11},{9,8},{10,9... | collective-permute-start | bytes 393224 | tf_op jit(solution)/shard_map/ppermute | solution.py:30
  82.0 12.3 %collective-permute-start.19 = (bf16[128,512]{1,0:T(8,128)(2,1)}, bf16[128,512]{1,0:T(8,128)(2,1)S(1)}, u32[]{:S(2)}, u32[]{:S(2)}) collective-permute-start(bf16[128,512]{1,0:T(8,128)(2,1)} %get-tuple-element.50), channel_id=1, source_target_pairs={{0,2},{1,3},{2,0},{3,1},{4,6},{5,7},{6,4},{7,5},{8,10},{9,11},{10,... | collective-permute-start | bytes 393224 | tf_op jit(solution)/shard_map/ppermute | solution.py:30
  86.5 7.9 %collective-permute-start.20 = (bf16[128,512]{1,0:T(8,128)(2,1)S(1)}, bf16[128,512]{1,0:T(8,128)(2,1)S(1)}, u32[]{:S(2)}, u32[]{:S(2)}) collective-permute-start(bf16[128,512]{1,0:T(8,128)(2,1)S(1)} %copy-done.31), channel_id=1, source_target_pairs={{0,1},{1,2},{2,3},{3,0},{4,5},{5,6},{6,7},{7,4},{8,9},{9,10},{10,1... | collective-permute-start | bytes 393224 | tf_op jit(solution)/shard_map/ppermute | solution.py:30
  90.1 5.9 %collective-permute-start.24 = (bf16[128,512]{1,0:T(8,128)(2,1)S(1)}, bf16[128,512]{1,0:T(8,128)(2,1)S(1)}, u32[]{:S(2)}, u32[]{:S(2)}) collective-permute-start(bf16[128,512]{1,0:T(8,128)(2,1)S(1)} %get-tuple-element.57), channel_id=1, source_target_pairs={{0,208},{1,209},{2,210},{3,211},{4,212},{5,213},{6,214},{7,215},{8... | collective-permute-start | bytes 393224 | tf_op jit(solution)/shard_map/ppermute | solution.py:30
  90.6 20.5 %collective-permute-start.15 = (bf16[128,2048]{1,0:T(8,128)(2,1)}, bf16[128,2048]{1,0:T(8,128)(2,1)S(1)}, u32[]{:S(2)}, u32[]{:S(2)}) collective-permute-start(bf16[128,2048]{1,0:T(8,128)(2,1)} %get-tuple-element.42), channel_id=1, source_target_pairs={{0,3},{1,0},{2,1},{3,2},{4,7},{5,4},{6,5},{7,6},{8,11},{9,8},{10,9... | collective-permute-start | bytes 1572872 | tf_op jit(solution)/shard_map/ppermute | solution.py:30
  92.6 18.5 %collective-permute-start.16 = (bf16[128,2048]{1,0:T(8,128)(2,1)}, bf16[128,2048]{1,0:T(8,128)(2,1)S(1)}, u32[]{:S(2)}, u32[]{:S(2)}) collective-permute-start(bf16[128,2048]{1,0:T(8,128)(2,1)} %get-tuple-element.43), channel_id=1, source_target_pairs={{0,2},{1,3},{2,0},{3,1},{4,6},{5,7},{6,4},{7,5},{8,10},{9,11},{10,... | collective-permute-start | bytes 1572872 | tf_op jit(solution)/shard_map/ppermute | solution.py:30
  94.4 27.4 %collective-permute-start.17 = (bf16[128,2048]{1,0:T(8,128)(2,1)}, bf16[128,2048]{1,0:T(8,128)(2,1)S(1)}, u32[]{:S(2)}, u32[]{:S(2)}) collective-permute-start(bf16[128,2048]{1,0:T(8,128)(2,1)} %get-tuple-element.44), channel_id=1, source_target_pairs={{0,1},{1,2},{2,3},{3,0},{4,5},{5,6},{6,7},{7,4},{8,9},{9,10},{10,1... | collective-permute-start | bytes 1572872 | tf_op jit(solution)/shard_map/ppermute | solution.py:30
  97.0 27.6 %all-to-all-start.2 = ((bf16[32,8,512]{2,1,0:T(8,128)(2,1)}), bf16[32,8,512]{2,1,0:T(8,128)(2,1)S(1)}, u32[]{:S(2)}, u32[]{:S(2)}) async-start(bf16[32,8,512]{2,1,0:T(8,128)(2,1)} %bitcast.3), calls=%async_computation.2 | async-start | bytes 524288 | tf_op jit(solution)/shard_map/all_to_all | solution.py:421
  104.1 7.0 %collective-permute-start.25 = (bf16[128,512]{1,0:T(8,128)(2,1)S(1)}, bf16[128,512]{1,0:T(8,128)(2,1)S(1)}, u32[]{:S(2)}, u32[]{:S(2)}) collective-permute-start(bf16[128,512]{1,0:T(8,128)(2,1)S(1)} %mirror_sum.1.after.refs_0_), channel_id=1, source_target_pairs={{0,64},{1,65},{2,66},{3,67},{4,68},{5,69},{6,70},{7,71},{8,72},{9,... | collective-permute-start | bytes 393224 | tf_op jit(solution)/shard_map/ppermute | solution.py:30
  121.8 9.9 %collective-permute-start.26 = (bf16[128,512]{1,0:T(8,128)(2,1)S(1)}, bf16[128,512]{1,0:T(8,128)(2,1)S(1)}, u32[]{:S(2)}, u32[]{:S(2)}) collective-permute-start(bf16[128,512]{1,0:T(8,128)(2,1)S(1)} %z_sum.2.refs_0_), channel_id=1, source_target_pairs={{0,128},{1,129},{2,130},{3,131},{4,132},{5,133},{6,134},{7,135},{8... | collective-permute-start | bytes 393224 | tf_op jit(solution)/shard_map/ppermute | solution.py:30
  132.4 4.3 %collective-permute-start.27 = (bf16[128,512]{1,0:T(8,128)(2,1)S(1)}, bf16[128,512]{1,0:T(8,128)(2,1)S(1)}, u32[]{:S(2)}, u32[]{:S(2)}) collective-permute-start(bf16[128,512]{1,0:T(8,128)(2,1)S(1)} %z_sum.3.mine), channel_id=1, source_target_pairs={{0,32},{1,33},{2,34},{3,35},{4,36},{5,37},{6,38},{7,39},{8,40},{9,... | collective-permute-start | bytes 393224 | tf_op jit(solution)/shard_map/ppermute | solution.py:30
  (31 other events, 286.4 us)

commit v3 on v2

--- a/solution.py
+++ b/solution.py
@@ -141,8 +141,7 @@
     return call(split_kernel, "split", out, full, after, ins=[ANY] * 2, scratch=scratch, mib=56)
 
 
-def join_kernel(p0, p1, p2, p3, full, token):
-    finish(token)
+def join_kernel(p0, p1, p2, p3, full):
     width = p0.shape[1] // (SLICES * NCO)
     for k, part in enumerate((p0, p1, p2, p3)):
         for at, block in feature_blocks(k):
@@ -151,7 +150,7 @@
 
 def join(parts):
     rows, columns = parts[0].shape
-    return call(join_kernel, "join", [like((rows, columns * NY), parts[0].dtype), TOKEN], *parts, mib=56)
+    return call(join_kernel, "join", [like((rows, columns * NY), parts[0].dtype)], *parts, mib=56)[0]
 
 
 def heads(block, t):
@@ -215,8 +214,8 @@
             grad_v[t * TILE : (t + 1) * TILE, k * HD : (k + 1) * HD] = grad.astype(BF16)
 
 
-def dscore_kernel(probs, values, upstream, queries, keys, grad_q, grad_k, token):
-    finish(token)
+def dscore_kernel(probs, values, upstream, queries, keys, *rest):
+    grad_q, grad_k = rest[-2:]
     scale = 1.0 / HD**0.5
     block = own_block(GROUP * TILE)
     for t in range(probs.shape[1]):
@@ -277,13 +276,12 @@
     return call(probs_kernel, "probs", out, scores, masks, upstream, *after, ins=ins, scratch=scratch, mib=56, flops=flops)
 
 
-def attention_dscore(probs, values, upstream, queries, keys):
+def attention_dscore(probs, values, upstream, queries, keys, after):
     wide, narrow, folded, _ = attention_specs(queries.shape[0])
-    token = (TOKEN, pl.BlockSpec(TOKEN.shape, lambda k: (0, 0)))
-    outs = [(like(queries.shape, BF16), wide), (like(keys.shape, BF16), narrow), token]
-    args = (probs, values, upstream, queries, keys)
+    outs = [(like(queries.shape, BF16), wide), (like(keys.shape, BF16), narrow)]
+    args = (probs, values, upstream, queries, keys, *after)
     flops = 6 * upstream.size * TILE
-    return per_head(dscore_kernel, "dscore", [folded, narrow, wide, wide, narrow], outs, args, flops)
+    return per_head(dscore_kernel, "dscore", [folded, narrow, wide, wide, narrow] + [ANY] * len(after), outs, args, flops)
 
 
 def slice_of(weights, s):
@@ -405,7 +403,7 @@
     out[...] = (a[...].astype(F32) + b[...].astype(F32)).astype(out.dtype)
 
 
-def halves_kernel(mine, other, after, out):
+def halves_kernel(mine, other, out):
     core, rows = at_place()[0], mine.shape[0]
     out[pl.ds(pl.multiple_of(core * rows, rows), rows), :] = mine[...]
     out[pl.ds(pl.multiple_of((1 - core) * rows, rows), rows), :] = other[...]
@@ -449,20 +447,19 @@
 
     out = [like((half, width), F32), like((half, width), BF16)]
     near, far = call(x_sum_kernel, "x_sum", out, keep, *arrived, backed, ins=[VMEM] * NX + [ANY])
-    small, order = [like((half, width), BF16)], [VMEM, VMEM, ANY]
+    small = [like((half, width), BF16)]
     total = call(pair_sum_kernel, "mirror_sum", small, near, permute(far, mirror), *parts, ins=[VMEM] * 2 + [ANY] * (NY - 1))[0]
 
     after, out = [VMEM] * 5 + [ANY], [like((slots, width), BF16)]
     value_buffer = call(place_kernel, "place", out, slot, partial, *parts, total, ins=after)[0]
     values = exchange(value_buffer)
-    grad_q, grad_k, scored = attention_dscore(probs, values, upstream, queries, keys)
-    grad_inputs, joined = join(columns)
-
-    after = [VMEM] * 2 + [ANY] * (NY - 1)
-    total = call(pair_sum_kernel, "z_sum", small, total, permute(total, flip_zl(1)), *columns[1:], ins=after)[0]
-    total = call(pair_sum_kernel, "z_sum", small, total, permute(total, flip_zl(2)), scored, ins=order)[0]
+    grad_q, grad_k = attention_dscore(probs, values, upstream, queries, keys, columns[1:])
+    grad_inputs = join(columns)
+
+    for bit in (1, 2):
+        total = call(pair_sum_kernel, "z_sum", small, total, permute(total, flip_zl(bit)))[0]
     out = [like((NCO * half, width), BF16)]
-    grad_weight = call(halves_kernel, "halves", out, total, permute(total, other_core), joined, ins=order)[0]
+    grad_weight = call(halves_kernel, "halves", out, total, permute(total, other_core))[0]
     return grad_inputs, grad_q, grad_k, grad_weight
 
 

time: 139 us -> 137 us (0.986)
  waiting for transfers between devices: 30.4 us -> 27.2 us
    ppermute x28, waiting for transfers between devices: 23.6 us -> 20.4 us  [permute(): return lax.ppermute(array, AXES, pairs)]
    unnamed x64 -> x60, local copies, waits for them, and re-layouts: 5.76 us -> 5.55 us
  transfers between devices with their start and end apart: 31 -> 31, of which waited for: 10 -> 10; matrix products, arithmetic and copies ran while one was open for 0% -> 0% of each run, Pallas kernels for 23% -> 19%
where the time goes in v3:
time: 137 us; the launch traced here: 136 us
  starting transfers between devices  68.1 us (50%)
  Pallas kernels  34.1 us (25%)
  waiting for transfers between devices  27.2 us (20%)
  local copies, waits for them, and re-layouts  5.55 us (4%)
    ppermute x28, starting transfers between devices, permute(): return lax.ppermute(array, AXES, pairs)  43.6 us
    pallas_call x17, Pallas kernels, call(): pl.pallas_call(kernel, out_shape=out, in_specs=[VMEM] * len(args) if ins...  27.7 us
    all_to_all x3, starting transfers between devices, exchange(): lax.all_to_all(buffer, 'fsdp', split_axis=0, concat_axis=0, tiled=True)  24.5 us
    ppermute x28, waiting for transfers between devices, permute(): return lax.ppermute(array, AXES, pairs)  20.4 us
    all_to_all x3, waiting for transfers between devices, exchange(): lax.all_to_all(buffer, 'fsdp', split_axis=0, concat_axis=0, tiled=True)  6.79 us
    pallas_call x1, Pallas kernels, per_head(): pl.pallas_call(kernel, grid=(KVH,), out_shape=[o for o, _ in outs], in_sp...  6.41 us
    unnamed x60, local copies, waits for them, and re-layouts  5.55 us
  transfers between devices with their start and end apart: 31, of which 10 were waited for; matrix products, arithmetic and copies ran while one was open for 0% of the time, Pallas kernels for 19%

profile of v3, /device:TPU:1, one launch (start us, length us, event | category | flops | bytes accessed | tf_op | source)
XLA Modules:
  0.0 136.0 jit_solution(18340785408396897444)
XLA Ops:
  0.6 6.5 %collective-permute-start = (bf16[256,512]{1,0:T(8,128)(2,1)}, bf16[256,512]{1,0:T(8,128)(2,1)S(1)}, u32[]{:S(2)}, u32[]{:S(2)}) collective-permute-start(bf16[256,512]{1,0:T(8,128)(2,1)} %a.1), channel_id=1, source_target_pairs={{0,208},{1,209},{2,210},{3,211},{4,212},{5,213},{6,214},{7,215},{8... | collective-permute-start | bytes 786440 | tf_op jit(solution)/shard_map/ppermute | solution.py:30
  7.1 1.4 %masks.1.after = s32[32,8,128]{2,1,0:T(8,128)} custom-call(s32[128]{0:T(128)} %slots_in.1, s32[128]{0:T(128)} %ids_in.1), custom_call_target="tpu_custom_call" | custom-call | bytes 132096 | tf_op jit(solution)/shard_map/masks/pallas_call | solution.py:55
  8.5 8.1 %all-to-all-start = ((s32[32,8,128]{2,1,0:T(8,128)}), s32[32,8,128]{2,1,0:T(8,128)S(1)}, u32[]{:S(2)}, u32[]{:S(2)}) async-start(s32[32,8,128]{2,1,0:T(8,128)} %masks.1.after), calls=%async_computation | async-start | bytes 262144 | tf_op jit(solution)/shard_map/all_to_all | solution.py:419
  16.7 3.5 %split.1 = (bf16[128,2048]{1,0:T(8,128)(2,1)}, bf16[128,2048]{1,0:T(8,128)(2,1)}, bf16[128,2048]{1,0:T(8,128)(2,1)}, bf16[128,2048]{1,0:T(8,128)(2,1)}) custom-call(bf16[128,8192]{1,0:T(8,128)(2,1)} %full_in.1, s32[32,8,128]{2,1,0:T(8,128)} %masks.1.after), custom_call_target="tpu_custom_call" | custom-call | bytes 4325376 | tf_op jit(solution)/shard_map/split/pallas_call | solution.py:55
  20.2 1.3 collective-permute-start.1
  21.5 2.4 %collective-permute-start.2 = (bf16[128,2048]{1,0:T(8,128)(2,1)}, bf16[128,2048]{1,0:T(8,128)(2,1)S(1)}, u32[]{:S(2)}, u32[]{:S(2)}) collective-permute-start(bf16[128,2048]{1,0:T(8,128)(2,1)} %get-tuple-element.32), channel_id=1, source_target_pairs={{0,2},{1,3},{2,0},{3,1},{4,6},{5,7},{6,4},{7,5},{8,10},{9,11},{10,... | collective-permute-start | bytes 1572872 | tf_op jit(solution)/shard_map/ppermute | solution.py:30
  25.1 3.1 %scores.1.scores_in = f32[4,2,8,1024]{3,2,1,0:T(8,128)} custom-call(bf16[256,4096]{1,0:T(8,128)(2,1)} %queries.3, bf16[256,512]{1,0:T(8,128)(2,1)} %keys.1), custom_call_target="tpu_custom_call" | custom-call | flops 268435456 | bytes 2621440 | tf_op jit(solution)/shard_map/scores/pallas_call | solution.py:55
  29.6 3.3 %probs.1 = (bf16[256,512]{1,0:T(8,128)(2,1)}, f32[4,2,8,1024]{3,2,1,0:T(8,128)}) custom-call(f32[4,2,8,1024]{3,2,1,0:T(8,128)} %scores.1.scores_in, s32[32,8,128]{2,1,0:T(8,128)} %copy-done.24, bf16[256,4096]{1,0:T(8,128)(2,1)} %upstream.3, bf16[256,512]{1,0:T(8,128)(2,1)} %copy-done), custom_call_target="tpu_custom_call" | custom-call | flops 268435456 | bytes 3276800 | tf_op jit(solution)/shard_map/probs/pallas_call | solution.py:55
  32.9 9.3 %all-to-all-start.1 = ((bf16[32,8,512]{2,1,0:T(8,128)(2,1)}), bf16[32,8,512]{2,1,0:T(8,128)(2,1)S(1)}, u32[]{:S(2)}, u32[]{:S(2)}) async-start(bf16[32,8,512]{2,1,0:T(8,128)(2,1)} %bitcast.9), calls=%async_computation.1 | async-start | bytes 524288 | tf_op jit(solution)/shard_map/all_to_all | solution.py:419
  42.1 1.3 collective-permute-start.7
  43.5 2.4 %collective-permute-start.8 = (bf16[256,512]{1,0:T(8,128)(2,1)S(1)}, bf16[256,512]{1,0:T(8,128)(2,1)S(1)}, u32[]{:S(2)}, u32[]{:S(2)}) collective-permute-start(bf16[256,512]{1,0:T(8,128)(2,1)S(1)} %copy-done.1), channel_id=1, source_target_pairs={{0,8},{1,9},{2,10},{3,11},{4,12},{5,13},{6,14},{7,15},{8,0},{9,1},... | collective-permute-start | bytes 786440 | tf_op jit(solution)/shard_map/ppermute | solution.py:30
  47.4 6.8 %all-to-all-done.1 = bf16[32,8,512]{2,1,0:T(8,128)(2,1)S(1)} async-done(((bf16[32,8,512]{2,1,0:T(8,128)(2,1)}), bf16[32,8,512]{2,1,0:T(8,128)(2,1)S(1)}, u32[]{:S(2)}, u32[]{:S(2)}) %all-to-all-start.1) | async-done | bytes 262176 | tf_op jit(solution)/shard_map/all_to_all | solution.py:419
  54.5 2.2 %collective-permute-start.5 = (bf16[128,512]{1,0:T(8,128)(2,1)S(1)}, bf16[128,512]{1,0:T(8,128)(2,1)S(1)}, u32[]{:S(2)}, u32[]{:S(2)}) collective-permute-start(bf16[128,512]{1,0:T(8,128)(2,1)S(1)} %pick.1.refs_4_.refs_0_), channel_id=1, source_target_pairs={{0,2},{1,3},{2,0},{3,1},{4,6},{5,7},{6,4},{7,5},{8,10},{9,11},{10,... | collective-permute-start | bytes 393224 | tf_op jit(solution)/shard_map/ppermute | solution.py:30
  58.4 2.5 %collective-permute-done.4.refs_5_.refs_1_ = bf16[128,512]{1,0:T(8,128)(2,1)S(1)} collective-permute-done((bf16[128,512]{1,0:T(8,128)(2,1)S(1)}, bf16[128,512]{1,0:T(8,128)(2,1)S(1)}, u32[]{:S(2)}, u32[]{:S(2)}) %collective-permute-start.4) | collective-permute-done | bytes 131104 | tf_op jit(solution)/shard_map/ppermute | solution.py:30
  61.5 2.2 %shares.1 = (f32[8,128,512]{2,1,0:T(8,128)S(1)}, bf16[8,128,512]{2,1,0:T(8,128)(2,1)S(1)}, f32[8,128]{1,0:T(8,128)S(1)}) custom-call(bf16[128,2048]{1,0:T(8,128)(2,1)S(1)} %copy-done.5, bf16[128,2048]{1,0:T(8,128)(2,1)S(1)} %collective-permute-done.1.refs_2_.refs_1_, bf16[128,2048]{1,0:T(8,128)(2,1)S(1)} %collective-permute-done.2.refs_3_.refs_2_, ...), custom_call_target="tpu_custom_call" | custom-call | flops 1073741824 | bytes 6557696 | tf_op jit(solution)/shard_map/shares/pallas_call | solution.py:55
  63.8 5.2 %collective-permute-start.14 = (bf16[8,128,512]{2,1,0:T(8,128)(2,1)S(1)}, bf16[8,128,512]{2,1,0:T(8,128)(2,1)S(1)}, u32[]{:S(2)}, u32[]{:S(2)}) collective-permute-start(bf16[8,128,512]{2,1,0:T(8,128)(2,1)S(1)} %get-tuple-element.36), channel_id=1, source_target_pairs={{0,32},{1,33},{2,34},{3,35},{4,36},{5,37},{6,38},{7,39},{8,40},{9,... | collective-permute-start | bytes 3145736 | tf_op jit(solution)/shard_map/ppermute | solution.py:30
  70.0 1.3 collective-permute-done.14.got
  72.3 1.6 %collective-permute-start.21 = (bf16[2,128,512]{2,1,0:T(8,128)(2,1)S(1)}, bf16[2,128,512]{2,1,0:T(8,128)(2,1)S(1)}, u32[]{:S(2)}, u32[]{:S(2)}) collective-permute-start(bf16[2,128,512]{2,1,0:T(8,128)(2,1)S(1)} %get-tuple-element.48), channel_id=1, source_target_pairs={{0,12},{1,13},{2,14},{3,15},{4,0},{5,1},{6,2},{7,3},{8,4},{9,5},{1... | collective-permute-start | bytes 786440 | tf_op jit(solution)/shard_map/ppermute | solution.py:30
  75.4 4.2 %partial_values.1 = (f32[128,512]{1,0:T(8,128)}, bf16[128,512]{1,0:T(8,128)(2,1)}, bf16[128,512]{1,0:T(8,128)(2,1)}, bf16[128,512]{1,0:T(8,128)(2,1)}) custom-call(bf16[128,2048]{1,0:T(8,128)(2,1)} %get-tuple-element.34.refs_0_, bf16[128,2048]{1,0:T(8,128)(2,1)} %copy-done.2, bf16[128,2048]{1,0:T(8,128)(2,1)} %copy-done.3, bf16[128,2048]{1,0:T(8,128)(2,1)} %copy-done.4, ...), custom_call_target="tpu_custom_call" | custom-call | flops 1073741824 | bytes 4853760 | tf_op jit(solution)/shard_map/partial_values/pallas_call | solution.py:55
  79.7 2.3 %collective-permute-start.18 = (bf16[128,512]{1,0:T(8,128)(2,1)}, bf16[128,512]{1,0:T(8,128)(2,1)S(1)}, u32[]{:S(2)}, u32[]{:S(2)}) collective-permute-start(bf16[128,512]{1,0:T(8,128)(2,1)} %get-tuple-element.45), channel_id=1, source_target_pairs={{0,3},{1,0},{2,1},{3,2},{4,7},{5,4},{6,5},{7,6},{8,11},{9,8},{10,9... | collective-permute-start | bytes 393224 | tf_op jit(solution)/shard_map/ppermute | solution.py:30
  82.0 4.4 %back.1 = (bf16[128,2048]{1,0:T(8,128)(2,1)}, bf16[128,2048]{1,0:T(8,128)(2,1)}, bf16[128,2048]{1,0:T(8,128)(2,1)}, bf16[128,2048]{1,0:T(8,128)(2,1)}, f32[8,128]{1,0:T(8,128)}) custom-call(bf16[128,512]{1,0:T(8,128)(2,1)} %copy-done.13, bf16[128,512]{1,0:T(8,128)(2,1)} %copy-done.17, bf16[128,512]{1,0:T(8,128)(2,1)} %copy-done.18, ...), custom_call_target="tpu_custom_call" | custom-call | flops 1073741824 | bytes 5246976 | tf_op jit(solution)/shard_map/back/pallas_call | solution.py:55
  87.2 2.1 %collective-permute-done.23.c = bf16[2,128,512]{2,1,0:T(8,128)(2,1)S(1)} collective-permute-done((bf16[2,128,512]{2,1,0:T(8,128)(2,1)S(1)}, bf16[2,128,512]{2,1,0:T(8,128)(2,1)S(1)}, u32[]{:S(2)}, u32[]{:S(2)}) %collective-permute-start.23) | collective-permute-done | bytes 262176 | tf_op jit(solution)/shard_map/ppermute | solution.py:30
  90.6 2.0 %collective-permute-start.15 = (bf16[128,2048]{1,0:T(8,128)(2,1)}, bf16[128,2048]{1,0:T(8,128)(2,1)S(1)}, u32[]{:S(2)}, u32[]{:S(2)}) collective-permute-start(bf16[128,2048]{1,0:T(8,128)(2,1)} %get-tuple-element.39), channel_id=1, source_target_pairs={{0,3},{1,0},{2,1},{3,2},{4,7},{5,4},{6,5},{7,6},{8,11},{9,8},{10,9... | collective-permute-start | bytes 1572872 | tf_op jit(solution)/shard_map/ppermute | solution.py:30
  92.6 1.8 %collective-permute-start.16 = (bf16[128,2048]{1,0:T(8,128)(2,1)}, bf16[128,2048]{1,0:T(8,128)(2,1)S(1)}, u32[]{:S(2)}, u32[]{:S(2)}) collective-permute-start(bf16[128,2048]{1,0:T(8,128)(2,1)} %get-tuple-element.40), channel_id=1, source_target_pairs={{0,2},{1,3},{2,0},{3,1},{4,6},{5,7},{6,4},{7,5},{8,10},{9,11},{10,... | collective-permute-start | bytes 1572872 | tf_op jit(solution)/shard_map/ppermute | solution.py:30
  94.4 1.6 %collective-permute-done.24.refs_1_ = bf16[128,512]{1,0:T(8,128)(2,1)S(1)} collective-permute-done((bf16[128,512]{1,0:T(8,128)(2,1)S(1)}, bf16[128,512]{1,0:T(8,128)(2,1)S(1)}, u32[]{:S(2)}, u32[]{:S(2)}) %collective-permute-start.24) | collective-permute-done | bytes 131104 | tf_op jit(solution)/shard_map/ppermute | solution.py:30
  97.0 7.1 %all-to-all-start.2 = ((bf16[32,8,512]{2,1,0:T(8,128)(2,1)}), bf16[32,8,512]{2,1,0:T(8,128)(2,1)S(1)}, u32[]{:S(2)}, u32[]{:S(2)}) async-start(bf16[32,8,512]{2,1,0:T(8,128)(2,1)} %bitcast.3), calls=%async_computation.2 | async-start | bytes 524288 | tf_op jit(solution)/shard_map/all_to_all | solution.py:419
  104.1 3.2 %collective-permute-start.25 = (bf16[128,512]{1,0:T(8,128)(2,1)S(1)}, bf16[128,512]{1,0:T(8,128)(2,1)S(1)}, u32[]{:S(2)}, u32[]{:S(2)}) collective-permute-start(bf16[128,512]{1,0:T(8,128)(2,1)S(1)} %mirror_sum.1.after.refs_0_), channel_id=1, source_target_pairs={{0,64},{1,65},{2,66},{3,67},{4,68},{5,69},{6,70},{7,71},{8,72},{9,... | collective-permute-start | bytes 393224 | tf_op jit(solution)/shard_map/ppermute | solution.py:30
  107.3 3.8 %collective-permute-done.25.refs_1_ = bf16[128,512]{1,0:T(8,128)(2,1)S(1)} collective-permute-done((bf16[128,512]{1,0:T(8,128)(2,1)S(1)}, bf16[128,512]{1,0:T(8,128)(2,1)S(1)}, u32[]{:S(2)}, u32[]{:S(2)}) %collective-permute-start.25) | collective-permute-done | bytes 131104 | tf_op jit(solution)/shard_map/ppermute | solution.py:30
  112.0 7.5 %collective-permute-done.26.refs_1_ = bf16[128,512]{1,0:T(8,128)(2,1)S(1)} collective-permute-done((bf16[128,512]{1,0:T(8,128)(2,1)S(1)}, bf16[128,512]{1,0:T(8,128)(2,1)S(1)}, u32[]{:S(2)}, u32[]{:S(2)}) %collective-permute-start.26) | collective-permute-done | bytes 131104 | tf_op jit(solution)/shard_map/ppermute | solution.py:30
  119.5 4.1 %collective-permute-start.27 = (bf16[128,512]{1,0:T(8,128)(2,1)S(1)}, bf16[128,512]{1,0:T(8,128)(2,1)S(1)}, u32[]{:S(2)}, u32[]{:S(2)}) collective-permute-start(bf16[128,512]{1,0:T(8,128)(2,1)S(1)} %z_sum.3.mine), channel_id=1, source_target_pairs={{0,32},{1,33},{2,34},{3,35},{4,36},{5,37},{6,38},{7,39},{8,40},{9,... | collective-permute-start | bytes 393224 | tf_op jit(solution)/shard_map/ppermute | solution.py:30
  124.8 3.3 %join.1 = bf16[128,8192]{1,0:T(8,128)(2,1)} custom-call(bf16[128,2048]{1,0:T(8,128)(2,1)} %get-tuple-element.38.p0, bf16[128,2048]{1,0:T(8,128)(2,1)} %copy-done.20, bf16[128,2048]{1,0:T(8,128)(2,1)} %copy-done.21, bf16[128,2048]{1,0:T(8,128)(2,1)} %copy-done.22), custom_call_target="tpu_custom_call" | custom-call | bytes 4194304 | tf_op jit(solution)/shard_map/join/pallas_call | solution.py:55
  129.6 6.4 %dscore.1 = (bf16[256,4096]{1,0:T(8,128)(2,1)}, bf16[256,512]{1,0:T(8,128)(2,1)}) custom-call(f32[4,2,8,1024]{3,2,1,0:T(8,128)} %get-tuple-element.42.probs, bf16[256,512]{1,0:T(8,128)(2,1)} %bitcast.8, bf16[256,4096]{1,0:T(8,128)(2,1)} %upstream.3, bf16[256,4096]{1,0:T(8,128)(2,1)} %queries.3, bf16[256,512]{1,0:T(8,128)(2,1)} %keys.1, ...), custom_call_target="tpu_custom_call" | custom-call | flops 805306368 | bytes 8912896 | tf_op jit(solution)/shard_map/dscore/pallas_call | solution.py:235
  (108 shorter events, 16.8 us)
Async XLA Ops:
  0.6 27.6 %collective-permute-start = (bf16[256,512]{1,0:T(8,128)(2,1)}, bf16[256,512]{1,0:T(8,128)(2,1)S(1)}, u32[]{:S(2)}, u32[]{:S(2)}) collective-permute-start(bf16[256,512]{1,0:T(8,128)(2,1)} %a.1), channel_id=1, source_target_pairs={{0,208},{1,209},{2,210},{3,211},{4,212},{5,213},{6,214},{7,215},{8... | collective-permute-start | bytes 786440 | tf_op jit(solution)/shard_map/ppermute | solution.py:30
  8.5 20.4 %all-to-all-start = ((s32[32,8,128]{2,1,0:T(8,128)}), s32[32,8,128]{2,1,0:T(8,128)S(1)}, u32[]{:S(2)}, u32[]{:S(2)}) async-start(s32[32,8,128]{2,1,0:T(8,128)} %masks.1.after), calls=%async_computation | async-start | bytes 262144 | tf_op jit(solution)/shard_map/all_to_all | solution.py:419
  20.2 25.7 %collective-permute-start.1 = (bf16[128,2048]{1,0:T(8,128)(2,1)}, bf16[128,2048]{1,0:T(8,128)(2,1)S(1)}, u32[]{:S(2)}, u32[]{:S(2)}) collective-permute-start(bf16[128,2048]{1,0:T(8,128)(2,1)} %get-tuple-element.31), channel_id=1, source_target_pairs={{0,1},{1,2},{2,3},{3,0},{4,5},{5,6},{6,7},{7,4},{8,9},{9,10},{10,1... | collective-permute-start | bytes 1572872 | tf_op jit(solution)/shard_map/ppermute | solution.py:30
  21.5 25.5 %collective-permute-start.2 = (bf16[128,2048]{1,0:T(8,128)(2,1)}, bf16[128,2048]{1,0:T(8,128)(2,1)S(1)}, u32[]{:S(2)}, u32[]{:S(2)}) collective-permute-start(bf16[128,2048]{1,0:T(8,128)(2,1)} %get-tuple-element.32), channel_id=1, source_target_pairs={{0,2},{1,3},{2,0},{3,1},{4,6},{5,7},{6,4},{7,5},{8,10},{9,11},{10,... | collective-permute-start | bytes 1572872 | tf_op jit(solution)/shard_map/ppermute | solution.py:30
  23.9 23.5 %collective-permute-start.3 = (bf16[128,2048]{1,0:T(8,128)(2,1)}, bf16[128,2048]{1,0:T(8,128)(2,1)S(1)}, u32[]{:S(2)}, u32[]{:S(2)}) collective-permute-start(bf16[128,2048]{1,0:T(8,128)(2,1)} %get-tuple-element.33), channel_id=1, source_target_pairs={{0,3},{1,0},{2,1},{3,2},{4,7},{5,4},{6,5},{7,6},{8,11},{9,8},{10,9... | collective-permute-start | bytes 1572872 | tf_op jit(solution)/shard_map/ppermute | solution.py:30
  28.9 32.6 %copy-start.5 = (bf16[128,2048]{1,0:T(8,128)(2,1)S(1)}, bf16[128,2048]{1,0:T(8,128)(2,1)}, u32[]{:S(2)}) copy-start(bf16[128,2048]{1,0:T(8,128)(2,1)} %get-tuple-element.34.refs_0_) | copy-start | bytes 1572868
  32.9 21.3 %all-to-all-start.1 = ((bf16[32,8,512]{2,1,0:T(8,128)(2,1)}), bf16[32,8,512]{2,1,0:T(8,128)(2,1)S(1)}, u32[]{:S(2)}, u32[]{:S(2)}) async-start(bf16[32,8,512]{2,1,0:T(8,128)(2,1)} %bitcast.9), calls=%async_computation.1 | async-start | bytes 524288 | tf_op jit(solution)/shard_map/all_to_all | solution.py:419
  42.1 14.6 %collective-permute-start.7 = (bf16[256,512]{1,0:T(8,128)(2,1)S(1)}, bf16[256,512]{1,0:T(8,128)(2,1)S(1)}, u32[]{:S(2)}, u32[]{:S(2)}) collective-permute-start(bf16[256,512]{1,0:T(8,128)(2,1)S(1)} %copy-done.1), channel_id=1, source_target_pairs={{0,4},{1,5},{2,6},{3,7},{4,8},{5,9},{6,10},{7,11},{8,12},{9,13},{1... | collective-permute-start | bytes 786440 | tf_op jit(solution)/shard_map/ppermute | solution.py:30
  43.5 14.3 %collective-permute-start.8 = (bf16[256,512]{1,0:T(8,128)(2,1)S(1)}, bf16[256,512]{1,0:T(8,128)(2,1)S(1)}, u32[]{:S(2)}, u32[]{:S(2)}) collective-permute-start(bf16[256,512]{1,0:T(8,128)(2,1)S(1)} %copy-done.1), channel_id=1, source_target_pairs={{0,8},{1,9},{2,10},{3,11},{4,12},{5,13},{6,14},{7,15},{8,0},{9,1},... | collective-permute-start | bytes 786440 | tf_op jit(solution)/shard_map/ppermute | solution.py:30
  45.9 12.6 %collective-permute-start.9 = (bf16[256,512]{1,0:T(8,128)(2,1)S(1)}, bf16[256,512]{1,0:T(8,128)(2,1)S(1)}, u32[]{:S(2)}, u32[]{:S(2)}) collective-permute-start(bf16[256,512]{1,0:T(8,128)(2,1)S(1)} %copy-done.1), channel_id=1, source_target_pairs={{0,12},{1,13},{2,14},{3,15},{4,0},{5,1},{6,2},{7,3},{8,4},{9,5},{1... | collective-permute-start | bytes 786440 | tf_op jit(solution)/shard_map/ppermute | solution.py:30
  54.4 6.5 %collective-permute-start.4 = (bf16[128,512]{1,0:T(8,128)(2,1)S(1)}, bf16[128,512]{1,0:T(8,128)(2,1)S(1)}, u32[]{:S(2)}, u32[]{:S(2)}) collective-permute-start(bf16[128,512]{1,0:T(8,128)(2,1)S(1)} %pick.1.refs_4_.refs_0_), channel_id=1, source_target_pairs={{0,1},{1,2},{2,3},{3,0},{4,5},{5,6},{6,7},{7,4},{8,9},{9,10},{10,1... | collective-permute-start | bytes 393224 | tf_op jit(solution)/shard_map/ppermute | solution.py:30
  54.5 6.4 %collective-permute-start.5 = (bf16[128,512]{1,0:T(8,128)(2,1)S(1)}, bf16[128,512]{1,0:T(8,128)(2,1)S(1)}, u32[]{:S(2)}, u32[]{:S(2)}) collective-permute-start(bf16[128,512]{1,0:T(8,128)(2,1)S(1)} %pick.1.refs_4_.refs_0_), channel_id=1, source_target_pairs={{0,2},{1,3},{2,0},{3,1},{4,6},{5,7},{6,4},{7,5},{8,10},{9,11},{10,... | collective-permute-start | bytes 393224 | tf_op jit(solution)/shard_map/ppermute | solution.py:30
  56.7 4.8 %collective-permute-start.6 = (bf16[128,512]{1,0:T(8,128)(2,1)S(1)}, bf16[128,512]{1,0:T(8,128)(2,1)S(1)}, u32[]{:S(2)}, u32[]{:S(2)}) collective-permute-start(bf16[128,512]{1,0:T(8,128)(2,1)S(1)} %pick.1.refs_4_.refs_0_), channel_id=1, source_target_pairs={{0,3},{1,0},{2,1},{3,2},{4,7},{5,4},{6,5},{7,6},{8,11},{9,8},{10,9... | collective-permute-start | bytes 393224 | tf_op jit(solution)/shard_map/ppermute | solution.py:30
  63.8 7.5 %collective-permute-start.14 = (bf16[8,128,512]{2,1,0:T(8,128)(2,1)S(1)}, bf16[8,128,512]{2,1,0:T(8,128)(2,1)S(1)}, u32[]{:S(2)}, u32[]{:S(2)}) collective-permute-start(bf16[8,128,512]{2,1,0:T(8,128)(2,1)S(1)} %get-tuple-element.36), channel_id=1, source_target_pairs={{0,32},{1,33},{2,34},{3,35},{4,36},{5,37},{6,38},{7,39},{8,40},{9,... | collective-permute-start | bytes 3145736 | tf_op jit(solution)/shard_map/ppermute | solution.py:30
  69.0 4.9 %collective-permute-start.10 = (bf16[256,512]{1,0:T(8,128)(2,1)S(1)}, bf16[256,512]{1,0:T(8,128)(2,1)S(1)}, u32[]{:S(2)}, u32[]{:S(2)}) collective-permute-start(bf16[256,512]{1,0:T(8,128)(2,1)S(1)} %copy-done.1), channel_id=1, source_target_pairs={{0,32},{1,33},{2,34},{3,35},{4,36},{5,37},{6,38},{7,39},{8,40},{9,... | collective-permute-start | bytes 786440 | tf_op jit(solution)/shard_map/ppermute | solution.py:30
  69.1 5.3 %collective-permute-start.11 = (bf16[256,512]{1,0:T(8,128)(2,1)S(1)}, bf16[256,512]{1,0:T(8,128)(2,1)S(1)}, u32[]{:S(2)}, u32[]{:S(2)}) collective-permute-start(bf16[256,512]{1,0:T(8,128)(2,1)S(1)} %collective-permute-done.7.refs_8_.refs_5_), channel_id=1, source_target_pairs={{0,32},{1,33},{2,34},{3,35},{4,36},{5,37},{6,38},{7,39},{8,40},{9,... | collective-permute-start | bytes 786440 | tf_op jit(solution)/shard_map/ppermute | solution.py:30
  69.5 5.1 %collective-permute-start.12 = (bf16[256,512]{1,0:T(8,128)(2,1)S(1)}, bf16[256,512]{1,0:T(8,128)(2,1)S(1)}, u32[]{:S(2)}, u32[]{:S(2)}) collective-permute-start(bf16[256,512]{1,0:T(8,128)(2,1)S(1)} %collective-permute-done.8.refs_9_.refs_6_), channel_id=1, source_target_pairs={{0,32},{1,33},{2,34},{3,35},{4,36},{5,37},{6,38},{7,39},{8,40},{9,... | collective-permute-start | bytes 786440 | tf_op jit(solution)/shard_map/ppermute | solution.py:30
  69.6 5.0 %collective-permute-start.13 = (bf16[256,512]{1,0:T(8,128)(2,1)S(1)}, bf16[256,512]{1,0:T(8,128)(2,1)S(1)}, u32[]{:S(2)}, u32[]{:S(2)}) collective-permute-start(bf16[256,512]{1,0:T(8,128)(2,1)S(1)} %collective-permute-done.9.refs_10_.refs_7_), channel_id=1, source_target_pairs={{0,32},{1,33},{2,34},{3,35},{4,36},{5,37},{6,38},{7,39},{8,40},{9,... | collective-permute-start | bytes 786440 | tf_op jit(solution)/shard_map/ppermute | solution.py:30
  72.3 14.1 %collective-permute-start.21 = (bf16[2,128,512]{2,1,0:T(8,128)(2,1)S(1)}, bf16[2,128,512]{2,1,0:T(8,128)(2,1)S(1)}, u32[]{:S(2)}, u32[]{:S(2)}) collective-permute-start(bf16[2,128,512]{2,1,0:T(8,128)(2,1)S(1)} %get-tuple-element.48), channel_id=1, source_target_pairs={{0,12},{1,13},{2,14},{3,15},{4,0},{5,1},{6,2},{7,3},{8,4},{9,5},{1... | collective-permute-start | bytes 786440 | tf_op jit(solution)/shard_map/ppermute | solution.py:30
  73.9 13.2 %collective-permute-start.22 = (bf16[2,128,512]{2,1,0:T(8,128)(2,1)S(1)}, bf16[2,128,512]{2,1,0:T(8,128)(2,1)S(1)}, u32[]{:S(2)}, u32[]{:S(2)}) collective-permute-start(bf16[2,128,512]{2,1,0:T(8,128)(2,1)S(1)} %get-tuple-element.49), channel_id=1, source_target_pairs={{0,8},{1,9},{2,10},{3,11},{4,12},{5,13},{6,14},{7,15},{8,0},{9,1},... | collective-permute-start | bytes 786440 | tf_op jit(solution)/shard_map/ppermute | solution.py:30
  74.4 14.9 %collective-permute-start.23 = (bf16[2,128,512]{2,1,0:T(8,128)(2,1)S(1)}, bf16[2,128,512]{2,1,0:T(8,128)(2,1)S(1)}, u32[]{:S(2)}, u32[]{:S(2)}) collective-permute-start(bf16[2,128,512]{2,1,0:T(8,128)(2,1)S(1)} %get-tuple-element.50), channel_id=1, source_target_pairs={{0,4},{1,5},{2,6},{3,7},{4,8},{5,9},{6,10},{7,11},{8,12},{9,13},{1... | collective-permute-start | bytes 786440 | tf_op jit(solution)/shard_map/ppermute | solution.py:30
  79.7 12.9 %collective-permute-start.18 = (bf16[128,512]{1,0:T(8,128)(2,1)}, bf16[128,512]{1,0:T(8,128)(2,1)S(1)}, u32[]{:S(2)}, u32[]{:S(2)}) collective-permute-start(bf16[128,512]{1,0:T(8,128)(2,1)} %get-tuple-element.45), channel_id=1, source_target_pairs={{0,3},{1,0},{2,1},{3,2},{4,7},{5,4},{6,5},{7,6},{8,11},{9,8},{10,9... | collective-permute-start | bytes 393224 | tf_op jit(solution)/shard_map/ppermute | solution.py:30
  82.0 12.4 %collective-permute-start.19 = (bf16[128,512]{1,0:T(8,128)(2,1)}, bf16[128,512]{1,0:T(8,128)(2,1)S(1)}, u32[]{:S(2)}, u32[]{:S(2)}) collective-permute-start(bf16[128,512]{1,0:T(8,128)(2,1)} %get-tuple-element.46), channel_id=1, source_target_pairs={{0,2},{1,3},{2,0},{3,1},{4,6},{5,7},{6,4},{7,5},{8,10},{9,11},{10,... | collective-permute-start | bytes 393224 | tf_op jit(solution)/shard_map/ppermute | solution.py:30
  86.4 8.0 %collective-permute-start.20 = (bf16[128,512]{1,0:T(8,128)(2,1)S(1)}, bf16[128,512]{1,0:T(8,128)(2,1)S(1)}, u32[]{:S(2)}, u32[]{:S(2)}) collective-permute-start(bf16[128,512]{1,0:T(8,128)(2,1)S(1)} %copy-done.29), channel_id=1, source_target_pairs={{0,1},{1,2},{2,3},{3,0},{4,5},{5,6},{6,7},{7,4},{8,9},{9,10},{10,1... | collective-permute-start | bytes 393224 | tf_op jit(solution)/shard_map/ppermute | solution.py:30
  90.1 5.9 %collective-permute-start.24 = (bf16[128,512]{1,0:T(8,128)(2,1)S(1)}, bf16[128,512]{1,0:T(8,128)(2,1)S(1)}, u32[]{:S(2)}, u32[]{:S(2)}) collective-permute-start(bf16[128,512]{1,0:T(8,128)(2,1)S(1)} %get-tuple-element.53), channel_id=1, source_target_pairs={{0,208},{1,209},{2,210},{3,211},{4,212},{5,213},{6,214},{7,215},{8... | collective-permute-start | bytes 393224 | tf_op jit(solution)/shard_map/ppermute | solution.py:30
  90.6 33.0 %collective-permute-start.15 = (bf16[128,2048]{1,0:T(8,128)(2,1)}, bf16[128,2048]{1,0:T(8,128)(2,1)S(1)}, u32[]{:S(2)}, u32[]{:S(2)}) collective-permute-start(bf16[128,2048]{1,0:T(8,128)(2,1)} %get-tuple-element.39), channel_id=1, source_target_pairs={{0,3},{1,0},{2,1},{3,2},{4,7},{5,4},{6,5},{7,6},{8,11},{9,8},{10,9... | collective-permute-start | bytes 1572872 | tf_op jit(solution)/shard_map/ppermute | solution.py:30
  92.6 31.0 %collective-permute-start.16 = (bf16[128,2048]{1,0:T(8,128)(2,1)}, bf16[128,2048]{1,0:T(8,128)(2,1)S(1)}, u32[]{:S(2)}, u32[]{:S(2)}) collective-permute-start(bf16[128,2048]{1,0:T(8,128)(2,1)} %get-tuple-element.40), channel_id=1, source_target_pairs={{0,2},{1,3},{2,0},{3,1},{4,6},{5,7},{6,4},{7,5},{8,10},{9,11},{10,... | collective-permute-start | bytes 1572872 | tf_op jit(solution)/shard_map/ppermute | solution.py:30
  94.4 29.3 %collective-permute-start.17 = (bf16[128,2048]{1,0:T(8,128)(2,1)}, bf16[128,2048]{1,0:T(8,128)(2,1)S(1)}, u32[]{:S(2)}, u32[]{:S(2)}) collective-permute-start(bf16[128,2048]{1,0:T(8,128)(2,1)} %get-tuple-element.41), channel_id=1, source_target_pairs={{0,1},{1,2},{2,3},{3,0},{4,5},{5,6},{6,7},{7,4},{8,9},{9,10},{10,1... | collective-permute-start | bytes 1572872 | tf_op jit(solution)/shard_map/ppermute | solution.py:30
  97.0 31.9 %all-to-all-start.2 = ((bf16[32,8,512]{2,1,0:T(8,128)(2,1)}), bf16[32,8,512]{2,1,0:T(8,128)(2,1)S(1)}, u32[]{:S(2)}, u32[]{:S(2)}) async-start(bf16[32,8,512]{2,1,0:T(8,128)(2,1)} %bitcast.3), calls=%async_computation.2 | async-start | bytes 524288 | tf_op jit(solution)/shard_map/all_to_all | solution.py:419
  104.1 6.9 %collective-permute-start.25 = (bf16[128,512]{1,0:T(8,128)(2,1)S(1)}, bf16[128,512]{1,0:T(8,128)(2,1)S(1)}, u32[]{:S(2)}, u32[]{:S(2)}) collective-permute-start(bf16[128,512]{1,0:T(8,128)(2,1)S(1)} %mirror_sum.1.after.refs_0_), channel_id=1, source_target_pairs={{0,64},{1,65},{2,66},{3,67},{4,68},{5,69},{6,70},{7,71},{8,72},{9,... | collective-permute-start | bytes 393224 | tf_op jit(solution)/shard_map/ppermute | solution.py:30
  111.1 8.3 %collective-permute-start.26 = (bf16[128,512]{1,0:T(8,128)(2,1)S(1)}, bf16[128,512]{1,0:T(8,128)(2,1)S(1)}, u32[]{:S(2)}, u32[]{:S(2)}) collective-permute-start(bf16[128,512]{1,0:T(8,128)(2,1)S(1)} %z_sum.2.refs_0_), channel_id=1, source_target_pairs={{0,128},{1,129},{2,130},{3,131},{4,132},{5,133},{6,134},{7,135},{8... | collective-permute-start | bytes 393224 | tf_op jit(solution)/shard_map/ppermute | solution.py:30
  119.5 8.7 %collective-permute-start.27 = (bf16[128,512]{1,0:T(8,128)(2,1)S(1)}, bf16[128,512]{1,0:T(8,128)(2,1)S(1)}, u32[]{:S(2)}, u32[]{:S(2)}) collective-permute-start(bf16[128,512]{1,0:T(8,128)(2,1)S(1)} %z_sum.3.mine), channel_id=1, source_target_pairs={{0,32},{1,33},{2,34},{3,35},{4,36},{5,37},{6,38},{7,39},{8,40},{9,... | collective-permute-start | bytes 393224 | tf_op jit(solution)/shard_map/ppermute | solution.py:30
  (29 other events, 237.0 us)

commit v4 on v3

--- a/solution.py
+++ b/solution.py
@@ -138,7 +138,7 @@
     rows, columns = full.shape
     out = [like((rows, columns // NY), full.dtype)] * NY
     scratch = (pltpu.VMEM(full.shape, full.dtype), pltpu.SemaphoreType.DMA((1,)))
-    return call(split_kernel, "split", out, full, after, ins=[ANY] * 2, scratch=scratch, mib=56)
+    return call(split_kernel, "split", out, full, after, ins=[ANY] * 2, scratch=scratch, mib=48)
 
 
 def join_kernel(p0, p1, p2, p3, full):
@@ -150,7 +150,7 @@
 
 def join(parts):
     rows, columns = parts[0].shape
-    return call(join_kernel, "join", [like((rows, columns * NY), parts[0].dtype)], *parts, mib=56)[0]
+    return call(join_kernel, "join", [like((rows, columns * NY), parts[0].dtype)], *parts, mib=48)[0]
 
 
 def heads(block, t):
@@ -238,7 +238,7 @@
         out_shape=[o for o, _ in outs],
         in_specs=ins,
         out_specs=[s for _, s in outs],
-        compiler_params=pltpu.CompilerParams(vmem_limit_bytes=56 * 1024 * 1024),
+        compiler_params=pltpu.CompilerParams(vmem_limit_bytes=48 * 1024 * 1024),
         cost_estimate=pl.CostEstimate(flops=flops, bytes_accessed=size, transcendentals=0),
         name=name,
     )(*args)
@@ -262,7 +262,7 @@
     scratch = (pltpu.VMEM((KVH, slots, GROUP * HD), BF16), pltpu.VMEM(keys.shape, BF16), sems)
     out = [like(folded_shape(slots), F32)]
     flops = 2 * queries.size * TILE
-    return call(scores_kernel, "scores", out, queries, keys, ins=[ANY] * 2, scratch=scratch, mib=56, flops=flops)[0]
+    return call(scores_kernel, "scores", out, queries, keys, ins=[ANY] * 2, scratch=scratch, mib=48, flops=flops)[0]
 
 
 def attention_probs(scores, masks, upstream, after):
@@ -273,7 +273,7 @@
     out = [like((slots, KVH * HD), BF16), like(scores.shape, F32)]
     flops = 2 * upstream.size * TILE
     ins = [ANY] * (3 + len(after))
-    return call(probs_kernel, "probs", out, scores, masks, upstream, *after, ins=ins, scratch=scratch, mib=56, flops=flops)
+    return call(probs_kernel, "probs", out, scores, masks, upstream, *after, ins=ins, scratch=scratch, mib=48, flops=flops)
 
 
 def attention_dscore(probs, values, upstream, queries, keys, after):
@@ -315,7 +315,7 @@
     out = [like((rows, width), F32)] + [like((rows, width), BF16)] * (NY - 1)
     flops = 2 * NY * pieces[0].size * width
     ins, scratch = [ANY] * (NY + SLICES + 1), staged(pieces, weights)
-    return call(partial_kernel, "partial_values", out, *pieces, *weights, after, ins=ins, scratch=scratch, mib=56, flops=flops)
+    return call(partial_kernel, "partial_values", out, *pieces, *weights, after, ins=ins, scratch=scratch, mib=48, flops=flops)
 
 
 def place_kernel(slot, own, a, b, c, after, out):
@@ -352,7 +352,7 @@
     flops = 2 * NY * rows * width * columns
     ins, scratch = [ANY] * (NY + SLICES + 1), staged(grads, weights)
     out = [like((rows, columns), BF16)] * NY + [TOKEN]
-    return call(back_kernel, "back", out, *grads, *weights, after, ins=ins, scratch=scratch, mib=56, flops=flops)
+    return call(back_kernel, "back", out, *grads, *weights, after, ins=ins, scratch=scratch, mib=48, flops=flops)
 
 
 def share_kernel(*refs):

time: 137 us -> 138 us (level)
  Pallas kernels: 34.1 us -> 26.4 us
  local copies, waits for them, and re-layouts: 5.55 us -> 12.1 us
  waiting for transfers between devices: 27.2 us -> 33.6 us
  starting transfers between devices: 68.1 us -> 64.2 us
    pallas_call x17, Pallas kernels: 27.7 us -> 20.4 us  [call(): pl.pallas_call(kernel, out_shape=out, in_specs=[VMEM] * len(args) if ins...]
    unnamed x60 -> x40, local copies, waits for them, and re-layouts: 5.55 us -> 12.1 us
    ppermute x28, waiting for transfers between devices: 20.4 us -> 26.4 us  [permute(): return lax.ppermute(array, AXES, pairs)]
    ppermute x28, starting transfers between devices: 43.6 us -> 38.2 us  [permute(): return lax.ppermute(array, AXES, pairs)]
    all_to_all x3, starting transfers between devices: 24.5 us -> 26.1 us  [exchange(): lax.all_to_all(buffer, 'fsdp', split_axis=0, concat_axis=0, tiled=True)]
  transfers between devices with their start and end apart: 31 -> 31, of which waited for: 10 -> 9; matrix products, arithmetic and copies ran while one was open for 0% -> 0% of each run, Pallas kernels for 19% -> 13%
where the time goes in v4:
time: 138 us; the launch traced here: 137 us
  starting transfers between devices  64.2 us (47%)
  waiting for transfers between devices  33.6 us (24%)
  Pallas kernels  26.4 us (19%)
  local copies, waits for them, and re-layouts  12.1 us (9%)
    ppermute x28, starting transfers between devices, permute(): return lax.ppermute(array, AXES, pairs)  38.2 us
    ppermute x28, waiting for transfers between devices, permute(): return lax.ppermute(array, AXES, pairs)  26.4 us
    all_to_all x3, starting transfers between devices, exchange(): lax.all_to_all(buffer, 'fsdp', split_axis=0, concat_axis=0, tiled=True)  26.1 us
    pallas_call x17, Pallas kernels, call(): pl.pallas_call(kernel, out_shape=out, in_specs=[VMEM] * len(args) if ins...  20.4 us
    unnamed x40, local copies, waits for them, and re-layouts  12.1 us
    all_to_all x3, waiting for transfers between devices, exchange(): lax.all_to_all(buffer, 'fsdp', split_axis=0, concat_axis=0, tiled=True)  7.16 us
    pallas_call x1, Pallas kernels, per_head(): pl.pallas_call(kernel, grid=(KVH,), out_shape=[o for o, _ in outs], in_sp...  6.03 us
  transfers between devices with their start and end apart: 31, of which 9 were waited for; matrix products, arithmetic and copies ran while one was open for 0% of the time, Pallas kernels for 13%

profile of v4, /device:TPU:1, one launch (start us, length us, event | category | flops | bytes accessed | tf_op | source)
XLA Modules:
  0.0 137.2 jit_solution(11010547599651751073)
XLA Ops:
  0.6 6.5 %collective-permute-start = (bf16[256,512]{1,0:T(8,128)(2,1)}, bf16[256,512]{1,0:T(8,128)(2,1)}, u32[]{:S(2)}, u32[]{:S(2)}) collective-permute-start(bf16[256,512]{1,0:T(8,128)(2,1)} %a.1), channel_id=1, source_target_pairs={{0,208},{1,209},{2,210},{3,211},{4,212},{5,213},{6,214},{7,215},{8... | collective-permute-start | bytes 786440 | tf_op jit(solution)/shard_map/ppermute | solution.py:30
  7.1 1.4 %masks.1.after = s32[32,8,128]{2,1,0:T(8,128)} custom-call(s32[128]{0:T(128)} %slots_in.1, s32[128]{0:T(128)} %ids_in.1), custom_call_target="tpu_custom_call" | custom-call | bytes 132096 | tf_op jit(solution)/shard_map/masks/pallas_call | solution.py:55
  8.6 8.3 %all-to-all-start = ((s32[32,8,128]{2,1,0:T(8,128)}), s32[32,8,128]{2,1,0:T(8,128)S(1)}, u32[]{:S(2)}, u32[]{:S(2)}) async-start(s32[32,8,128]{2,1,0:T(8,128)} %masks.1.after), calls=%async_computation | async-start | bytes 262144 | tf_op jit(solution)/shard_map/all_to_all | solution.py:419
  16.8 1.6 %copy-done.3 = bf16[128,8192]{1,0:T(8,128)(2,1)S(1)} copy-done((bf16[128,8192]{1,0:T(8,128)(2,1)S(1)}, bf16[128,8192]{1,0:T(8,128)(2,1)}, u32[]{:S(2)}) %copy-start.3) | copy-done | bytes 2097176
  19.3 1.7 %split.1 = (bf16[128,2048]{1,0:T(8,128)(2,1)S(1)}, bf16[128,2048]{1,0:T(8,128)(2,1)}, bf16[128,2048]{1,0:T(8,128)(2,1)}, bf16[128,2048]{1,0:T(8,128)(2,1)}) custom-call(bf16[128,8192]{1,0:T(8,128)(2,1)S(1)} %copy-done.3, s32[32,8,128]{2,1,0:T(8,128)S(1)} %copy-done.7), custom_call_target="tpu_custom_call" | custom-call | bytes 4325376 | tf_op jit(solution)/shard_map/split/pallas_call | solution.py:55
  21.1 1.3 collective-permute-start.1
  22.4 2.4 %collective-permute-start.2 = (bf16[128,2048]{1,0:T(8,128)(2,1)}, bf16[128,2048]{1,0:T(8,128)(2,1)S(1)}, u32[]{:S(2)}, u32[]{:S(2)}) collective-permute-start(bf16[128,2048]{1,0:T(8,128)(2,1)} %get-tuple-element.32), channel_id=1, source_target_pairs={{0,2},{1,3},{2,0},{3,1},{4,6},{5,7},{6,4},{7,5},{8,10},{9,11},{10,... | collective-permute-start | bytes 1572872 | tf_op jit(solution)/shard_map/ppermute | solution.py:30
  26.0 1.5 %scores.1.scores_in = f32[4,2,8,1024]{3,2,1,0:T(8,128)S(1)} custom-call(bf16[256,4096]{1,0:T(8,128)(2,1)S(1)} %copy-done, bf16[256,512]{1,0:T(8,128)(2,1)S(1)} %copy-done.8), custom_call_target="tpu_custom_call" | custom-call | flops 268435456 | bytes 2621440 | tf_op jit(solution)/shard_map/scores/pallas_call | solution.py:55
  29.2 1.6 %copy-done.1 = bf16[256,4096]{1,0:T(8,128)(2,1)S(1)} copy-done((bf16[256,4096]{1,0:T(8,128)(2,1)S(1)}, bf16[256,4096]{1,0:T(8,128)(2,1)}, u32[]{:S(2)}) %copy-start.1) | copy-done | bytes 2097176
  31.7 2.4 %probs.1 = (bf16[256,512]{1,0:T(8,128)(2,1)}, f32[4,2,8,1024]{3,2,1,0:T(8,128)S(1)}) custom-call(f32[4,2,8,1024]{3,2,1,0:T(8,128)S(1)} %copy-done.11, s32[32,8,128]{2,1,0:T(8,128)S(1)} %all-to-all-done.masks_in, bf16[256,4096]{1,0:T(8,128)(2,1)S(1)} %copy-done.1, bf16[256,512]{1,0:T(8,128)(2,1)S(1)} %pair.1.rest_0_.refs_4_), custom_call_target="tpu_custom_call" | custom-call | flops 268435456 | bytes 3276800 | tf_op jit(solution)/shard_map/probs/pallas_call | solution.py:55
  34.8 9.2 %all-to-all-start.1 = ((bf16[32,8,512]{2,1,0:T(8,128)(2,1)}), bf16[32,8,512]{2,1,0:T(8,128)(2,1)S(1)}, u32[]{:S(2)}, u32[]{:S(2)}) async-start(bf16[32,8,512]{2,1,0:T(8,128)(2,1)} %bitcast.1), calls=%async_computation.1 | async-start | bytes 524288 | tf_op jit(solution)/shard_map/all_to_all | solution.py:419
  44.1 1.3 collective-permute-start.7
  45.4 2.4 %collective-permute-start.8 = (bf16[256,512]{1,0:T(8,128)(2,1)S(1)}, bf16[256,512]{1,0:T(8,128)(2,1)S(1)}, u32[]{:S(2)}, u32[]{:S(2)}) collective-permute-start(bf16[256,512]{1,0:T(8,128)(2,1)S(1)} %pair.1.rest_0_.refs_4_), channel_id=1, source_target_pairs={{0,8},{1,9},{2,10},{3,11},{4,12},{5,13},{6,14},{7,15},{8,0},{9,1},... | collective-permute-start | bytes 786440 | tf_op jit(solution)/shard_map/ppermute | solution.py:30
  49.0 7.2 %all-to-all-done.1 = bf16[32,8,512]{2,1,0:T(8,128)(2,1)S(1)} async-done(((bf16[32,8,512]{2,1,0:T(8,128)(2,1)}), bf16[32,8,512]{2,1,0:T(8,128)(2,1)S(1)}, u32[]{:S(2)}, u32[]{:S(2)}) %all-to-all-start.1) | async-done | bytes 262176 | tf_op jit(solution)/shard_map/all_to_all | solution.py:419
  56.4 2.2 %collective-permute-start.5 = (bf16[128,512]{1,0:T(8,128)(2,1)S(1)}, bf16[128,512]{1,0:T(8,128)(2,1)S(1)}, u32[]{:S(2)}, u32[]{:S(2)}) collective-permute-start(bf16[128,512]{1,0:T(8,128)(2,1)S(1)} %pick.1.refs_4_.refs_0_), channel_id=1, source_target_pairs={{0,2},{1,3},{2,0},{3,1},{4,6},{5,7},{6,4},{7,5},{8,10},{9,11},{10,... | collective-permute-start | bytes 393224 | tf_op jit(solution)/shard_map/ppermute | solution.py:30
  60.4 2.5 %collective-permute-done.4.refs_5_.refs_1_ = bf16[128,512]{1,0:T(8,128)(2,1)S(1)} collective-permute-done((bf16[128,512]{1,0:T(8,128)(2,1)S(1)}, bf16[128,512]{1,0:T(8,128)(2,1)S(1)}, u32[]{:S(2)}, u32[]{:S(2)}) %collective-permute-start.4) | collective-permute-done | bytes 131104 | tf_op jit(solution)/shard_map/ppermute | solution.py:30
  63.4 2.5 %shares.1 = (f32[8,128,512]{2,1,0:T(8,128)S(1)}, bf16[8,128,512]{2,1,0:T(8,128)(2,1)S(1)}, f32[8,128]{1,0:T(8,128)S(1)}) custom-call(bf16[128,2048]{1,0:T(8,128)(2,1)S(1)} %copy-done.13, bf16[128,2048]{1,0:T(8,128)(2,1)S(1)} %collective-permute-done.1.refs_2_.refs_1_, bf16[128,2048]{1,0:T(8,128)(2,1)S(1)} %collective-permute-done.2.refs_3_.refs_2_, ...), custom_call_target="tpu_custom_call" | custom-call | flops 1073741824 | bytes 6557696 | tf_op jit(solution)/shard_map/shares/pallas_call | solution.py:55
  66.0 5.3 %collective-permute-start.14 = (bf16[8,128,512]{2,1,0:T(8,128)(2,1)S(1)}, bf16[8,128,512]{2,1,0:T(8,128)(2,1)S(1)}, u32[]{:S(2)}, u32[]{:S(2)}) collective-permute-start(bf16[8,128,512]{2,1,0:T(8,128)(2,1)S(1)} %get-tuple-element.36), channel_id=1, source_target_pairs={{0,32},{1,33},{2,34},{3,35},{4,36},{5,37},{6,38},{7,39},{8,40},{9,... | collective-permute-start | bytes 3145736 | tf_op jit(solution)/shard_map/ppermute | solution.py:30
  72.3 1.3 collective-permute-done.14.got
  73.7 1.5 %collective-permute-start.21 = (bf16[2,128,512]{2,1,0:T(8,128)(2,1)S(1)}, bf16[2,128,512]{2,1,0:T(8,128)(2,1)S(1)}, u32[]{:S(2)}, u32[]{:S(2)}) collective-permute-start(bf16[2,128,512]{2,1,0:T(8,128)(2,1)S(1)} %get-tuple-element.48), channel_id=1, source_target_pairs={{0,12},{1,13},{2,14},{3,15},{4,0},{5,1},{6,2},{7,3},{8,4},{9,5},{1... | collective-permute-start | bytes 786440 | tf_op jit(solution)/shard_map/ppermute | solution.py:30
  75.9 2.5 %partial_values.1 = (f32[128,512]{1,0:T(8,128)S(1)}, bf16[128,512]{1,0:T(8,128)(2,1)S(1)}, bf16[128,512]{1,0:T(8,128)(2,1)S(1)}, bf16[128,512]{1,0:T(8,128)(2,1)S(1)}) custom-call(bf16[128,2048]{1,0:T(8,128)(2,1)S(1)} %copy-done.13, bf16[128,2048]{1,0:T(8,128)(2,1)S(1)} %collective-permute-done.1.refs_2_.refs_1_, ...), custom_call_target="tpu_custom_call" | custom-call | flops 1073741824 | bytes 4853760 | tf_op jit(solution)/shard_map/partial_values/pallas_call | solution.py:55
  78.4 2.5 %collective-permute-start.18 = (bf16[128,512]{1,0:T(8,128)(2,1)S(1)}, bf16[128,512]{1,0:T(8,128)(2,1)S(1)}, u32[]{:S(2)}, u32[]{:S(2)}) collective-permute-start(bf16[128,512]{1,0:T(8,128)(2,1)S(1)} %get-tuple-element.45), channel_id=1, source_target_pairs={{0,3},{1,0},{2,1},{3,2},{4,7},{5,4},{6,5},{7,6},{8,11},{9,8},{10,9... | collective-permute-start | bytes 393224 | tf_op jit(solution)/shard_map/ppermute | solution.py:30
  80.9 3.2 %back.1 = (bf16[128,2048]{1,0:T(8,128)(2,1)S(1)}, bf16[128,2048]{1,0:T(8,128)(2,1)}, bf16[128,2048]{1,0:T(8,128)(2,1)}, bf16[128,2048]{1,0:T(8,128)(2,1)S(1)}, f32[8,128]{1,0:T(8,128)S(1)}) custom-call(bf16[128,512]{1,0:T(8,128)(2,1)S(1)} %pick.1.refs_4_.refs_0_, bf16[128,512]{1,0:T(8,128)(2,1)S(1)} %collective-permute-done.4.refs_5_.refs_1_, ...), custom_call_target="tpu_custom_call" | custom-call | flops 1073741824 | bytes 5246976 | tf_op jit(solution)/shard_map/back/pallas_call | solution.py:55
  85.6 5.0 %collective-permute-done.23.c = bf16[2,128,512]{2,1,0:T(8,128)(2,1)S(1)} collective-permute-done((bf16[2,128,512]{2,1,0:T(8,128)(2,1)S(1)}, bf16[2,128,512]{2,1,0:T(8,128)(2,1)S(1)}, u32[]{:S(2)}, u32[]{:S(2)}) %collective-permute-start.23) | collective-permute-done | bytes 262176 | tf_op jit(solution)/shard_map/ppermute | solution.py:30
  91.2 2.2 %collective-permute-start.15 = (bf16[128,2048]{1,0:T(8,128)(2,1)}, bf16[128,2048]{1,0:T(8,128)(2,1)S(1)}, u32[]{:S(2)}, u32[]{:S(2)}) collective-permute-start(bf16[128,2048]{1,0:T(8,128)(2,1)} %get-tuple-element.39), channel_id=1, source_target_pairs={{0,3},{1,0},{2,1},{3,2},{4,7},{5,4},{6,5},{7,6},{8,11},{9,8},{10,9... | collective-permute-start | bytes 1572872 | tf_op jit(solution)/shard_map/ppermute | solution.py:30
  94.0 2.6 %collective-permute-done.24.refs_1_ = bf16[128,512]{1,0:T(8,128)(2,1)S(1)} collective-permute-done((bf16[128,512]{1,0:T(8,128)(2,1)S(1)}, bf16[128,512]{1,0:T(8,128)(2,1)S(1)}, u32[]{:S(2)}, u32[]{:S(2)}) %collective-permute-start.24) | collective-permute-done | bytes 131104 | tf_op jit(solution)/shard_map/ppermute | solution.py:30
  97.6 8.6 %all-to-all-start.2 = ((bf16[32,8,512]{2,1,0:T(8,128)(2,1)}), bf16[32,8,512]{2,1,0:T(8,128)(2,1)}, u32[]{:S(2)}, u32[]{:S(2)}) async-start(bf16[32,8,512]{2,1,0:T(8,128)(2,1)} %bitcast.3), calls=%async_computation.2 | async-start | bytes 524288 | tf_op jit(solution)/shard_map/all_to_all | solution.py:419
  106.3 7.3 %collective-permute-done.25.refs_1_ = bf16[128,512]{1,0:T(8,128)(2,1)S(1)} collective-permute-done((bf16[128,512]{1,0:T(8,128)(2,1)S(1)}, bf16[128,512]{1,0:T(8,128)(2,1)S(1)}, u32[]{:S(2)}, u32[]{:S(2)}) %collective-permute-start.25) | collective-permute-done | bytes 131104 | tf_op jit(solution)/shard_map/ppermute | solution.py:30
  113.7 6.4 %collective-permute-done.26.refs_1_ = bf16[128,512]{1,0:T(8,128)(2,1)S(1)} collective-permute-done((bf16[128,512]{1,0:T(8,128)(2,1)S(1)}, bf16[128,512]{1,0:T(8,128)(2,1)S(1)}, u32[]{:S(2)}, u32[]{:S(2)}) %collective-permute-start.26) | collective-permute-done | bytes 131104 | tf_op jit(solution)/shard_map/ppermute | solution.py:30
  120.2 3.5 %collective-permute-start.27 = (bf16[128,512]{1,0:T(8,128)(2,1)S(1)}, bf16[128,512]{1,0:T(8,128)(2,1)S(1)}, u32[]{:S(2)}, u32[]{:S(2)}) collective-permute-start(bf16[128,512]{1,0:T(8,128)(2,1)S(1)} %z_sum.3.mine), channel_id=1, source_target_pairs={{0,32},{1,33},{2,34},{3,35},{4,36},{5,37},{6,38},{7,39},{8,40},{9,... | collective-permute-start | bytes 393224 | tf_op jit(solution)/shard_map/ppermute | solution.py:30
  126.6 1.8 %join.1 = bf16[128,8192]{1,0:T(8,128)(2,1)} custom-call(bf16[128,2048]{1,0:T(8,128)(2,1)S(1)} %copy-done.15, bf16[128,2048]{1,0:T(8,128)(2,1)S(1)} %collective-permute-done.15.p1.rest_0_, bf16[128,2048]{1,0:T(8,128)(2,1)S(1)} %collective-permute-done.16.p2.rest_1_, bf16[128,2048]{1,0:T(8,128)(2,1)S(1)} %copy-done.5), custom_call_target="tpu_custom_call" | custom-call | bytes 4194304 | tf_op jit(solution)/shard_map/join/pallas_call | solution.py:55
  131.1 6.0 %dscore.1 = (bf16[256,4096]{1,0:T(8,128)(2,1)}, bf16[256,512]{1,0:T(8,128)(2,1)}) custom-call(f32[4,2,8,1024]{3,2,1,0:T(8,128)S(1)} %copy-done.18, bf16[256,512]{1,0:T(8,128)(2,1)} %bitcast.4.values, bf16[256,4096]{1,0:T(8,128)(2,1)S(1)} %copy-done.2, bf16[256,4096]{1,0:T(8,128)(2,1)} %queries.3, bf16[256,512]{1,0:T(8,128)(2,1)S(1)} %copy-done.9, ...), custom_call_target="tpu_custom_call" | custom-call | flops 805306368 | bytes 8912896 | tf_op jit(solution)/shard_map/dscore/pallas_call | solution.py:235
  (88 shorter events, 20.7 us)
Async XLA Ops:
  0.6 27.5 %collective-permute-start = (bf16[256,512]{1,0:T(8,128)(2,1)}, bf16[256,512]{1,0:T(8,128)(2,1)}, u32[]{:S(2)}, u32[]{:S(2)}) collective-permute-start(bf16[256,512]{1,0:T(8,128)(2,1)} %a.1), channel_id=1, source_target_pairs={{0,208},{1,209},{2,210},{3,211},{4,212},{5,213},{6,214},{7,215},{8... | collective-permute-start | bytes 786440 | tf_op jit(solution)/shard_map/ppermute | solution.py:30
  8.6 20.6 %all-to-all-start = ((s32[32,8,128]{2,1,0:T(8,128)}), s32[32,8,128]{2,1,0:T(8,128)S(1)}, u32[]{:S(2)}, u32[]{:S(2)}) async-start(s32[32,8,128]{2,1,0:T(8,128)} %masks.1.after), calls=%async_computation | async-start | bytes 262144 | tf_op jit(solution)/shard_map/all_to_all | solution.py:419
  21.1 26.7 %collective-permute-start.1 = (bf16[128,2048]{1,0:T(8,128)(2,1)}, bf16[128,2048]{1,0:T(8,128)(2,1)S(1)}, u32[]{:S(2)}, u32[]{:S(2)}) collective-permute-start(bf16[128,2048]{1,0:T(8,128)(2,1)} %get-tuple-element.31), channel_id=1, source_target_pairs={{0,1},{1,2},{2,3},{3,0},{4,5},{5,6},{6,7},{7,4},{8,9},{9,10},{10,1... | collective-permute-start | bytes 1572872 | tf_op jit(solution)/shard_map/ppermute | solution.py:30
  22.4 26.6 %collective-permute-start.2 = (bf16[128,2048]{1,0:T(8,128)(2,1)}, bf16[128,2048]{1,0:T(8,128)(2,1)S(1)}, u32[]{:S(2)}, u32[]{:S(2)}) collective-permute-start(bf16[128,2048]{1,0:T(8,128)(2,1)} %get-tuple-element.32), channel_id=1, source_target_pairs={{0,2},{1,3},{2,0},{3,1},{4,6},{5,7},{6,4},{7,5},{8,10},{9,11},{10,... | collective-permute-start | bytes 1572872 | tf_op jit(solution)/shard_map/ppermute | solution.py:30
  24.8 24.2 %collective-permute-start.3 = (bf16[128,2048]{1,0:T(8,128)(2,1)}, bf16[128,2048]{1,0:T(8,128)(2,1)}, u32[]{:S(2)}, u32[]{:S(2)}) collective-permute-start(bf16[128,2048]{1,0:T(8,128)(2,1)} %get-tuple-element.33), channel_id=1, source_target_pairs={{0,3},{1,0},{2,1},{3,2},{4,7},{5,4},{6,5},{7,6},{8,11},{9,8},{10,9... | collective-permute-start | bytes 1572872 | tf_op jit(solution)/shard_map/ppermute | solution.py:30
  31.7 31.7 %copy-start.13 = (bf16[128,2048]{1,0:T(8,128)(2,1)S(1)}, bf16[128,2048]{1,0:T(8,128)(2,1)}, u32[]{:S(2)}) copy-start(bf16[128,2048]{1,0:T(8,128)(2,1)} %copy-done.12) | copy-start | bytes 1572868
  34.8 21.3 %all-to-all-start.1 = ((bf16[32,8,512]{2,1,0:T(8,128)(2,1)}), bf16[32,8,512]{2,1,0:T(8,128)(2,1)S(1)}, u32[]{:S(2)}, u32[]{:S(2)}) async-start(bf16[32,8,512]{2,1,0:T(8,128)(2,1)} %bitcast.1), calls=%async_computation.1 | async-start | bytes 524288 | tf_op jit(solution)/shard_map/all_to_all | solution.py:419
  44.1 14.6 %collective-permute-start.7 = (bf16[256,512]{1,0:T(8,128)(2,1)S(1)}, bf16[256,512]{1,0:T(8,128)(2,1)S(1)}, u32[]{:S(2)}, u32[]{:S(2)}) collective-permute-start(bf16[256,512]{1,0:T(8,128)(2,1)S(1)} %pair.1.rest_0_.refs_4_), channel_id=1, source_target_pairs={{0,4},{1,5},{2,6},{3,7},{4,8},{5,9},{6,10},{7,11},{8,12},{9,13},{1... | collective-permute-start | bytes 786440 | tf_op jit(solution)/shard_map/ppermute | solution.py:30
  45.4 14.3 %collective-permute-start.8 = (bf16[256,512]{1,0:T(8,128)(2,1)S(1)}, bf16[256,512]{1,0:T(8,128)(2,1)S(1)}, u32[]{:S(2)}, u32[]{:S(2)}) collective-permute-start(bf16[256,512]{1,0:T(8,128)(2,1)S(1)} %pair.1.rest_0_.refs_4_), channel_id=1, source_target_pairs={{0,8},{1,9},{2,10},{3,11},{4,12},{5,13},{6,14},{7,15},{8,0},{9,1},... | collective-permute-start | bytes 786440 | tf_op jit(solution)/shard_map/ppermute | solution.py:30
  47.8 12.6 %collective-permute-start.9 = (bf16[256,512]{1,0:T(8,128)(2,1)S(1)}, bf16[256,512]{1,0:T(8,128)(2,1)S(1)}, u32[]{:S(2)}, u32[]{:S(2)}) collective-permute-start(bf16[256,512]{1,0:T(8,128)(2,1)S(1)} %pair.1.rest_0_.refs_4_), channel_id=1, source_target_pairs={{0,12},{1,13},{2,14},{3,15},{4,0},{5,1},{6,2},{7,3},{8,4},{9,5},{1... | collective-permute-start | bytes 786440 | tf_op jit(solution)/shard_map/ppermute | solution.py:30
  56.4 6.5 %collective-permute-start.4 = (bf16[128,512]{1,0:T(8,128)(2,1)S(1)}, bf16[128,512]{1,0:T(8,128)(2,1)S(1)}, u32[]{:S(2)}, u32[]{:S(2)}) collective-permute-start(bf16[128,512]{1,0:T(8,128)(2,1)S(1)} %pick.1.refs_4_.refs_0_), channel_id=1, source_target_pairs={{0,1},{1,2},{2,3},{3,0},{4,5},{5,6},{6,7},{7,4},{8,9},{9,10},{10,1... | collective-permute-start | bytes 393224 | tf_op jit(solution)/shard_map/ppermute | solution.py:30
  56.4 6.4 %collective-permute-start.5 = (bf16[128,512]{1,0:T(8,128)(2,1)S(1)}, bf16[128,512]{1,0:T(8,128)(2,1)S(1)}, u32[]{:S(2)}, u32[]{:S(2)}) collective-permute-start(bf16[128,512]{1,0:T(8,128)(2,1)S(1)} %pick.1.refs_4_.refs_0_), channel_id=1, source_target_pairs={{0,2},{1,3},{2,0},{3,1},{4,6},{5,7},{6,4},{7,5},{8,10},{9,11},{10,... | collective-permute-start | bytes 393224 | tf_op jit(solution)/shard_map/ppermute | solution.py:30
  58.7 4.8 %collective-permute-start.6 = (bf16[128,512]{1,0:T(8,128)(2,1)S(1)}, bf16[128,512]{1,0:T(8,128)(2,1)S(1)}, u32[]{:S(2)}, u32[]{:S(2)}) collective-permute-start(bf16[128,512]{1,0:T(8,128)(2,1)S(1)} %pick.1.refs_4_.refs_0_), channel_id=1, source_target_pairs={{0,3},{1,0},{2,1},{3,2},{4,7},{5,4},{6,5},{7,6},{8,11},{9,8},{10,9... | collective-permute-start | bytes 393224 | tf_op jit(solution)/shard_map/ppermute | solution.py:30
  66.0 7.6 %collective-permute-start.14 = (bf16[8,128,512]{2,1,0:T(8,128)(2,1)S(1)}, bf16[8,128,512]{2,1,0:T(8,128)(2,1)S(1)}, u32[]{:S(2)}, u32[]{:S(2)}) collective-permute-start(bf16[8,128,512]{2,1,0:T(8,128)(2,1)S(1)} %get-tuple-element.36), channel_id=1, source_target_pairs={{0,32},{1,33},{2,34},{3,35},{4,36},{5,37},{6,38},{7,39},{8,40},{9,... | collective-permute-start | bytes 3145736 | tf_op jit(solution)/shard_map/ppermute | solution.py:30
  71.3 3.9 %collective-permute-start.10 = (bf16[256,512]{1,0:T(8,128)(2,1)S(1)}, bf16[256,512]{1,0:T(8,128)(2,1)S(1)}, u32[]{:S(2)}, u32[]{:S(2)}) collective-permute-start(bf16[256,512]{1,0:T(8,128)(2,1)S(1)} %pair.1.rest_0_.refs_4_), channel_id=1, source_target_pairs={{0,32},{1,33},{2,34},{3,35},{4,36},{5,37},{6,38},{7,39},{8,40},{9,... | collective-permute-start | bytes 786440 | tf_op jit(solution)/shard_map/ppermute | solution.py:30
  71.4 4.5 %collective-permute-start.11 = (bf16[256,512]{1,0:T(8,128)(2,1)S(1)}, bf16[256,512]{1,0:T(8,128)(2,1)S(1)}, u32[]{:S(2)}, u32[]{:S(2)}) collective-permute-start(bf16[256,512]{1,0:T(8,128)(2,1)S(1)} %collective-permute-done.7.refs_8_.refs_5_), channel_id=1, source_target_pairs={{0,32},{1,33},{2,34},{3,35},{4,36},{5,37},{6,38},{7,39},{8,40},{9,... | collective-permute-start | bytes 786440 | tf_op jit(solution)/shard_map/ppermute | solution.py:30
  71.8 4.1 %collective-permute-start.12 = (bf16[256,512]{1,0:T(8,128)(2,1)S(1)}, bf16[256,512]{1,0:T(8,128)(2,1)S(1)}, u32[]{:S(2)}, u32[]{:S(2)}) collective-permute-start(bf16[256,512]{1,0:T(8,128)(2,1)S(1)} %collective-permute-done.8.refs_9_.refs_6_), channel_id=1, source_target_pairs={{0,32},{1,33},{2,34},{3,35},{4,36},{5,37},{6,38},{7,39},{8,40},{9,... | collective-permute-start | bytes 786440 | tf_op jit(solution)/shard_map/ppermute | solution.py:30
  71.9 4.0 %collective-permute-start.13 = (bf16[256,512]{1,0:T(8,128)(2,1)S(1)}, bf16[256,512]{1,0:T(8,128)(2,1)S(1)}, u32[]{:S(2)}, u32[]{:S(2)}) collective-permute-start(bf16[256,512]{1,0:T(8,128)(2,1)S(1)} %collective-permute-done.9.refs_10_.refs_7_), channel_id=1, source_target_pairs={{0,32},{1,33},{2,34},{3,35},{4,36},{5,37},{6,38},{7,39},{8,40},{9,... | collective-permute-start | bytes 786440 | tf_op jit(solution)/shard_map/ppermute | solution.py:30
  73.7 11.2 %collective-permute-start.21 = (bf16[2,128,512]{2,1,0:T(8,128)(2,1)S(1)}, bf16[2,128,512]{2,1,0:T(8,128)(2,1)S(1)}, u32[]{:S(2)}, u32[]{:S(2)}) collective-permute-start(bf16[2,128,512]{2,1,0:T(8,128)(2,1)S(1)} %get-tuple-element.48), channel_id=1, source_target_pairs={{0,12},{1,13},{2,14},{3,15},{4,0},{5,1},{6,2},{7,3},{8,4},{9,5},{1... | collective-permute-start | bytes 786440 | tf_op jit(solution)/shard_map/ppermute | solution.py:30
  75.2 10.4 %collective-permute-start.22 = (bf16[2,128,512]{2,1,0:T(8,128)(2,1)S(1)}, bf16[2,128,512]{2,1,0:T(8,128)(2,1)S(1)}, u32[]{:S(2)}, u32[]{:S(2)}) collective-permute-start(bf16[2,128,512]{2,1,0:T(8,128)(2,1)S(1)} %get-tuple-element.49), channel_id=1, source_target_pairs={{0,8},{1,9},{2,10},{3,11},{4,12},{5,13},{6,14},{7,15},{8,0},{9,1},... | collective-permute-start | bytes 786440 | tf_op jit(solution)/shard_map/ppermute | solution.py:30
  75.9 14.7 %collective-permute-start.23 = (bf16[2,128,512]{2,1,0:T(8,128)(2,1)S(1)}, bf16[2,128,512]{2,1,0:T(8,128)(2,1)S(1)}, u32[]{:S(2)}, u32[]{:S(2)}) collective-permute-start(bf16[2,128,512]{2,1,0:T(8,128)(2,1)S(1)} %get-tuple-element.50), channel_id=1, source_target_pairs={{0,4},{1,5},{2,6},{3,7},{4,8},{5,9},{6,10},{7,11},{8,12},{9,13},{1... | collective-permute-start | bytes 786440 | tf_op jit(solution)/shard_map/ppermute | solution.py:30
  78.4 14.9 %collective-permute-start.18 = (bf16[128,512]{1,0:T(8,128)(2,1)S(1)}, bf16[128,512]{1,0:T(8,128)(2,1)S(1)}, u32[]{:S(2)}, u32[]{:S(2)}) collective-permute-start(bf16[128,512]{1,0:T(8,128)(2,1)S(1)} %get-tuple-element.45), channel_id=1, source_target_pairs={{0,3},{1,0},{2,1},{3,2},{4,7},{5,4},{6,5},{7,6},{8,11},{9,8},{10,9... | collective-permute-start | bytes 393224 | tf_op jit(solution)/shard_map/ppermute | solution.py:30
  80.9 12.5 %collective-permute-start.19 = (bf16[128,512]{1,0:T(8,128)(2,1)S(1)}, bf16[128,512]{1,0:T(8,128)(2,1)S(1)}, u32[]{:S(2)}, u32[]{:S(2)}) collective-permute-start(bf16[128,512]{1,0:T(8,128)(2,1)S(1)} %get-tuple-element.46), channel_id=1, source_target_pairs={{0,2},{1,3},{2,0},{3,1},{4,6},{5,7},{6,4},{7,5},{8,10},{9,11},{10,... | collective-permute-start | bytes 393224 | tf_op jit(solution)/shard_map/ppermute | solution.py:30
  84.9 9.1 %collective-permute-start.20 = (bf16[128,512]{1,0:T(8,128)(2,1)S(1)}, bf16[128,512]{1,0:T(8,128)(2,1)S(1)}, u32[]{:S(2)}, u32[]{:S(2)}) collective-permute-start(bf16[128,512]{1,0:T(8,128)(2,1)S(1)} %get-tuple-element.47), channel_id=1, source_target_pairs={{0,1},{1,2},{2,3},{3,0},{4,5},{5,6},{6,7},{7,4},{8,9},{9,10},{10,1... | collective-permute-start | bytes 393224 | tf_op jit(solution)/shard_map/ppermute | solution.py:30
  90.7 5.9 %collective-permute-start.24 = (bf16[128,512]{1,0:T(8,128)(2,1)S(1)}, bf16[128,512]{1,0:T(8,128)(2,1)S(1)}, u32[]{:S(2)}, u32[]{:S(2)}) collective-permute-start(bf16[128,512]{1,0:T(8,128)(2,1)S(1)} %get-tuple-element.53), channel_id=1, source_target_pairs={{0,208},{1,209},{2,210},{3,211},{4,212},{5,213},{6,214},{7,215},{8... | collective-permute-start | bytes 393224 | tf_op jit(solution)/shard_map/ppermute | solution.py:30
  91.2 32.5 %collective-permute-start.15 = (bf16[128,2048]{1,0:T(8,128)(2,1)}, bf16[128,2048]{1,0:T(8,128)(2,1)S(1)}, u32[]{:S(2)}, u32[]{:S(2)}) collective-permute-start(bf16[128,2048]{1,0:T(8,128)(2,1)} %get-tuple-element.39), channel_id=1, source_target_pairs={{0,3},{1,0},{2,1},{3,2},{4,7},{5,4},{6,5},{7,6},{8,11},{9,8},{10,9... | collective-permute-start | bytes 1572872 | tf_op jit(solution)/shard_map/ppermute | solution.py:30
  93.3 30.3 %collective-permute-start.16 = (bf16[128,2048]{1,0:T(8,128)(2,1)}, bf16[128,2048]{1,0:T(8,128)(2,1)S(1)}, u32[]{:S(2)}, u32[]{:S(2)}) collective-permute-start(bf16[128,2048]{1,0:T(8,128)(2,1)} %get-tuple-element.40), channel_id=1, source_target_pairs={{0,2},{1,3},{2,0},{3,1},{4,6},{5,7},{6,4},{7,5},{8,10},{9,11},{10,... | collective-permute-start | bytes 1572872 | tf_op jit(solution)/shard_map/ppermute | solution.py:30
  93.4 30.3 %collective-permute-start.17 = (bf16[128,2048]{1,0:T(8,128)(2,1)S(1)}, bf16[128,2048]{1,0:T(8,128)(2,1)S(1)}, u32[]{:S(2)}, u32[]{:S(2)}) collective-permute-start(bf16[128,2048]{1,0:T(8,128)(2,1)S(1)} %get-tuple-element.41), channel_id=1, source_target_pairs={{0,1},{1,2},{2,3},{3,0},{4,5},{5,6},{6,7},{7,4},{8,9},{9,10},{10,1... | collective-permute-start | bytes 1572872 | tf_op jit(solution)/shard_map/ppermute | solution.py:30
  97.6 31.6 %all-to-all-start.2 = ((bf16[32,8,512]{2,1,0:T(8,128)(2,1)}), bf16[32,8,512]{2,1,0:T(8,128)(2,1)}, u32[]{:S(2)}, u32[]{:S(2)}) async-start(bf16[32,8,512]{2,1,0:T(8,128)(2,1)} %bitcast.3), calls=%async_computation.2 | async-start | bytes 524288 | tf_op jit(solution)/shard_map/all_to_all | solution.py:419
  106.1 7.4 %collective-permute-start.25 = (bf16[128,512]{1,0:T(8,128)(2,1)S(1)}, bf16[128,512]{1,0:T(8,128)(2,1)S(1)}, u32[]{:S(2)}, u32[]{:S(2)}) collective-permute-start(bf16[128,512]{1,0:T(8,128)(2,1)S(1)} %mirror_sum.1.after.refs_0_), channel_id=1, source_target_pairs={{0,64},{1,65},{2,66},{3,67},{4,68},{5,69},{6,70},{7,71},{8,72},{9,... | collective-permute-start | bytes 393224 | tf_op jit(solution)/shard_map/ppermute | solution.py:30
  113.6 6.5 %collective-permute-start.26 = (bf16[128,512]{1,0:T(8,128)(2,1)S(1)}, bf16[128,512]{1,0:T(8,128)(2,1)S(1)}, u32[]{:S(2)}, u32[]{:S(2)}) collective-permute-start(bf16[128,512]{1,0:T(8,128)(2,1)S(1)} %z_sum.2.refs_0_), channel_id=1, source_target_pairs={{0,128},{1,129},{2,130},{3,131},{4,132},{5,133},{6,134},{7,135},{8... | collective-permute-start | bytes 393224 | tf_op jit(solution)/shard_map/ppermute | solution.py:30
  120.2 8.2 %collective-permute-start.27 = (bf16[128,512]{1,0:T(8,128)(2,1)S(1)}, bf16[128,512]{1,0:T(8,128)(2,1)S(1)}, u32[]{:S(2)}, u32[]{:S(2)}) collective-permute-start(bf16[128,512]{1,0:T(8,128)(2,1)S(1)} %z_sum.3.mine), channel_id=1, source_target_pairs={{0,32},{1,33},{2,34},{3,35},{4,36},{5,37},{6,38},{7,39},{8,40},{9,... | collective-permute-start | bytes 393224 | tf_op jit(solution)/shard_map/ppermute | solution.py:30
  (19 other events, 92.5 us)

commit v5 on v2

--- a/solution.py
+++ b/solution.py
@@ -458,8 +458,8 @@
     grad_q, grad_k, scored = attention_dscore(probs, values, upstream, queries, keys)
     grad_inputs, joined = join(columns)
 
-    after = [VMEM] * 2 + [ANY] * (NY - 1)
-    total = call(pair_sum_kernel, "z_sum", small, total, permute(total, flip_zl(1)), *columns[1:], ins=after)[0]
+    after = [VMEM] * 2 + [ANY] * 2
+    total = call(pair_sum_kernel, "z_sum", small, total, permute(total, flip_zl(1)), columns[1], columns[3], ins=after)[0]
     total = call(pair_sum_kernel, "z_sum", small, total, permute(total, flip_zl(2)), scored, ins=order)[0]
     out = [like((NCO * half, width), BF16)]
     grad_weight = call(halves_kernel, "halves", out, total, permute(total, other_core), joined, ins=order)[0]

time: 139 us -> 138 us (level)
  waiting for transfers between devices: 30.4 us -> 22.3 us
  starting transfers between devices: 66.8 us -> 73.1 us
    ppermute x28, waiting for transfers between devices: 23.6 us -> 15.6 us  [permute(): return lax.ppermute(array, AXES, pairs)]
    ppermute x28, starting transfers between devices: 42.3 us -> 48.6 us  [permute(): return lax.ppermute(array, AXES, pairs)]
    unnamed x64 -> x66, local copies, waits for them, and re-layouts: 5.76 us -> 6.53 us
  transfers between devices with their start and end apart: 31 -> 31, of which waited for: 10 -> 9; matrix products, arithmetic and copies ran while one was open for 0% -> 0% of each run, Pallas kernels for 23% -> 23%
where the time goes in v5:
time: 138 us; the launch traced here: 137 us
  starting transfers between devices  73.1 us (53%)
  Pallas kernels  34.1 us (25%)
  waiting for transfers between devices  22.3 us (16%)
  local copies, waits for them, and re-layouts  6.53 us (5%)
    ppermute x28, starting transfers between devices, permute(): return lax.ppermute(array, AXES, pairs)  48.6 us
    pallas_call x17, Pallas kernels, call(): pl.pallas_call(kernel, out_shape=out, in_specs=[VMEM] * len(args) if ins...  27.7 us
    all_to_all x3, starting transfers between devices, exchange(): lax.all_to_all(buffer, 'fsdp', split_axis=0, concat_axis=0, tiled=True)  24.5 us
    ppermute x28, waiting for transfers between devices, permute(): return lax.ppermute(array, AXES, pairs)  15.6 us
    all_to_all x3, waiting for transfers between devices, exchange(): lax.all_to_all(buffer, 'fsdp', split_axis=0, concat_axis=0, tiled=True)  6.76 us
    unnamed x66, local copies, waits for them, and re-layouts  6.53 us
    pallas_call x1, Pallas kernels, per_head(): pl.pallas_call(kernel, grid=(KVH,), out_shape=[o for o, _ in outs], in_sp...  6.41 us
  transfers between devices with their start and end apart: 31, of which 9 were waited for; matrix products, arithmetic and copies ran while one was open for 0% of the time, Pallas kernels for 23%

profile of v5, /device:TPU:1, one launch (start us, length us, event | category | flops | bytes accessed | tf_op | source)
XLA Modules:
  0.0 137.1 jit_solution(9514245998712559695)
XLA Ops:
  0.6 6.5 %collective-permute-start = (bf16[256,512]{1,0:T(8,128)(2,1)}, bf16[256,512]{1,0:T(8,128)(2,1)S(1)}, u32[]{:S(2)}, u32[]{:S(2)}) collective-permute-start(bf16[256,512]{1,0:T(8,128)(2,1)} %a.1), channel_id=1, source_target_pairs={{0,208},{1,209},{2,210},{3,211},{4,212},{5,213},{6,214},{7,215},{8... | collective-permute-start | bytes 786440 | tf_op jit(solution)/shard_map/ppermute | solution.py:30
  7.1 1.4 %masks.1.after = s32[32,8,128]{2,1,0:T(8,128)} custom-call(s32[128]{0:T(128)} %slots_in.1, s32[128]{0:T(128)} %ids_in.1), custom_call_target="tpu_custom_call" | custom-call | bytes 132096 | tf_op jit(solution)/shard_map/masks/pallas_call | solution.py:55
  8.5 8.1 %all-to-all-start = ((s32[32,8,128]{2,1,0:T(8,128)}), s32[32,8,128]{2,1,0:T(8,128)S(1)}, u32[]{:S(2)}, u32[]{:S(2)}) async-start(s32[32,8,128]{2,1,0:T(8,128)} %masks.1.after), calls=%async_computation | async-start | bytes 262144 | tf_op jit(solution)/shard_map/all_to_all | solution.py:421
  16.7 3.5 %split.1 = (bf16[128,2048]{1,0:T(8,128)(2,1)}, bf16[128,2048]{1,0:T(8,128)(2,1)}, bf16[128,2048]{1,0:T(8,128)(2,1)}, bf16[128,2048]{1,0:T(8,128)(2,1)}) custom-call(bf16[128,8192]{1,0:T(8,128)(2,1)} %full_in.1, s32[32,8,128]{2,1,0:T(8,128)} %masks.1.after), custom_call_target="tpu_custom_call" | custom-call | bytes 4325376 | tf_op jit(solution)/shard_map/split/pallas_call | solution.py:55
  20.2 1.3 collective-permute-start.1
  21.5 2.4 %collective-permute-start.2 = (bf16[128,2048]{1,0:T(8,128)(2,1)}, bf16[128,2048]{1,0:T(8,128)(2,1)S(1)}, u32[]{:S(2)}, u32[]{:S(2)}) collective-permute-start(bf16[128,2048]{1,0:T(8,128)(2,1)} %get-tuple-element.35), channel_id=1, source_target_pairs={{0,2},{1,3},{2,0},{3,1},{4,6},{5,7},{6,4},{7,5},{8,10},{9,11},{10,... | collective-permute-start | bytes 1572872 | tf_op jit(solution)/shard_map/ppermute | solution.py:30
  25.1 3.1 %scores.1.scores_in = f32[4,2,8,1024]{3,2,1,0:T(8,128)} custom-call(bf16[256,4096]{1,0:T(8,128)(2,1)} %queries.3, bf16[256,512]{1,0:T(8,128)(2,1)} %keys.1), custom_call_target="tpu_custom_call" | custom-call | flops 268435456 | bytes 2621440 | tf_op jit(solution)/shard_map/scores/pallas_call | solution.py:55
  29.6 3.3 %probs.1 = (bf16[256,512]{1,0:T(8,128)(2,1)}, f32[4,2,8,1024]{3,2,1,0:T(8,128)}) custom-call(f32[4,2,8,1024]{3,2,1,0:T(8,128)} %scores.1.scores_in, s32[32,8,128]{2,1,0:T(8,128)} %copy-done.26, bf16[256,4096]{1,0:T(8,128)(2,1)} %upstream.3, bf16[256,512]{1,0:T(8,128)(2,1)} %copy-done), custom_call_target="tpu_custom_call" | custom-call | flops 268435456 | bytes 3276800 | tf_op jit(solution)/shard_map/probs/pallas_call | solution.py:55
  32.8 9.2 %all-to-all-start.1 = ((bf16[32,8,512]{2,1,0:T(8,128)(2,1)}), bf16[32,8,512]{2,1,0:T(8,128)(2,1)S(1)}, u32[]{:S(2)}, u32[]{:S(2)}) async-start(bf16[32,8,512]{2,1,0:T(8,128)(2,1)} %bitcast.9), calls=%async_computation.1 | async-start | bytes 524288 | tf_op jit(solution)/shard_map/all_to_all | solution.py:421
  42.1 1.3 collective-permute-start.7
  43.4 2.4 %collective-permute-start.8 = (bf16[256,512]{1,0:T(8,128)(2,1)S(1)}, bf16[256,512]{1,0:T(8,128)(2,1)S(1)}, u32[]{:S(2)}, u32[]{:S(2)}) collective-permute-start(bf16[256,512]{1,0:T(8,128)(2,1)S(1)} %copy-done.1), channel_id=1, source_target_pairs={{0,8},{1,9},{2,10},{3,11},{4,12},{5,13},{6,14},{7,15},{8,0},{9,1},... | collective-permute-start | bytes 786440 | tf_op jit(solution)/shard_map/ppermute | solution.py:30
  47.4 6.8 %all-to-all-done.1 = bf16[32,8,512]{2,1,0:T(8,128)(2,1)S(1)} async-done(((bf16[32,8,512]{2,1,0:T(8,128)(2,1)}), bf16[32,8,512]{2,1,0:T(8,128)(2,1)S(1)}, u32[]{:S(2)}, u32[]{:S(2)}) %all-to-all-start.1) | async-done | bytes 262176 | tf_op jit(solution)/shard_map/all_to_all | solution.py:421
  54.5 2.2 %collective-permute-start.5 = (bf16[128,512]{1,0:T(8,128)(2,1)S(1)}, bf16[128,512]{1,0:T(8,128)(2,1)S(1)}, u32[]{:S(2)}, u32[]{:S(2)}) collective-permute-start(bf16[128,512]{1,0:T(8,128)(2,1)S(1)} %pick.1.refs_4_.refs_0_), channel_id=1, source_target_pairs={{0,2},{1,3},{2,0},{3,1},{4,6},{5,7},{6,4},{7,5},{8,10},{9,11},{10,... | collective-permute-start | bytes 393224 | tf_op jit(solution)/shard_map/ppermute | solution.py:30
  58.4 2.5 %collective-permute-done.4.refs_5_.refs_1_ = bf16[128,512]{1,0:T(8,128)(2,1)S(1)} collective-permute-done((bf16[128,512]{1,0:T(8,128)(2,1)S(1)}, bf16[128,512]{1,0:T(8,128)(2,1)S(1)}, u32[]{:S(2)}, u32[]{:S(2)}) %collective-permute-start.4) | collective-permute-done | bytes 131104 | tf_op jit(solution)/shard_map/ppermute | solution.py:30
  61.5 2.2 %shares.1 = (f32[8,128,512]{2,1,0:T(8,128)S(1)}, bf16[8,128,512]{2,1,0:T(8,128)(2,1)S(1)}, f32[8,128]{1,0:T(8,128)S(1)}) custom-call(bf16[128,2048]{1,0:T(8,128)(2,1)S(1)} %copy-done.7, bf16[128,2048]{1,0:T(8,128)(2,1)S(1)} %collective-permute-done.1.refs_2_.refs_1_, bf16[128,2048]{1,0:T(8,128)(2,1)S(1)} %collective-permute-done.2.refs_3_.refs_2_, ...), custom_call_target="tpu_custom_call" | custom-call | flops 1073741824 | bytes 6557696 | tf_op jit(solution)/shard_map/shares/pallas_call | solution.py:55
  63.7 5.3 %collective-permute-start.14 = (bf16[8,128,512]{2,1,0:T(8,128)(2,1)S(1)}, bf16[8,128,512]{2,1,0:T(8,128)(2,1)S(1)}, u32[]{:S(2)}, u32[]{:S(2)}) collective-permute-start(bf16[8,128,512]{2,1,0:T(8,128)(2,1)S(1)} %get-tuple-element.39), channel_id=1, source_target_pairs={{0,32},{1,33},{2,34},{3,35},{4,36},{5,37},{6,38},{7,39},{8,40},{9,... | collective-permute-start | bytes 3145736 | tf_op jit(solution)/shard_map/ppermute | solution.py:30
  70.0 1.3 collective-permute-done.14.got
  72.3 1.6 %collective-permute-start.21 = (bf16[2,128,512]{2,1,0:T(8,128)(2,1)S(1)}, bf16[2,128,512]{2,1,0:T(8,128)(2,1)S(1)}, u32[]{:S(2)}, u32[]{:S(2)}) collective-permute-start(bf16[2,128,512]{2,1,0:T(8,128)(2,1)S(1)} %get-tuple-element.52), channel_id=1, source_target_pairs={{0,12},{1,13},{2,14},{3,15},{4,0},{5,1},{6,2},{7,3},{8,4},{9,5},{1... | collective-permute-start | bytes 786440 | tf_op jit(solution)/shard_map/ppermute | solution.py:30
  75.4 4.3 %partial_values.1 = (f32[128,512]{1,0:T(8,128)}, bf16[128,512]{1,0:T(8,128)(2,1)}, bf16[128,512]{1,0:T(8,128)(2,1)}, bf16[128,512]{1,0:T(8,128)(2,1)}) custom-call(bf16[128,2048]{1,0:T(8,128)(2,1)} %get-tuple-element.37.refs_0_, bf16[128,2048]{1,0:T(8,128)(2,1)} %copy-done.2, bf16[128,2048]{1,0:T(8,128)(2,1)} %copy-done.3, bf16[128,2048]{1,0:T(8,128)(2,1)} %copy-done.4, ...), custom_call_target="tpu_custom_call" | custom-call | flops 1073741824 | bytes 4853760 | tf_op jit(solution)/shard_map/partial_values/pallas_call | solution.py:55
  79.7 2.3 %collective-permute-start.18 = (bf16[128,512]{1,0:T(8,128)(2,1)}, bf16[128,512]{1,0:T(8,128)(2,1)S(1)}, u32[]{:S(2)}, u32[]{:S(2)}) collective-permute-start(bf16[128,512]{1,0:T(8,128)(2,1)} %get-tuple-element.49), channel_id=1, source_target_pairs={{0,3},{1,0},{2,1},{3,2},{4,7},{5,4},{6,5},{7,6},{8,11},{9,8},{10,9... | collective-permute-start | bytes 393224 | tf_op jit(solution)/shard_map/ppermute | solution.py:30
  82.0 4.4 %back.1 = (bf16[128,2048]{1,0:T(8,128)(2,1)}, bf16[128,2048]{1,0:T(8,128)(2,1)}, bf16[128,2048]{1,0:T(8,128)(2,1)}, bf16[128,2048]{1,0:T(8,128)(2,1)}, f32[8,128]{1,0:T(8,128)}) custom-call(bf16[128,512]{1,0:T(8,128)(2,1)} %copy-done.15, bf16[128,512]{1,0:T(8,128)(2,1)} %copy-done.21, bf16[128,512]{1,0:T(8,128)(2,1)} %copy-done.22, ...), custom_call_target="tpu_custom_call" | custom-call | flops 1073741824 | bytes 5246976 | tf_op jit(solution)/shard_map/back/pallas_call | solution.py:55
  87.2 2.1 %collective-permute-done.23.c = bf16[2,128,512]{2,1,0:T(8,128)(2,1)S(1)} collective-permute-done((bf16[2,128,512]{2,1,0:T(8,128)(2,1)S(1)}, bf16[2,128,512]{2,1,0:T(8,128)(2,1)S(1)}, u32[]{:S(2)}, u32[]{:S(2)}) %collective-permute-start.23) | collective-permute-done | bytes 262176 | tf_op jit(solution)/shard_map/ppermute | solution.py:30
  90.6 2.0 %collective-permute-start.15 = (bf16[128,2048]{1,0:T(8,128)(2,1)}, bf16[128,2048]{1,0:T(8,128)(2,1)S(1)}, u32[]{:S(2)}, u32[]{:S(2)}) collective-permute-start(bf16[128,2048]{1,0:T(8,128)(2,1)} %get-tuple-element.42), channel_id=1, source_target_pairs={{0,3},{1,0},{2,1},{3,2},{4,7},{5,4},{6,5},{7,6},{8,11},{9,8},{10,9... | collective-permute-start | bytes 1572872 | tf_op jit(solution)/shard_map/ppermute | solution.py:30
  92.6 3.4 %collective-permute-done.24.refs_1_ = bf16[128,512]{1,0:T(8,128)(2,1)S(1)} collective-permute-done((bf16[128,512]{1,0:T(8,128)(2,1)S(1)}, bf16[128,512]{1,0:T(8,128)(2,1)S(1)}, u32[]{:S(2)}, u32[]{:S(2)}) %collective-permute-start.24) | collective-permute-done | bytes 131104 | tf_op jit(solution)/shard_map/ppermute | solution.py:30
  97.0 7.1 %all-to-all-start.2 = ((bf16[32,8,512]{2,1,0:T(8,128)(2,1)}), bf16[32,8,512]{2,1,0:T(8,128)(2,1)S(1)}, u32[]{:S(2)}, u32[]{:S(2)}) async-start(bf16[32,8,512]{2,1,0:T(8,128)(2,1)} %bitcast.3), calls=%async_computation.2 | async-start | bytes 524288 | tf_op jit(solution)/shard_map/all_to_all | solution.py:421
  104.1 2.8 %collective-permute-start.16 = (bf16[128,2048]{1,0:T(8,128)(2,1)S(1)}, bf16[128,2048]{1,0:T(8,128)(2,1)S(1)}, u32[]{:S(2)}, u32[]{:S(2)}) collective-permute-start(bf16[128,2048]{1,0:T(8,128)(2,1)S(1)} %copy-done.31), channel_id=1, source_target_pairs={{0,2},{1,3},{2,0},{3,1},{4,6},{5,7},{6,4},{7,5},{8,10},{9,11},{10,... | collective-permute-start | bytes 1572872 | tf_op jit(solution)/shard_map/ppermute | solution.py:30
  106.9 2.9 %collective-permute-start.25 = (bf16[128,512]{1,0:T(8,128)(2,1)S(1)}, bf16[128,512]{1,0:T(8,128)(2,1)S(1)}, u32[]{:S(2)}, u32[]{:S(2)}) collective-permute-start(bf16[128,512]{1,0:T(8,128)(2,1)S(1)} %mirror_sum.1.after.refs_0_), channel_id=1, source_target_pairs={{0,64},{1,65},{2,66},{3,67},{4,68},{5,69},{6,70},{7,71},{8,72},{9,... | collective-permute-start | bytes 393224 | tf_op jit(solution)/shard_map/ppermute | solution.py:30
  109.8 4.6 %collective-permute-done.25.refs_1_ = bf16[128,512]{1,0:T(8,128)(2,1)S(1)} collective-permute-done((bf16[128,512]{1,0:T(8,128)(2,1)S(1)}, bf16[128,512]{1,0:T(8,128)(2,1)S(1)}, u32[]{:S(2)}, u32[]{:S(2)}) %collective-permute-start.25) | collective-permute-done | bytes 131104 | tf_op jit(solution)/shard_map/ppermute | solution.py:30
  114.4 2.7 %collective-permute-start.26 = (bf16[128,512]{1,0:T(8,128)(2,1)S(1)}, bf16[128,512]{1,0:T(8,128)(2,1)S(1)}, u32[]{:S(2)}, u32[]{:S(2)}) collective-permute-start(bf16[128,512]{1,0:T(8,128)(2,1)S(1)} %z_sum.2.refs_0_), channel_id=1, source_target_pairs={{0,128},{1,129},{2,130},{3,131},{4,132},{5,133},{6,134},{7,135},{8... | collective-permute-start | bytes 393224 | tf_op jit(solution)/shard_map/ppermute | solution.py:30
  117.9 6.4 %dscore.1 = (bf16[256,4096]{1,0:T(8,128)(2,1)}, bf16[256,512]{1,0:T(8,128)(2,1)}, f32[8,128]{1,0:T(8,128)}) custom-call(f32[4,2,8,1024]{3,2,1,0:T(8,128)} %get-tuple-element.46.probs, bf16[256,512]{1,0:T(8,128)(2,1)} %bitcast.8, bf16[256,4096]{1,0:T(8,128)(2,1)} %upstream.3, bf16[256,4096]{1,0:T(8,128)(2,1)} %queries.3, bf16[256,512]{1,0:T(8,128)(2,1)} %keys.1), custom_call_target="tpu_custom_call" | custom-call | flops 805306368 | bytes 7344128 | tf_op jit(solution)/shard_map/dscore/pallas_call | solution.py:236
  125.0 6.5 %collective-permute-start.27 = (bf16[128,512]{1,0:T(8,128)(2,1)S(1)}, bf16[128,512]{1,0:T(8,128)(2,1)S(1)}, u32[]{:S(2)}, u32[]{:S(2)}) collective-permute-start(bf16[128,512]{1,0:T(8,128)(2,1)S(1)} %z_sum.3.mine), channel_id=1, source_target_pairs={{0,32},{1,33},{2,34},{3,35},{4,36},{5,37},{6,38},{7,39},{8,40},{9,... | collective-permute-start | bytes 393224 | tf_op jit(solution)/shard_map/ppermute | solution.py:30
  132.3 3.3 %join.1 = (bf16[128,8192]{1,0:T(8,128)(2,1)}, f32[8,128]{1,0:T(8,128)}) custom-call(bf16[128,2048]{1,0:T(8,128)(2,1)} %get-tuple-element.41.p0, bf16[128,2048]{1,0:T(8,128)(2,1)} %copy-done.5, bf16[128,2048]{1,0:T(8,128)(2,1)} %copy-done.25, bf16[128,2048]{1,0:T(8,128)(2,1)} %copy-done.6), custom_call_target="tpu_custom_call" | custom-call | bytes 4198400 | tf_op jit(solution)/shard_map/join/pallas_call | solution.py:55
  (114 shorter events, 16.9 us)
Async XLA Ops:
  0.6 27.5 %collective-permute-start = (bf16[256,512]{1,0:T(8,128)(2,1)}, bf16[256,512]{1,0:T(8,128)(2,1)S(1)}, u32[]{:S(2)}, u32[]{:S(2)}) collective-permute-start(bf16[256,512]{1,0:T(8,128)(2,1)} %a.1), channel_id=1, source_target_pairs={{0,208},{1,209},{2,210},{3,211},{4,212},{5,213},{6,214},{7,215},{8... | collective-permute-start | bytes 786440 | tf_op jit(solution)/shard_map/ppermute | solution.py:30
  8.5 20.4 %all-to-all-start = ((s32[32,8,128]{2,1,0:T(8,128)}), s32[32,8,128]{2,1,0:T(8,128)S(1)}, u32[]{:S(2)}, u32[]{:S(2)}) async-start(s32[32,8,128]{2,1,0:T(8,128)} %masks.1.after), calls=%async_computation | async-start | bytes 262144 | tf_op jit(solution)/shard_map/all_to_all | solution.py:421
  20.2 25.6 %collective-permute-start.1 = (bf16[128,2048]{1,0:T(8,128)(2,1)}, bf16[128,2048]{1,0:T(8,128)(2,1)S(1)}, u32[]{:S(2)}, u32[]{:S(2)}) collective-permute-start(bf16[128,2048]{1,0:T(8,128)(2,1)} %get-tuple-element.34), channel_id=1, source_target_pairs={{0,1},{1,2},{2,3},{3,0},{4,5},{5,6},{6,7},{7,4},{8,9},{9,10},{10,1... | collective-permute-start | bytes 1572872 | tf_op jit(solution)/shard_map/ppermute | solution.py:30
  21.5 25.5 %collective-permute-start.2 = (bf16[128,2048]{1,0:T(8,128)(2,1)}, bf16[128,2048]{1,0:T(8,128)(2,1)S(1)}, u32[]{:S(2)}, u32[]{:S(2)}) collective-permute-start(bf16[128,2048]{1,0:T(8,128)(2,1)} %get-tuple-element.35), channel_id=1, source_target_pairs={{0,2},{1,3},{2,0},{3,1},{4,6},{5,7},{6,4},{7,5},{8,10},{9,11},{10,... | collective-permute-start | bytes 1572872 | tf_op jit(solution)/shard_map/ppermute | solution.py:30
  23.9 23.5 %collective-permute-start.3 = (bf16[128,2048]{1,0:T(8,128)(2,1)}, bf16[128,2048]{1,0:T(8,128)(2,1)S(1)}, u32[]{:S(2)}, u32[]{:S(2)}) collective-permute-start(bf16[128,2048]{1,0:T(8,128)(2,1)} %get-tuple-element.36), channel_id=1, source_target_pairs={{0,3},{1,0},{2,1},{3,2},{4,7},{5,4},{6,5},{7,6},{8,11},{9,8},{10,9... | collective-permute-start | bytes 1572872 | tf_op jit(solution)/shard_map/ppermute | solution.py:30
  28.9 32.5 %copy-start.7 = (bf16[128,2048]{1,0:T(8,128)(2,1)S(1)}, bf16[128,2048]{1,0:T(8,128)(2,1)}, u32[]{:S(2)}) copy-start(bf16[128,2048]{1,0:T(8,128)(2,1)} %get-tuple-element.37.refs_0_) | copy-start | bytes 1572868
  32.8 21.3 %all-to-all-start.1 = ((bf16[32,8,512]{2,1,0:T(8,128)(2,1)}), bf16[32,8,512]{2,1,0:T(8,128)(2,1)S(1)}, u32[]{:S(2)}, u32[]{:S(2)}) async-start(bf16[32,8,512]{2,1,0:T(8,128)(2,1)} %bitcast.9), calls=%async_computation.1 | async-start | bytes 524288 | tf_op jit(solution)/shard_map/all_to_all | solution.py:421
  42.1 14.6 %collective-permute-start.7 = (bf16[256,512]{1,0:T(8,128)(2,1)S(1)}, bf16[256,512]{1,0:T(8,128)(2,1)S(1)}, u32[]{:S(2)}, u32[]{:S(2)}) collective-permute-start(bf16[256,512]{1,0:T(8,128)(2,1)S(1)} %copy-done.1), channel_id=1, source_target_pairs={{0,4},{1,5},{2,6},{3,7},{4,8},{5,9},{6,10},{7,11},{8,12},{9,13},{1... | collective-permute-start | bytes 786440 | tf_op jit(solution)/shard_map/ppermute | solution.py:30
  43.4 14.3 %collective-permute-start.8 = (bf16[256,512]{1,0:T(8,128)(2,1)S(1)}, bf16[256,512]{1,0:T(8,128)(2,1)S(1)}, u32[]{:S(2)}, u32[]{:S(2)}) collective-permute-start(bf16[256,512]{1,0:T(8,128)(2,1)S(1)} %copy-done.1), channel_id=1, source_target_pairs={{0,8},{1,9},{2,10},{3,11},{4,12},{5,13},{6,14},{7,15},{8,0},{9,1},... | collective-permute-start | bytes 786440 | tf_op jit(solution)/shard_map/ppermute | solution.py:30
  45.8 12.6 %collective-permute-start.9 = (bf16[256,512]{1,0:T(8,128)(2,1)S(1)}, bf16[256,512]{1,0:T(8,128)(2,1)S(1)}, u32[]{:S(2)}, u32[]{:S(2)}) collective-permute-start(bf16[256,512]{1,0:T(8,128)(2,1)S(1)} %copy-done.1), channel_id=1, source_target_pairs={{0,12},{1,13},{2,14},{3,15},{4,0},{5,1},{6,2},{7,3},{8,4},{9,5},{1... | collective-permute-start | bytes 786440 | tf_op jit(solution)/shard_map/ppermute | solution.py:30
  54.4 6.5 %collective-permute-start.4 = (bf16[128,512]{1,0:T(8,128)(2,1)S(1)}, bf16[128,512]{1,0:T(8,128)(2,1)S(1)}, u32[]{:S(2)}, u32[]{:S(2)}) collective-permute-start(bf16[128,512]{1,0:T(8,128)(2,1)S(1)} %pick.1.refs_4_.refs_0_), channel_id=1, source_target_pairs={{0,1},{1,2},{2,3},{3,0},{4,5},{5,6},{6,7},{7,4},{8,9},{9,10},{10,1... | collective-permute-start | bytes 393224 | tf_op jit(solution)/shard_map/ppermute | solution.py:30
  54.5 6.4 %collective-permute-start.5 = (bf16[128,512]{1,0:T(8,128)(2,1)S(1)}, bf16[128,512]{1,0:T(8,128)(2,1)S(1)}, u32[]{:S(2)}, u32[]{:S(2)}) collective-permute-start(bf16[128,512]{1,0:T(8,128)(2,1)S(1)} %pick.1.refs_4_.refs_0_), channel_id=1, source_target_pairs={{0,2},{1,3},{2,0},{3,1},{4,6},{5,7},{6,4},{7,5},{8,10},{9,11},{10,... | collective-permute-start | bytes 393224 | tf_op jit(solution)/shard_map/ppermute | solution.py:30
  56.7 4.8 %collective-permute-start.6 = (bf16[128,512]{1,0:T(8,128)(2,1)S(1)}, bf16[128,512]{1,0:T(8,128)(2,1)S(1)}, u32[]{:S(2)}, u32[]{:S(2)}) collective-permute-start(bf16[128,512]{1,0:T(8,128)(2,1)S(1)} %pick.1.refs_4_.refs_0_), channel_id=1, source_target_pairs={{0,3},{1,0},{2,1},{3,2},{4,7},{5,4},{6,5},{7,6},{8,11},{9,8},{10,9... | collective-permute-start | bytes 393224 | tf_op jit(solution)/shard_map/ppermute | solution.py:30
  63.7 7.5 %collective-permute-start.14 = (bf16[8,128,512]{2,1,0:T(8,128)(2,1)S(1)}, bf16[8,128,512]{2,1,0:T(8,128)(2,1)S(1)}, u32[]{:S(2)}, u32[]{:S(2)}) collective-permute-start(bf16[8,128,512]{2,1,0:T(8,128)(2,1)S(1)} %get-tuple-element.39), channel_id=1, source_target_pairs={{0,32},{1,33},{2,34},{3,35},{4,36},{5,37},{6,38},{7,39},{8,40},{9,... | collective-permute-start | bytes 3145736 | tf_op jit(solution)/shard_map/ppermute | solution.py:30
  69.0 5.0 %collective-permute-start.10 = (bf16[256,512]{1,0:T(8,128)(2,1)S(1)}, bf16[256,512]{1,0:T(8,128)(2,1)S(1)}, u32[]{:S(2)}, u32[]{:S(2)}) collective-permute-start(bf16[256,512]{1,0:T(8,128)(2,1)S(1)} %copy-done.1), channel_id=1, source_target_pairs={{0,32},{1,33},{2,34},{3,35},{4,36},{5,37},{6,38},{7,39},{8,40},{9,... | collective-permute-start | bytes 786440 | tf_op jit(solution)/shard_map/ppermute | solution.py:30
  69.1 5.3 %collective-permute-start.11 = (bf16[256,512]{1,0:T(8,128)(2,1)S(1)}, bf16[256,512]{1,0:T(8,128)(2,1)S(1)}, u32[]{:S(2)}, u32[]{:S(2)}) collective-permute-start(bf16[256,512]{1,0:T(8,128)(2,1)S(1)} %collective-permute-done.7.refs_8_.refs_5_), channel_id=1, source_target_pairs={{0,32},{1,33},{2,34},{3,35},{4,36},{5,37},{6,38},{7,39},{8,40},{9,... | collective-permute-start | bytes 786440 | tf_op jit(solution)/shard_map/ppermute | solution.py:30
  69.5 5.1 %collective-permute-start.12 = (bf16[256,512]{1,0:T(8,128)(2,1)S(1)}, bf16[256,512]{1,0:T(8,128)(2,1)S(1)}, u32[]{:S(2)}, u32[]{:S(2)}) collective-permute-start(bf16[256,512]{1,0:T(8,128)(2,1)S(1)} %collective-permute-done.8.refs_9_.refs_6_), channel_id=1, source_target_pairs={{0,32},{1,33},{2,34},{3,35},{4,36},{5,37},{6,38},{7,39},{8,40},{9,... | collective-permute-start | bytes 786440 | tf_op jit(solution)/shard_map/ppermute | solution.py:30
  69.6 5.0 %collective-permute-start.13 = (bf16[256,512]{1,0:T(8,128)(2,1)S(1)}, bf16[256,512]{1,0:T(8,128)(2,1)S(1)}, u32[]{:S(2)}, u32[]{:S(2)}) collective-permute-start(bf16[256,512]{1,0:T(8,128)(2,1)S(1)} %collective-permute-done.9.refs_10_.refs_7_), channel_id=1, source_target_pairs={{0,32},{1,33},{2,34},{3,35},{4,36},{5,37},{6,38},{7,39},{8,40},{9,... | collective-permute-start | bytes 786440 | tf_op jit(solution)/shard_map/ppermute | solution.py:30
  72.3 14.1 %collective-permute-start.21 = (bf16[2,128,512]{2,1,0:T(8,128)(2,1)S(1)}, bf16[2,128,512]{2,1,0:T(8,128)(2,1)S(1)}, u32[]{:S(2)}, u32[]{:S(2)}) collective-permute-start(bf16[2,128,512]{2,1,0:T(8,128)(2,1)S(1)} %get-tuple-element.52), channel_id=1, source_target_pairs={{0,12},{1,13},{2,14},{3,15},{4,0},{5,1},{6,2},{7,3},{8,4},{9,5},{1... | collective-permute-start | bytes 786440 | tf_op jit(solution)/shard_map/ppermute | solution.py:30
  73.9 13.2 %collective-permute-start.22 = (bf16[2,128,512]{2,1,0:T(8,128)(2,1)S(1)}, bf16[2,128,512]{2,1,0:T(8,128)(2,1)S(1)}, u32[]{:S(2)}, u32[]{:S(2)}) collective-permute-start(bf16[2,128,512]{2,1,0:T(8,128)(2,1)S(1)} %get-tuple-element.53), channel_id=1, source_target_pairs={{0,8},{1,9},{2,10},{3,11},{4,12},{5,13},{6,14},{7,15},{8,0},{9,1},... | collective-permute-start | bytes 786440 | tf_op jit(solution)/shard_map/ppermute | solution.py:30
  74.3 14.9 %collective-permute-start.23 = (bf16[2,128,512]{2,1,0:T(8,128)(2,1)S(1)}, bf16[2,128,512]{2,1,0:T(8,128)(2,1)S(1)}, u32[]{:S(2)}, u32[]{:S(2)}) collective-permute-start(bf16[2,128,512]{2,1,0:T(8,128)(2,1)S(1)} %get-tuple-element.54), channel_id=1, source_target_pairs={{0,4},{1,5},{2,6},{3,7},{4,8},{5,9},{6,10},{7,11},{8,12},{9,13},{1... | collective-permute-start | bytes 786440 | tf_op jit(solution)/shard_map/ppermute | solution.py:30
  79.7 12.9 %collective-permute-start.18 = (bf16[128,512]{1,0:T(8,128)(2,1)}, bf16[128,512]{1,0:T(8,128)(2,1)S(1)}, u32[]{:S(2)}, u32[]{:S(2)}) collective-permute-start(bf16[128,512]{1,0:T(8,128)(2,1)} %get-tuple-element.49), channel_id=1, source_target_pairs={{0,3},{1,0},{2,1},{3,2},{4,7},{5,4},{6,5},{7,6},{8,11},{9,8},{10,9... | collective-permute-start | bytes 393224 | tf_op jit(solution)/shard_map/ppermute | solution.py:30
  82.0 10.6 %collective-permute-start.19 = (bf16[128,512]{1,0:T(8,128)(2,1)}, bf16[128,512]{1,0:T(8,128)(2,1)S(1)}, u32[]{:S(2)}, u32[]{:S(2)}) collective-permute-start(bf16[128,512]{1,0:T(8,128)(2,1)} %get-tuple-element.50), channel_id=1, source_target_pairs={{0,2},{1,3},{2,0},{3,1},{4,6},{5,7},{6,4},{7,5},{8,10},{9,11},{10,... | collective-permute-start | bytes 393224 | tf_op jit(solution)/shard_map/ppermute | solution.py:30
  86.4 6.2 %collective-permute-start.20 = (bf16[128,512]{1,0:T(8,128)(2,1)S(1)}, bf16[128,512]{1,0:T(8,128)(2,1)S(1)}, u32[]{:S(2)}, u32[]{:S(2)}) collective-permute-start(bf16[128,512]{1,0:T(8,128)(2,1)S(1)} %copy-done.32), channel_id=1, source_target_pairs={{0,1},{1,2},{2,3},{3,0},{4,5},{5,6},{6,7},{7,4},{8,9},{9,10},{10,1... | collective-permute-start | bytes 393224 | tf_op jit(solution)/shard_map/ppermute | solution.py:30
  90.1 5.9 %collective-permute-start.24 = (bf16[128,512]{1,0:T(8,128)(2,1)S(1)}, bf16[128,512]{1,0:T(8,128)(2,1)S(1)}, u32[]{:S(2)}, u32[]{:S(2)}) collective-permute-start(bf16[128,512]{1,0:T(8,128)(2,1)S(1)} %get-tuple-element.57), channel_id=1, source_target_pairs={{0,208},{1,209},{2,210},{3,211},{4,212},{5,213},{6,214},{7,215},{8... | collective-permute-start | bytes 393224 | tf_op jit(solution)/shard_map/ppermute | solution.py:30
  90.6 23.8 %collective-permute-start.15 = (bf16[128,2048]{1,0:T(8,128)(2,1)}, bf16[128,2048]{1,0:T(8,128)(2,1)S(1)}, u32[]{:S(2)}, u32[]{:S(2)}) collective-permute-start(bf16[128,2048]{1,0:T(8,128)(2,1)} %get-tuple-element.42), channel_id=1, source_target_pairs={{0,3},{1,0},{2,1},{3,2},{4,7},{5,4},{6,5},{7,6},{8,11},{9,8},{10,9... | collective-permute-start | bytes 1572872 | tf_op jit(solution)/shard_map/ppermute | solution.py:30
  92.6 21.8 %collective-permute-start.17 = (bf16[128,2048]{1,0:T(8,128)(2,1)}, bf16[128,2048]{1,0:T(8,128)(2,1)S(1)}, u32[]{:S(2)}, u32[]{:S(2)}) collective-permute-start(bf16[128,2048]{1,0:T(8,128)(2,1)} %get-tuple-element.44), channel_id=1, source_target_pairs={{0,1},{1,2},{2,3},{3,0},{4,5},{5,6},{6,7},{7,4},{8,9},{9,10},{10,1... | collective-permute-start | bytes 1572872 | tf_op jit(solution)/shard_map/ppermute | solution.py:30
  97.0 20.2 %all-to-all-start.2 = ((bf16[32,8,512]{2,1,0:T(8,128)(2,1)}), bf16[32,8,512]{2,1,0:T(8,128)(2,1)S(1)}, u32[]{:S(2)}, u32[]{:S(2)}) async-start(bf16[32,8,512]{2,1,0:T(8,128)(2,1)} %bitcast.3), calls=%async_computation.2 | async-start | bytes 524288 | tf_op jit(solution)/shard_map/all_to_all | solution.py:421
  104.1 27.4 %collective-permute-start.16 = (bf16[128,2048]{1,0:T(8,128)(2,1)S(1)}, bf16[128,2048]{1,0:T(8,128)(2,1)S(1)}, u32[]{:S(2)}, u32[]{:S(2)}) collective-permute-start(bf16[128,2048]{1,0:T(8,128)(2,1)S(1)} %copy-done.31), channel_id=1, source_target_pairs={{0,2},{1,3},{2,0},{3,1},{4,6},{5,7},{6,4},{7,5},{8,10},{9,11},{10,... | collective-permute-start | bytes 1572872 | tf_op jit(solution)/shard_map/ppermute | solution.py:30
  106.9 7.5 %collective-permute-start.25 = (bf16[128,512]{1,0:T(8,128)(2,1)S(1)}, bf16[128,512]{1,0:T(8,128)(2,1)S(1)}, u32[]{:S(2)}, u32[]{:S(2)}) collective-permute-start(bf16[128,512]{1,0:T(8,128)(2,1)S(1)} %mirror_sum.1.after.refs_0_), channel_id=1, source_target_pairs={{0,64},{1,65},{2,66},{3,67},{4,68},{5,69},{6,70},{7,71},{8,72},{9,... | collective-permute-start | bytes 393224 | tf_op jit(solution)/shard_map/ppermute | solution.py:30
  114.4 9.8 %collective-permute-start.26 = (bf16[128,512]{1,0:T(8,128)(2,1)S(1)}, bf16[128,512]{1,0:T(8,128)(2,1)S(1)}, u32[]{:S(2)}, u32[]{:S(2)}) collective-permute-start(bf16[128,512]{1,0:T(8,128)(2,1)S(1)} %z_sum.2.refs_0_), channel_id=1, source_target_pairs={{0,128},{1,129},{2,130},{3,131},{4,132},{5,133},{6,134},{7,135},{8... | collective-permute-start | bytes 393224 | tf_op jit(solution)/shard_map/ppermute | solution.py:30
  125.0 10.6 %collective-permute-start.27 = (bf16[128,512]{1,0:T(8,128)(2,1)S(1)}, bf16[128,512]{1,0:T(8,128)(2,1)S(1)}, u32[]{:S(2)}, u32[]{:S(2)}) collective-permute-start(bf16[128,512]{1,0:T(8,128)(2,1)S(1)} %z_sum.3.mine), channel_id=1, source_target_pairs={{0,32},{1,33},{2,34},{3,35},{4,36},{5,37},{6,38},{7,39},{8,40},{9,... | collective-permute-start | bytes 393224 | tf_op jit(solution)/shard_map/ppermute | solution.py:30
  (32 other events, 270.1 us)
